TPU v7x, 256 devices: a whole 4x4x8 slice. The times are simulated.
256 devices in a mesh: section: 16 (over y_hi, z), expert: 16 (over x, y_lo, core).
Axes of the slice: x: 4, y: 4 (y_hi: 2, y_lo: 2; y = y_hi * 2 + y_lo), z: 8, core: 2. Of those that a mesh axis runs over, the one named last changes fastest.
Arguments:
- tokens: bfloat16 [16, 2048, 3584], P('section', 'expert'), may hold values from -6 to 6
- norm_gain: float32 [16, 3584], P('section'), may hold values from 0.1 to 1.9
- expert_ids: int32 [16, 2048, 2], P('section', 'expert'), may hold values from 0 to 3, all different within a row; in each aligned block of 128 rows (0 to 127, 128 to 255, ..., all dimensions but the last counted through in order) at most 80 rows name the same one
- gate_values: float32 [16, 2048, 2], P('section', 'expert'), may hold values from 0.2 to 1
- gate_weight: bfloat16 [16, 3584, 8192], P('section', None, 'expert'), may hold values from -0.09375 to 0.09375
- up_weight: bfloat16 [16, 3584, 8192], P('section', None, 'expert'), may hold values from -0.09375 to 0.09375
- down_weight: bfloat16 [16, 8192, 3584], P('section', 'expert'), may hold values from -0.125 to 0.125
Outputs:
- handed: bfloat16 [16, 2048, 3584], P('section', 'expert')
Inputs may be any that keep to these rules, and one draw needn't show every extreme that they name: `expert_ids`: each token names 2 different experts. Of the 128 tokens of one device (aligned blocks of 128 rows), at most 80 choose any one expert, and exactly 80 choose some expert in some blocks.
All inputs are finite; a program needn't handle non-finite values.
Results may differ from a plain program's by a relative error of at most 0.0053.
Values may be sent and summed in bfloat16 or wider, within the bound.
No kernel may reach another device: no remote copies, remote signals or barrier semaphores. Data moves between devices by JAX's collectives and lax.ppermute only.
A program may use at most 128 MiB of HBM per device.

v0:
```python
import jax
import jax.numpy as jnp
from jax import lax
from jax.sharding import PartitionSpec as P

EXPERTS = 4
TOP = 2
CAP = 80


def shifted(shard, axis, by):
    devices = lax.axis_size(axis)
    return lax.ppermute(shard, axis, [(i, (i + by) % devices) for i in range(devices)])


def on_device(tokens, norm_gain, expert_ids, gate_values, gate_weight, up_weight, down_weight):
    resident = tokens[0]
    choice_ids = expert_ids[0]
    weights_in = gate_values[0]
    gate_local = gate_weight[0]
    up_local = up_weight[0]
    down_local = down_weight[0]
    owners = lax.axis_size("expert")
    shards = owners // EXPERTS
    tok_count = resident.shape[0]
    model_dim = resident.shape[1]
    capacity = CAP
    widened = resident.astype(jnp.float32)
    scale = lax.rsqrt(jnp.mean(widened * widened, axis=-1, keepdims=True) + 1e-06)
    normed = (widened * scale * norm_gain[0][None, :]).astype(jnp.bfloat16)
    flat_ids = choice_ids.reshape(-1)
    onehot = (flat_ids[:, None] == jnp.arange(EXPERTS, dtype=jnp.int32)[None, :]).astype(jnp.int32)
    position = jnp.cumsum(onehot, axis=0) - 1
    slot_of = jnp.sum(position * onehot, axis=1).reshape(tok_count, TOP)
    target = choice_ids * capacity + slot_of
    dispatch_matrix = jnp.sum(
        (
            target[:, :, None] == jnp.arange(EXPERTS * capacity, dtype=jnp.int32)[None, None, :]
        ).astype(jnp.bfloat16),
        axis=1,
    )
    outgoing = jnp.einsum(
        "tr,td->rd", dispatch_matrix, normed, preferred_element_type=jnp.float32
    ).astype(jnp.bfloat16)
    outgoing = jnp.repeat(outgoing.reshape(EXPERTS, capacity, model_dim), shards, axis=0)
    arrived = lax.all_to_all(outgoing, "expert", split_axis=0, concat_axis=0, tiled=True)
    sources = arrived.shape[0]
    count = arrived.shape[1]
    flat_rows = arrived.reshape(sources * count, model_dim)
    gate = jnp.dot(flat_rows, gate_local, preferred_element_type=jnp.float32)
    upward = jnp.dot(flat_rows, up_local, preferred_element_type=jnp.float32)
    hidden = (jax.nn.silu(gate) * upward).astype(jnp.bfloat16)
    partial_out = jnp.dot(hidden, down_local, preferred_element_type=jnp.float32).astype(
        jnp.bfloat16
    )
    partials = partial_out.reshape(sources, count, model_dim)
    returned = lax.all_to_all(partials, "expert", split_axis=0, concat_axis=0, tiled=True)
    summed = jnp.sum(
        returned.astype(jnp.float32).reshape(EXPERTS, shards, capacity, model_dim), axis=1
    )
    picked = summed.reshape(EXPERTS * capacity, model_dim)[target]
    mixture = jnp.sum(weights_in[:, :, None] * picked, axis=1)
    layer_out = (widened + mixture).astype(jnp.bfloat16)
    handed = shifted(layer_out, "section", 1)
    return handed[None]


def solution(mesh):
    in_specs = (
        P("section", "expert", None),
        P("section", None),
        P("section", "expert", None),
        P("section", "expert", None),
        P("section", None, "expert"),
        P("section", None, "expert"),
        P("section", "expert", None),
    )
    out_specs = P("section", "expert", None)
    return jax.shard_map(
        on_device, mesh=mesh, in_specs=in_specs, out_specs=out_specs, check_vma=False
    )
```

profile of v0, /device:TPU:12, one launch (start us, length us, event | category | flops | bytes accessed | tf_op | source)
XLA Modules:
  0.0 351.1 jit_solution(5249072071380361276)
XLA Ops:
  0.0 0.8 copy.19
  0.8 0.0 copy-start.2
  0.8 0.1 eq.42
  0.9 0.1 eq.38
  1.1 1.2 reduce-window.6
  2.3 0.1 slice.10
  2.4 0.1 copy.22
  2.5 0.1 copy.23
  2.6 0.1 add_bitcast_fusion
  2.7 0.1 reshape.96
  2.9 0.1 copy.24
  3.0 0.1 fusion.28
  3.0 1.4 fusion.18
  4.5 0.8 reduce.1
  5.2 2.0 convolution_convert_fusion.1
  7.3 0.0 copy-done.2
  7.3 0.9 broadcast_in_dim.4
  8.2 0.0 copy-start.5
  8.2 106.9 %all_to_all.10 = bf16[16,80,3584]{2,1,0:T(8,128)(2,1)S(1)} all-to-all(bf16[16,80,3584]{2,1,0:T(8,128)(2,1)S(1)} %bitcast.60), channel_id=1, replica_groups=mesh['section'=16,'expert'=16] {'expert'}, dimensions={0} | all-to-all | bytes 18350080 | tf_op jit(solution)/shard_map/all_to_all | solution.py:46
  115.1 0.0 copy-start
  115.1 3.5 %copy-done = bf16[16,80,3584]{2,1,0:T(8,128)(2,1)} copy-done((bf16[16,80,3584]{2,1,0:T(8,128)(2,1)}, bf16[16,80,3584]{2,1,0:T(8,128)(2,1)S(1)}, u32[]{:S(2)}) %copy-start) | copy-done | bytes 9175064
  118.6 0.0 copy-done.5
  118.6 4.9 %fusion.3 = f32[1280,512]{1,0:T(8,128)S(1)} fusion(bf16[1280,3584]{1,0:T(8,128)(2,1)S(1)} %bitcast.63, bf16[1,3584,512]{2,1,0:T(8,128)(2,1)S(1)} %copy-done.5), kind=kOutput, calls=%fused_computation.7 | convolution fusion | flops 4697620480 | bytes 15466496 | tf_op jit(solution)/shard_map/dot_general | solution.py:50
  123.6 16.5 %convolution_convert_fusion = bf16[1280,3584]{1,0:T(8,128)(2,1)} fusion(bf16[1,512,3584]{2,1,0:T(8,128)(2,1)} %param.13, bf16[1280,3584]{1,0:T(8,128)(2,1)} %bitcast.64, bf16[1,3584,512]{2,1,0:T(8,128)(2,1)} %param.12, f32[1280,512]{1,0:T(8,128)S(1)} %fusion.3), kind=kOutput, calls=%fused_computation.2 | convolution fusion | flops 9403760640 | bytes 28311552 | tf_op jit(solution)/shard_map/dot_general | solution.py:53
  140.1 0.0 copy-start.3
  140.1 0.0 copy-start.4
  140.1 6.8 %all-to-all-start.1 = ((bf16[16,80,3584]{2,1,0:T(8,128)(2,1)}), bf16[16,80,3584]{2,1,0:T(8,128)(2,1)}, u32[]{:S(2)}, u32[]{:S(2)}) async-start(bf16[16,80,3584]{2,1,0:T(8,128)(2,1)} %bitcast.62), calls=%async_computation.1 | async-start | bytes 18350080 | tf_op jit(solution)/shard_map/all_to_all | solution.py:57
  146.9 0.1 reshape.104
  147.1 0.0 copy-done.3
  147.1 0.1 reshape.110
  147.2 0.0 copy-done.4
  147.2 0.1 copy.18
  147.4 146.0 %all-to-all-done.1 = bf16[16,80,3584]{2,1,0:T(8,128)(2,1)} async-done(((bf16[16,80,3584]{2,1,0:T(8,128)(2,1)}), bf16[16,80,3584]{2,1,0:T(8,128)(2,1)}, u32[]{:S(2)}, u32[]{:S(2)}) %all-to-all-start.1) | async-done | bytes 9175072 | tf_op jit(solution)/shard_map/all_to_all | solution.py:57
  293.4 7.7 %convert_reduce_fusion = f32[4,80,3584]{2,1,0:T(8,128)} fusion(bf16[16,80,3584]{2,1,0:T(8,128)(2,1)} %all-to-all-done.1), kind=kLoop, calls=%fused_computation.1 | loop fusion | flops 8028160 | bytes 13762560 | tf_op jit(solution)/shard_map/reduce_sum | solution.py:58
  301.1 7.5 %gather_fusion = f32[256,3584]{1,0:T(8,128)} fusion(f32[320,3584]{1,0:T(8,128)} %bitcast.59, s32[1024]{0:T(1024)S(1)} %pad_clamp_fusion), kind=kCustom, calls=%fused_computation | custom fusion | bytes 7341056 | tf_op jit(solution)/shard_map/gather | solution.py:61
  308.5 5.6 %reshape.109 = f32[128,2,3584]{2,1,0:T(2,128)} reshape(f32[256,3584]{1,0:T(8,128)} %gather_fusion) | data formatting | bytes 7340032 | tf_op jit(solution)/shard_map/gather | solution.py:61
  314.1 0.0 copy-start.1
  314.1 7.4 %multiply_reduce_fusion = f32[128,3584]{1,0:T(8,128)S(1)} fusion(f32[128,2,3584]{2,1,0:T(2,128)} %reshape.109, f32[128,2]{1,0:T(8,128)S(1)} %copy.18), kind=kLoop, calls=%fused_computation.9 | loop fusion | flops 1376256 | bytes 5506048 | tf_op jit(solution)/shard_map/reduce_sum | solution.py:62
  321.5 0.0 copy-done.1
  321.5 0.2 fusion.21
  321.6 2.0 collective-permute-start
  323.6 26.5 %collective-permute-done = bf16[128,3584]{1,0:T(8,128)(2,1)S(1)} collective-permute-done((bf16[128,3584]{1,0:T(8,128)(2,1)S(1)}, bf16[128,3584]{1,0:T(8,128)(2,1)S(1)}, u32[]{:S(2)}, u32[]{:S(2)}) %collective-permute-start) | collective-permute-done | bytes 917536 | tf_op jit(solution)/shard_map/ppermute | solution.py:13
  350.1 0.9 copy.28
  (8 shorter events, 0.1 us)
Async XLA Ops:
  0.8 6.5 %copy-start.2 = (s32[1,128,2]{2,1,0:T(8,128)}, s32[1,128,2]{2,1,0:T(8,128)S(1)}, u32[]{:S(2)}) copy-start(s32[1,128,2]{2,1,0:T(8,128)S(1)} %copy.19) | copy-start | bytes 3076
  8.2 110.5 %copy-start.5 = (bf16[1,3584,512]{2,1,0:T(8,128)(2,1)S(1)}, bf16[1,3584,512]{2,1,0:T(8,128)(2,1)}, u32[]{:S(2)}) copy-start(bf16[1,3584,512]{2,1,0:T(8,128)(2,1)} %param.11) | copy-start | bytes 11010052
  115.1 3.5 %copy-start = (bf16[16,80,3584]{2,1,0:T(8,128)(2,1)}, bf16[16,80,3584]{2,1,0:T(8,128)(2,1)S(1)}, u32[]{:S(2)}) copy-start(bf16[16,80,3584]{2,1,0:T(8,128)(2,1)S(1)} %all_to_all.10) | copy-start | bytes 27525124
  140.1 7.0 %copy-start.3 = (s32[1,128,2]{2,1,0:T(8,128)S(1)}, s32[1,128,2]{2,1,0:T(8,128)}, u32[]{:S(2)}) copy-start(s32[1,128,2]{2,1,0:T(8,128)} %copy-done.2) | copy-start | bytes 3076
  140.1 7.1 %copy-start.4 = (f32[1,128,2]{1,2,0:T(2,128)S(1)}, f32[1,128,2]{1,2,0:T(2,128)}, u32[]{:S(2)}) copy-start(f32[1,128,2]{1,2,0:T(2,128)} %param.10) | copy-start | bytes 3076
  140.1 153.3 %all-to-all-start.1 = ((bf16[16,80,3584]{2,1,0:T(8,128)(2,1)}), bf16[16,80,3584]{2,1,0:T(8,128)(2,1)}, u32[]{:S(2)}, u32[]{:S(2)}) async-start(bf16[16,80,3584]{2,1,0:T(8,128)(2,1)} %bitcast.62), calls=%async_computation.1 | async-start | bytes 18350080 | tf_op jit(solution)/shard_map/all_to_all | solution.py:57
  314.1 7.4 %copy-start.1 = (bf16[1,128,3584]{2,1,0:T(8,128)(2,1)S(1)}, bf16[1,128,3584]{2,1,0:T(8,128)(2,1)}, u32[]{:S(2)}) copy-start(bf16[1,128,3584]{2,1,0:T(8,128)(2,1)} %param.7) | copy-start | bytes 2752516
  321.6 28.5 %collective-permute-start = (bf16[128,3584]{1,0:T(8,128)(2,1)S(1)}, bf16[128,3584]{1,0:T(8,128)(2,1)S(1)}, u32[]{:S(2)}, u32[]{:S(2)}) collective-permute-start(bf16[128,3584]{1,0:T(8,128)(2,1)S(1)} %fusion.21), channel_id=1, source_target_pairs={{0,16},{16,32},{32,48},{48,64},{64,80},{80,96},{96,112},{112,128},... | collective-permute-start | bytes 2752520 | tf_op jit(solution)/shard_map/ppermute | solution.py:13
where the time goes:
time: 352 us; the launch traced here: 351 us
  waiting for transfers between devices  172 us (49%)
  blocking collectives  107 us (30%)
  matrix products  23.5 us (7%)
  local copies, waits for them, and re-layouts  20.3 us (6%)
  other arithmetic  18.9 us (5%)
  starting transfers between devices  8.82 us (3%)
    all_to_all x1, waiting for transfers between devices, on_device(): lax.all_to_all(partials, 'expert', split_axis=0, concat_axis=0, tiled=True)  146 us
    all_to_all x1, blocking collectives, on_device(): lax.all_to_all(outgoing, 'expert', split_axis=0, concat_axis=0, tiled=True)  107 us
    ppermute x1, waiting for transfers between devices, shifted(): lax.ppermute(shard, axis, [(i, (i + by) % devices) for i in range(devices)])  26.5 us
    dot_general x1, matrix products, on_device(): jnp.dot(hidden, down_local, preferred_element_type=jnp.float32)  16.5 us
    gather x2, local copies, waits for them, and re-layouts, on_device(): picked = summed.reshape(EXPERTS * capacity, model_dim)[target]  13 us
    reduce_sum x1, other arithmetic, on_device(): jnp.sum(returned.astype(jnp.float32).reshape(EXPERTS, shards, capacity, m...  7.69 us
    reduce_sum x1, other arithmetic, on_device(): mixture = jnp.sum(weights_in[:, :, None] * picked, axis=1)  7.4 us
  transfers between devices with their start and end apart: 2, of which 2 were waited for; matrix products, arithmetic and copies ran while one was open for 0% of the time, Pallas kernels for 0%

commit v1 on v0

v1 whole, which is shorter than its diff:
```python
import functools

import jax
import jax.numpy as jnp
from jax import lax
from jax.experimental import pallas as pl
from jax.experimental.pallas import tpu as pltpu
from jax.sharding import PartitionSpec as P

EXPERTS = 4
CAP = 80
CHUNKS = 2
F32 = jnp.float32
BF16 = jnp.bfloat16


def moved(value, dx, dy, dc):
    pairs = []
    for i in range(16):
        x, y, c = i // 4, (i // 2) % 2, i % 2
        pairs.append((i, ((x + dx) % 4) * 4 + ((y + dy) % 2) * 2 + (c + dc) % 2))
    return lax.ppermute(value, "expert", pairs)


def shifted(shard, axis, by):
    devices = lax.axis_size(axis)
    return lax.ppermute(shard, axis, [(i, (i + by) % devices) for i in range(devices)])


def route_kernel(tok_ref, gain_ref, ids_ref, gv_ref, out_ref, high_ref, low_ref):
    wide = tok_ref[...].astype(F32)
    scale = lax.rsqrt(jnp.mean(wide * wide, axis=-1, keepdims=True) + 1e-06)
    normed = (wide * scale * gain_ref[...]).astype(BF16)
    count = wide.shape[0]
    first, second = ids_ref[0:1, :], ids_ref[1:2, :]
    kind = lax.broadcasted_iota(jnp.int32, (16, count), 0)
    chosen = (kind == first) | (kind == second)
    before = (
        lax.broadcasted_iota(jnp.int32, (count, count), 0)
        < lax.broadcasted_iota(jnp.int32, (count, count), 1)
    )
    place = jnp.dot(
        chosen.astype(F32).astype(BF16), before.astype(F32).astype(BF16), preferred_element_type=F32
    )
    weight = jnp.where(kind == first, gv_ref[0:1, :], 0.0) + jnp.where(
        kind == second, gv_ref[1:2, :], 0.0
    )
    slot = lax.broadcasted_iota(jnp.int32, (CAP, count), 0).astype(F32)
    for d in range(EXPERTS):
        spot = jnp.where(chosen[d : d + 1, :], place[d : d + 1, :], -1.0)
        hit = slot == spot
        pick = jnp.where(hit, 1.0, 0.0).astype(BF16)
        out_ref[d] = jnp.dot(pick, normed, preferred_element_type=F32).astype(BF16)
        full = jnp.where(hit, weight[d : d + 1, :], 0.0)
        high = full.astype(BF16)
        high_ref[d] = high
        low_ref[d] = (full - high.astype(F32)).astype(BF16)


def route(tok, gain, ids, gv):
    count, dim = tok.shape
    return pl.pallas_call(
        route_kernel,
        out_shape=(
            jax.ShapeDtypeStruct((EXPERTS, CAP, dim), BF16),
            jax.ShapeDtypeStruct((EXPERTS, CAP, count), BF16),
            jax.ShapeDtypeStruct((EXPERTS, CAP, count), BF16),
        ),
        in_specs=[pl.BlockSpec(memory_space=pltpu.VMEM)] * 4,
        out_specs=[pl.BlockSpec(memory_space=pltpu.VMEM)] * 3,
        cost_estimate=pl.CostEstimate(
            flops=2 * EXPERTS * CAP * count * dim, bytes_accessed=6 * count * dim, transcendentals=0
        ),
        compiler_params=pltpu.CompilerParams(vmem_limit_bytes=32 << 20),
        name="route",
    )(tok, gain, ids, gv)


def weighted(high, low, rows):
    dims = (((0,), (0,)), ((), ()))
    return lax.dot_general(high, rows, dims, preferred_element_type=F32) + lax.dot_general(
        low, rows, dims, preferred_element_type=F32
    )


def mix_kernel(kinds, extra, high_ref, low_ref, *refs):
    out_ref = refs[-1]
    total = None
    for kind, ref in zip(kinds, refs):
        part = weighted(high_ref[kind], low_ref[kind], ref[...])
        total = part if total is None else total + part
    for ref in refs[len(kinds) : len(kinds) + extra]:
        total = total + ref[...].astype(F32)
    out_ref[...] = total.astype(BF16)


def mix(kinds, high, low, blocks, extra):
    count, dim = high.shape[2], blocks[0].shape[1]
    tile = 896 if dim % 896 == 0 else dim
    return pl.pallas_call(
        functools.partial(mix_kernel, kinds, len(extra)),
        grid=(dim // tile,),
        out_shape=jax.ShapeDtypeStruct((count, dim), BF16),
        in_specs=[pl.BlockSpec((EXPERTS, CAP, count), lambda i: (0, 0, 0))] * 2
        + [pl.BlockSpec((CAP, tile), lambda i: (0, i))] * len(blocks)
        + [pl.BlockSpec((count, tile), lambda i: (0, i))] * len(extra),
        out_specs=pl.BlockSpec((count, tile), lambda i: (0, i)),
        cost_estimate=pl.CostEstimate(
            flops=4 * len(blocks) * CAP * count * dim,
            bytes_accessed=2 * dim * (len(blocks) * CAP + (len(extra) + 1) * count),
            transcendentals=0,
        ),
        name="mix",
    )(high, low, *blocks, *extra)


def on_device(tokens, norm_gain, expert_ids, gate_values, gate_weight, up_weight, down_weight):
    tok = tokens[0]
    dim = tok.shape[1]
    column = lax.axis_index("expert") // 4
    ids = (expert_ids[0].T - column + EXPERTS) % EXPERTS
    gv = gate_values[0].T
    tok_across = moved(tok, 0, 1, 0)
    choice = jnp.concatenate([ids.astype(F32), gv], axis=0)
    choice_across = moved(choice, 0, 1, 0)
    gates = (gate_weight[0], moved(gate_weight[0], 0, 0, 1))
    ups = (up_weight[0], moved(up_weight[0], 0, 0, 1))
    downs = (down_weight[0], moved(down_weight[0], 0, 0, 1))

    own, own_high, own_low = route(tok, norm_gain, ids, gv)
    own_far = moved(own[2], 2, 0, 0)
    own_right = moved(own[1], 1, 0, 0)
    own_left = moved(own[3], -1, 0, 0)
    across, across_high, across_low = route(
        tok_across, norm_gain, choice_across[:2].astype(jnp.int32), choice_across[2:]
    )
    across_right = moved(across[1], 1, 0, 0)
    across_left = moved(across[3], -1, 0, 0)
    across_far = moved(own_far, 0, 1, 0)

    def hidden_of(rows):
        result = []
        for gate_w, up_w in zip(gates, ups):
            gate = jnp.dot(rows, gate_w, preferred_element_type=F32)
            upward = jnp.dot(rows, up_w, preferred_element_type=F32)
            result.append((jax.nn.silu(gate) * upward).astype(BF16))
        return result

    def down_of(hidden, lo, hi):
        return (
            jnp.dot(hidden[0], downs[0][:, lo:hi], preferred_element_type=F32)
            + jnp.dot(hidden[1], downs[1][:, lo:hi], preferred_element_type=F32)
        ).astype(BF16)

    early = hidden_of(jnp.concatenate([own[0], across[0], own_far, own_right, own_left], axis=0))
    late = hidden_of(jnp.concatenate([across_far, across_right, across_left], axis=0))
    width = dim // CHUNKS
    outs = []
    for k in range(CHUNKS):
        lo, hi = k * width, (k + 1) * width
        late_out = down_of(late, lo, hi)
        early_out = down_of(early, lo, hi)
        blocks = [early_out[i * CAP : (i + 1) * CAP] for i in range(5)]
        late_blocks = [late_out[i * CAP : (i + 1) * CAP] for i in range(3)]
        far_in = moved(late_blocks[0], 0, 1, 0)
        back_right = moved(late_blocks[1], -1, 0, 0)
        back_left = moved(late_blocks[2], 1, 0, 0)
        my_right = moved(blocks[3], -1, 0, 0)
        my_left = moved(blocks[4], 1, 0, 0)
        far_sum = (blocks[2].astype(F32) + far_in.astype(F32)).astype(BF16)
        my_far = moved(far_sum, 2, 0, 0)
        theirs = mix((0, 1, 3), across_high, across_low, (blocks[1], back_right, back_left), ())
        mine = moved(theirs, 0, 1, 0)
        layer_out = mix(
            (0, 1, 3, 2),
            own_high,
            own_low,
            (blocks[0], my_right, my_left, my_far),
            (mine, tok[:, lo:hi]),
        )
        outs.append(shifted(layer_out, "section", 1))
    return jnp.concatenate(outs, axis=1)[None]


def solution(mesh):
    in_specs = (
        P("section", "expert", None),
        P("section", None),
        P("section", "expert", None),
        P("section", "expert", None),
        P("section", None, "expert"),
        P("section", None, "expert"),
        P("section", "expert", None),
    )
    out_specs = P("section", "expert", None)
    return jax.shard_map(
        on_device, mesh=mesh, in_specs=in_specs, out_specs=out_specs, check_vma=False
    )
```

time: 352 us -> 161 us (0.46)
  the two profiles are of different devices: /device:TPU:12 before, /device:TPU:2 now
where the time goes in v1:
time: 161 us; the launch traced here: 160 us
  waiting for transfers between devices  78.9 us (49%)
  starting transfers between devices  32.9 us (20%)
  matrix products  17 us (11%)
  Pallas kernels  15.2 us (9%)
  local copies, waits for them, and re-layouts  11.5 us (7%)
  other arithmetic  4.42 us (3%)
    ppermute x25, waiting for transfers between devices, moved(): return lax.ppermute(value, 'expert', pairs)  66.6 us
    ppermute x25, starting transfers between devices, moved(): return lax.ppermute(value, 'expert', pairs)  31 us
    pallas_call x4, Pallas kernels, mix(): pl.pallas_call(functools.partial(mix_kernel, kinds, len(extra)), grid=(di...  13.1 us
    ppermute x2, waiting for transfers between devices, shifted(): lax.ppermute(shard, axis, [(i, (i + by) % devices) for i in range(devices)])  12.3 us
    unnamed x44, local copies, waits for them, and re-layouts  6.55 us
    dot_general x4, matrix products, hidden_of(): upward = jnp.dot(rows, up_w, preferred_element_type=F32)  5.52 us
    dot_general x4, matrix products, hidden_of(): gate = jnp.dot(rows, gate_w, preferred_element_type=F32)  5.35 us
  transfers between devices with their start and end apart: 27, of which 12 were waited for; matrix products, arithmetic and copies ran while one was open for 13% of the time, Pallas kernels for 9%

profile of v1, /device:TPU:2, one launch (start us, length us, event | category | flops | bytes accessed | tf_op | source)
XLA Modules:
  0.0 160.4 jit_solution(619397446097536773)
XLA Ops:
  0.0 1.6 collective-permute-start
  3.4 1.2 copy-done
  6.0 1.0 route.2
  7.2 2.2 %collective-permute-start.2 = (bf16[80,3584]{1,0:T(8,128)(2,1)S(1)}, bf16[80,3584]{1,0:T(8,128)(2,1)S(1)}, u32[]{:S(2)}, u32[]{:S(2)}) collective-permute-start(bf16[80,3584]{1,0:T(8,128)(2,1)S(1)} %get-tuple-element.23), channel_id=1, source_target_pairs={{0,8},{1,9},{2,10},{3,11},{4,12},{5,13},{6,14},{7,15},{8,0},{9,1},... | collective-permute-start | bytes 1720328 | tf_op jit(solution)/shard_map/ppermute | solution.py:22
  9.4 1.6 collective-permute-start.3
  11.5 10.9 %collective-permute-done.1 = f32[4,128]{1,0:T(4,128)S(1)} collective-permute-done((f32[4,128]{1,0:T(4,128)S(1)}, f32[4,128]{1,0:T(4,128)S(1)}, u32[]{:S(2)}, u32[]{:S(2)}) %collective-permute-start.1) | collective-permute-done | bytes 2080 | tf_op jit(solution)/shard_map/ppermute | solution.py:22
  23.0 1.0 route.3
  24.8 10.5 %collective-permute-done.3 = bf16[80,3584]{1,0:T(8,128)(2,1)S(1)} collective-permute-done((bf16[80,3584]{1,0:T(8,128)(2,1)S(1)}, bf16[80,3584]{1,0:T(8,128)(2,1)S(1)}, u32[]{:S(2)}, u32[]{:S(2)}) %collective-permute-start.3) | collective-permute-done | bytes 573472 | tf_op jit(solution)/shard_map/ppermute | solution.py:22
  35.3 1.6 collective-permute-start.10
  37.0 1.6 %fusion.27 = f32[400,512]{1,0:T(8,128)S(1)} fusion(bf16[400,3584]{1,0:T(8,128)(2,1)S(1)} %constant_dynamic-update-slice_fusion, bf16[1,3584,512]{2,1,0:T(8,128)(2,1)S(1)} %copy-done.17), kind=kOutput, calls=%fused_computation.52 | convolution fusion | flops 1468006400 | bytes 7356416 | tf_op jit(solution)/shard_map/dot_general | solution.py:144
  39.0 1.7 %multiply_convert_fusion.1 = bf16[400,512]{1,0:T(8,128)(2,1)S(1)} fusion(f32[400,512]{1,0:T(8,128)S(1)} %fusion.27, bf16[400,3584]{1,0:T(8,128)(2,1)S(1)} %constant_dynamic-update-slice_fusion, bf16[1,3584,512]{2,1,0:T(8,128)(2,1)S(1)} %copy-done.18), kind=kOutput, calls=%fused_computation.22 | convolution fusion | flops 1469235200 | bytes 7766016 | tf_op jit(solution)/shard_map/dot_general | solution.py:145
  43.2 5.4 %collective-permute-done.10 = bf16[80,3584]{1,0:T(8,128)(2,1)S(1)} collective-permute-done((bf16[80,3584]{1,0:T(8,128)(2,1)S(1)}, bf16[80,3584]{1,0:T(8,128)(2,1)S(1)}, u32[]{:S(2)}, u32[]{:S(2)}) %collective-permute-start.10) | collective-permute-done | bytes 573472 | tf_op jit(solution)/shard_map/ppermute | solution.py:22
  48.6 1.9 %collective-permute-start.12 = (bf16[80,3584]{1,0:T(8,128)(2,1)S(1)}, bf16[80,3584]{1,0:T(8,128)(2,1)S(1)}, u32[]{:S(2)}, u32[]{:S(2)}) collective-permute-start(bf16[80,3584]{1,0:T(8,128)(2,1)S(1)} %get-tuple-element.19), channel_id=1, source_target_pairs={{0,12},{1,13},{2,14},{3,15},{4,0},{5,1},{6,2},{7,3},{8,4},{9,5},{1... | collective-permute-start | bytes 1720328 | tf_op jit(solution)/shard_map/ppermute | solution.py:22
  50.6 3.6 %collective-permute-done.11 = bf16[80,3584]{1,0:T(8,128)(2,1)S(1)} collective-permute-done((bf16[80,3584]{1,0:T(8,128)(2,1)S(1)}, bf16[80,3584]{1,0:T(8,128)(2,1)S(1)}, u32[]{:S(2)}, u32[]{:S(2)}) %collective-permute-start.11) | collective-permute-done | bytes 573472 | tf_op jit(solution)/shard_map/ppermute | solution.py:22
  54.2 7.9 %collective-permute-done.12 = bf16[80,3584]{1,0:T(8,128)(2,1)S(1)} collective-permute-done((bf16[80,3584]{1,0:T(8,128)(2,1)S(1)}, bf16[80,3584]{1,0:T(8,128)(2,1)S(1)}, u32[]{:S(2)}, u32[]{:S(2)}) %collective-permute-start.12) | collective-permute-done | bytes 573472 | tf_op jit(solution)/shard_map/ppermute | solution.py:22
  62.1 1.0 fusion.25
  63.2 1.1 multiply_convert_fusion.3
  65.5 1.6 %fusion.36 = f32[400,512]{1,0:T(8,128)S(1)} fusion(bf16[400,3584]{1,0:T(8,128)(2,1)S(1)} %constant_dynamic-update-slice_fusion, bf16[3584,512]{1,0:T(8,128)(2,1)S(1)} %collective-permute-done.5), kind=kOutput, calls=%fused_computation.61 | convolution fusion | flops 1468006400 | bytes 7356416 | tf_op jit(solution)/shard_map/dot_general | solution.py:144
  67.1 1.7 %multiply_convert_fusion = bf16[400,512]{1,0:T(8,128)(2,1)S(1)} fusion(f32[400,512]{1,0:T(8,128)S(1)} %fusion.36, bf16[400,3584]{1,0:T(8,128)(2,1)S(1)} %constant_dynamic-update-slice_fusion, bf16[3584,512]{1,0:T(8,128)(2,1)S(1)} %collective-permute-done.6), kind=kOutput, calls=%fused_computation.21 | convolution fusion | flops 1469235200 | bytes 7766016 | tf_op jit(solution)/shard_map/dot_general | solution.py:145
  68.9 0.9 fusion.1
  69.8 0.9 fusion.31
  70.7 1.0 fusion.37
  71.7 1.1 multiply_convert_fusion.2
  74.2 1.7 %collective-permute-start.21 = (bf16[80,1792]{1,0:T(8,128)(2,1)}, bf16[80,1792]{1,0:T(8,128)(2,1)}, u32[]{:S(2)}, u32[]{:S(2)}) collective-permute-start(bf16[80,1792]{1,0:T(8,128)(2,1)} %get-tuple-element.39), channel_id=1, source_target_pairs={{0,2},{1,3},{2,0},{3,1},{4,6},{5,7},{6,4},{7,5},{8,10},{9,11},{10,... | collective-permute-start | bytes 860168 | tf_op jit(solution)/shard_map/ppermute | solution.py:22
  76.0 2.5 %collective-permute-start.23 = (bf16[80,1792]{1,0:T(8,128)(2,1)S(1)}, bf16[80,1792]{1,0:T(8,128)(2,1)S(1)}, u32[]{:S(2)}, u32[]{:S(2)}) collective-permute-start(bf16[80,1792]{1,0:T(8,128)(2,1)S(1)} %get-tuple-element.38), channel_id=1, source_target_pairs={{0,12},{1,13},{2,14},{3,15},{4,0},{5,1},{6,2},{7,3},{8,4},{9,5},{1... | collective-permute-start | bytes 860168 | tf_op jit(solution)/shard_map/ppermute | solution.py:22
  79.1 0.9 fusion.33
  80.0 2.0 %collective-permute-start.15 = (bf16[80,1792]{1,0:T(8,128)(2,1)}, bf16[80,1792]{1,0:T(8,128)(2,1)}, u32[]{:S(2)}, u32[]{:S(2)}) collective-permute-start(bf16[80,1792]{1,0:T(8,128)(2,1)} %get-tuple-element.35), channel_id=1, source_target_pairs={{0,12},{1,13},{2,14},{3,15},{4,0},{5,1},{6,2},{7,3},{8,4},{9,5},{1... | collective-permute-start | bytes 860168 | tf_op jit(solution)/shard_map/ppermute | solution.py:22
  82.1 0.9 fusion
  83.0 1.1 copy-done.9
  84.1 1.0 fusion.30
  85.5 2.6 %collective-permute-start.19 = (bf16[80,1792]{1,0:T(8,128)(2,1)S(1)}, bf16[80,1792]{1,0:T(8,128)(2,1)}, u32[]{:S(2)}, u32[]{:S(2)}) collective-permute-start(bf16[80,1792]{1,0:T(8,128)(2,1)S(1)} %get-tuple-element.30), channel_id=1, source_target_pairs={{0,12},{1,13},{2,14},{3,15},{4,0},{5,1},{6,2},{7,3},{8,4},{9,5},{1... | collective-permute-start | bytes 860168 | tf_op jit(solution)/shard_map/ppermute | solution.py:22
  88.8 3.0 %mix.6 = bf16[128,1792]{1,0:T(8,128)(2,1)} custom-call(bf16[4,80,128]{2,1,0:T(8,128)(2,1)} %copy-done.2, bf16[4,80,128]{2,1,0:T(8,128)(2,1)} %copy-done.3, bf16[80,1792]{1,0:T(8,128)(2,1)} %get-tuple-element.28.refs_0_, bf16[80,1792]{1,0:T(8,128)(2,1)} %copy-done.14, bf16[80,1792]{1,0:T(8,128)(2,1)} %copy-done.15), custom_call_target="tpu_custom_call" | custom-call | flops 220200960 | bytes 1318912 | tf_op jit(solution)/shard_map/mix/pallas_call | solution.py:100
  91.9 3.3 %collective-permute-start.8 = (bf16[80,1792]{1,0:T(8,128)(2,1)}, bf16[80,1792]{1,0:T(8,128)(2,1)}, u32[]{:S(2)}, u32[]{:S(2)}) collective-permute-start(bf16[80,1792]{1,0:T(8,128)(2,1)} %get-tuple-element.26), channel_id=1, source_target_pairs={{0,12},{1,13},{2,14},{3,15},{4,0},{5,1},{6,2},{7,3},{8,4},{9,5},{1... | collective-permute-start | bytes 860168 | tf_op jit(solution)/shard_map/ppermute | solution.py:22
  95.2 3.0 %mix.4 = bf16[128,1792]{1,0:T(8,128)(2,1)} custom-call(bf16[4,80,128]{2,1,0:T(8,128)(2,1)} %copy-done.2, bf16[4,80,128]{2,1,0:T(8,128)(2,1)} %copy-done.3, bf16[80,1792]{1,0:T(8,128)(2,1)} %get-tuple-element.24.refs_0_, bf16[80,1792]{1,0:T(8,128)(2,1)} %collective-permute-done.15.refs_1_, bf16[80,1792]{1,0:T(8,128)(2,1)} %collective-permute-done.16.refs_2_), custom_call_target="tpu_custom_call" | custom-call | flops 220200960 | bytes 1318912 | tf_op jit(solution)/shard_map/mix/pallas_call | solution.py:100
  98.5 1.0 add_convert_fusion
  99.5 5.5 %collective-permute-done.13 = bf16[80,1792]{1,0:T(8,128)(2,1)S(1)} collective-permute-done((bf16[80,1792]{1,0:T(8,128)(2,1)}, bf16[80,1792]{1,0:T(8,128)(2,1)S(1)}, u32[]{:S(2)}, u32[]{:S(2)}) %collective-permute-start.13) | collective-permute-done | bytes 286752 | tf_op jit(solution)/shard_map/ppermute | solution.py:22
  105.1 5.5 %collective-permute-start.22 = (bf16[80,1792]{1,0:T(8,128)(2,1)S(1)}, bf16[80,1792]{1,0:T(8,128)(2,1)S(1)}, u32[]{:S(2)}, u32[]{:S(2)}) collective-permute-start(bf16[80,1792]{1,0:T(8,128)(2,1)S(1)} %add_convert_fusion), channel_id=1, source_target_pairs={{0,8},{1,9},{2,10},{3,11},{4,12},{5,13},{6,14},{7,15},{8,0},{9,1},... | collective-permute-start | bytes 860168 | tf_op jit(solution)/shard_map/ppermute | solution.py:22
  110.6 1.0 add_convert_fusion.1
  112.1 4.1 %collective-permute-done.22.refs_3_ = bf16[80,1792]{1,0:T(8,128)(2,1)S(1)} collective-permute-done((bf16[80,1792]{1,0:T(8,128)(2,1)S(1)}, bf16[80,1792]{1,0:T(8,128)(2,1)S(1)}, u32[]{:S(2)}, u32[]{:S(2)}) %collective-permute-start.22) | collective-permute-done | bytes 286752 | tf_op jit(solution)/shard_map/ppermute | solution.py:22
  116.1 1.6 %collective-permute-start.17 = (bf16[128,1792]{1,0:T(8,128)(2,1)}, bf16[128,1792]{1,0:T(8,128)(2,1)S(1)}, u32[]{:S(2)}, u32[]{:S(2)}) collective-permute-start(bf16[128,1792]{1,0:T(8,128)(2,1)} %mix.4), channel_id=1, source_target_pairs={{0,2},{1,3},{2,0},{3,1},{4,6},{5,7},{6,4},{7,5},{8,10},{9,11},{10,... | collective-permute-start | bytes 1376264 | tf_op jit(solution)/shard_map/ppermute | solution.py:22
  117.8 1.0 fusion.32
  118.8 4.3 %collective-permute-done.25.refs_4_ = bf16[128,1792]{1,0:T(8,128)(2,1)S(1)} collective-permute-done((bf16[128,1792]{1,0:T(8,128)(2,1)S(1)}, bf16[128,1792]{1,0:T(8,128)(2,1)S(1)}, u32[]{:S(2)}, u32[]{:S(2)}) %collective-permute-start.25) | collective-permute-done | bytes 458784 | tf_op jit(solution)/shard_map/ppermute | solution.py:22
  123.9 3.5 %mix.7 = bf16[128,1792]{1,0:T(8,128)(2,1)} custom-call(bf16[4,80,128]{2,1,0:T(8,128)(2,1)} %copy-done.4, bf16[4,80,128]{2,1,0:T(8,128)(2,1)} %copy-done.5, bf16[80,1792]{1,0:T(8,128)(2,1)} %get-tuple-element.31.refs_0_, bf16[80,1792]{1,0:T(8,128)(2,1)} %collective-permute-done.19.refs_1_, bf16[80,1792]{1,0:T(8,128)(2,1)} %collective-permute-done.20.refs_2_, ...), custom_call_target="tpu_custom_call" | custom-call | flops 293601280 | bytes 2523136 | tf_op jit(solution)/shard_map/mix/pallas_call | solution.py:100
  127.4 1.9 %collective-permute-start.26 = (bf16[128,1792]{1,0:T(8,128)(2,1)}, bf16[128,1792]{1,0:T(8,128)(2,1)S(1)}, u32[]{:S(2)}, u32[]{:S(2)}) collective-permute-start(bf16[128,1792]{1,0:T(8,128)(2,1)} %mix.7), channel_id=1, source_target_pairs={{0,16},{16,32},{32,48},{48,64},{64,80},{80,96},{96,112},{112,128},... | collective-permute-start | bytes 1376264 | tf_op jit(solution)/shard_map/ppermute | solution.py:27
  129.4 13.4 %collective-permute-done.17.refs_4_ = bf16[128,1792]{1,0:T(8,128)(2,1)S(1)} collective-permute-done((bf16[128,1792]{1,0:T(8,128)(2,1)}, bf16[128,1792]{1,0:T(8,128)(2,1)S(1)}, u32[]{:S(2)}, u32[]{:S(2)}) %collective-permute-start.17) | collective-permute-done | bytes 458784 | tf_op jit(solution)/shard_map/ppermute | solution.py:22
  143.6 3.5 %mix.5 = bf16[128,1792]{1,0:T(8,128)(2,1)} custom-call(bf16[4,80,128]{2,1,0:T(8,128)(2,1)} %copy-done.4, bf16[4,80,128]{2,1,0:T(8,128)(2,1)} %copy-done.5, bf16[80,1792]{1,0:T(8,128)(2,1)} %get-tuple-element.27.refs_0_, bf16[80,1792]{1,0:T(8,128)(2,1)} %collective-permute-done.8.refs_1_, bf16[80,1792]{1,0:T(8,128)(2,1)} %collective-permute-done.9.refs_2_, ...), custom_call_target="tpu_custom_call" | custom-call | flops 293601280 | bytes 2523136 | tf_op jit(solution)/shard_map/mix/pallas_call | solution.py:100
  147.1 12.3 %collective-permute-done.18 = bf16[128,1792]{1,0:T(8,128)(2,1)S(1)} collective-permute-done((bf16[128,1792]{1,0:T(8,128)(2,1)}, bf16[128,1792]{1,0:T(8,128)(2,1)S(1)}, u32[]{:S(2)}, u32[]{:S(2)}) %collective-permute-start.18) | collective-permute-done | bytes 458784 | tf_op jit(solution)/shard_map/ppermute | solution.py:27
  159.4 1.0 maximum_bitcast_fusion
  (87 shorter events, 14.9 us)
Async XLA Ops:
  0.0 22.4 %collective-permute-start = (bf16[128,3584]{1,0:T(8,128)(2,1)}, bf16[128,3584]{1,0:T(8,128)(2,1)S(1)}, u32[]{:S(2)}, u32[]{:S(2)}) collective-permute-start(bf16[128,3584]{1,0:T(8,128)(2,1)} %bitcast.60), channel_id=1, source_target_pairs={{0,2},{1,3},{2,0},{3,1},{4,6},{5,7},{6,4},{7,5},{8,10},{9,11},{10,... | collective-permute-start | bytes 2752520 | tf_op jit(solution)/shard_map/ppermute | solution.py:22
  3.0 19.4 %collective-permute-start.1 = (f32[4,128]{1,0:T(4,128)S(1)}, f32[4,128]{1,0:T(4,128)S(1)}, u32[]{:S(2)}, u32[]{:S(2)}) collective-permute-start(f32[4,128]{1,0:T(4,128)S(1)} %pad_maximum_fusion), channel_id=1, source_target_pairs={{0,2},{1,3},{2,0},{3,1},{4,6},{5,7},{6,4},{7,5},{8,10},{9,11},{10,... | collective-permute-start | bytes 6152 | tf_op jit(solution)/shard_map/ppermute | solution.py:22
  3.4 1.2 copy-start
  4.6 0.7 copy-start.6
  5.3 0.7 copy-start.7
  6.0 16.4 %copy-start.17 = (bf16[1,3584,512]{2,1,0:T(8,128)(2,1)S(1)}, bf16[1,3584,512]{2,1,0:T(8,128)(2,1)}, u32[]{:S(2)}) copy-start(bf16[1,3584,512]{2,1,0:T(8,128)(2,1)} %param.11) | copy-start | bytes 11010052
  7.0 15.9 %copy-start.4 = (bf16[4,80,128]{2,1,0:T(8,128)(2,1)}, bf16[4,80,128]{2,1,0:T(8,128)(2,1)S(1)}, u32[]{:S(2)}) copy-start(bf16[4,80,128]{2,1,0:T(8,128)(2,1)S(1)} %get-tuple-element.11.high_ref) | copy-start | bytes 245764
  7.0 15.9 %copy-start.5 = (bf16[4,80,128]{2,1,0:T(8,128)(2,1)}, bf16[4,80,128]{2,1,0:T(8,128)(2,1)S(1)}, u32[]{:S(2)}) copy-start(bf16[4,80,128]{2,1,0:T(8,128)(2,1)S(1)} %get-tuple-element.12.low_ref) | copy-start | bytes 245764
  7.2 17.6 %copy-start.8 = (bf16[1,512,3584]{2,1,0:T(8,128)(2,1)S(1)}, bf16[1,512,3584]{2,1,0:T(8,128)(2,1)}, u32[]{:S(2)}) copy-start(bf16[1,512,3584]{2,1,0:T(8,128)(2,1)} %param.13) | copy-start | bytes 11010052
  7.2 17.5 %collective-permute-start.2 = (bf16[80,3584]{1,0:T(8,128)(2,1)S(1)}, bf16[80,3584]{1,0:T(8,128)(2,1)S(1)}, u32[]{:S(2)}, u32[]{:S(2)}) collective-permute-start(bf16[80,3584]{1,0:T(8,128)(2,1)S(1)} %get-tuple-element.23), channel_id=1, source_target_pairs={{0,8},{1,9},{2,10},{3,11},{4,12},{5,13},{6,14},{7,15},{8,0},{9,1},... | collective-permute-start | bytes 1720328 | tf_op jit(solution)/shard_map/ppermute | solution.py:22
  9.4 25.9 %collective-permute-start.3 = (bf16[80,3584]{1,0:T(8,128)(2,1)S(1)}, bf16[80,3584]{1,0:T(8,128)(2,1)S(1)}, u32[]{:S(2)}, u32[]{:S(2)}) collective-permute-start(bf16[80,3584]{1,0:T(8,128)(2,1)S(1)} %get-tuple-element.22), channel_id=1, source_target_pairs={{0,4},{1,5},{2,6},{3,7},{4,8},{5,9},{6,10},{7,11},{8,12},{9,13},{1... | collective-permute-start | bytes 1720328 | tf_op jit(solution)/shard_map/ppermute | solution.py:22
  11.0 25.9 %collective-permute-start.4 = (bf16[80,3584]{1,0:T(8,128)(2,1)S(1)}, bf16[80,3584]{1,0:T(8,128)(2,1)S(1)}, u32[]{:S(2)}, u32[]{:S(2)}) collective-permute-start(bf16[80,3584]{1,0:T(8,128)(2,1)S(1)} %get-tuple-element.21), channel_id=1, source_target_pairs={{0,12},{1,13},{2,14},{3,15},{4,0},{5,1},{6,2},{7,3},{8,4},{9,5},{1... | collective-permute-start | bytes 1720328 | tf_op jit(solution)/shard_map/ppermute | solution.py:22
  22.3 43.1 %collective-permute-start.5 = (bf16[3584,512]{1,0:T(8,128)(2,1)S(1)}, bf16[3584,512]{1,0:T(8,128)(2,1)S(1)}, u32[]{:S(2)}, u32[]{:S(2)}) collective-permute-start(bf16[3584,512]{1,0:T(8,128)(2,1)S(1)} %bitcast.70), channel_id=1, source_target_pairs={{0,1},{1,0},{2,3},{3,2},{4,5},{5,4},{6,7},{7,6},{8,9},{9,8},{10,11... | collective-permute-start | bytes 11010056 | tf_op jit(solution)/shard_map/ppermute | solution.py:22
  22.4 44.8 %collective-permute-start.6 = (bf16[3584,512]{1,0:T(8,128)(2,1)}, bf16[3584,512]{1,0:T(8,128)(2,1)S(1)}, u32[]{:S(2)}, u32[]{:S(2)}) collective-permute-start(bf16[3584,512]{1,0:T(8,128)(2,1)} %bitcast.71), channel_id=1, source_target_pairs={{0,1},{1,0},{2,3},{3,2},{4,5},{5,4},{6,7},{7,6},{8,9},{9,8},{10,11... | collective-permute-start | bytes 11010056 | tf_op jit(solution)/shard_map/ppermute | solution.py:22
  24.0 12.9 %copy-start.2 = (bf16[4,80,128]{2,1,0:T(8,128)(2,1)}, bf16[4,80,128]{2,1,0:T(8,128)(2,1)S(1)}, u32[]{:S(2)}) copy-start(bf16[4,80,128]{2,1,0:T(8,128)(2,1)S(1)} %get-tuple-element.15.high_ref) | copy-start | bytes 245764
  24.0 12.9 %copy-start.3 = (bf16[4,80,128]{2,1,0:T(8,128)(2,1)}, bf16[4,80,128]{2,1,0:T(8,128)(2,1)S(1)}, u32[]{:S(2)}) copy-start(bf16[4,80,128]{2,1,0:T(8,128)(2,1)S(1)} %get-tuple-element.16.low_ref) | copy-start | bytes 245764
  24.7 44.1 %collective-permute-start.7 = (bf16[512,3584]{1,0:T(8,128)(2,1)S(1)}, bf16[512,3584]{1,0:T(8,128)(2,1)S(1)}, u32[]{:S(2)}, u32[]{:S(2)}) collective-permute-start(bf16[512,3584]{1,0:T(8,128)(2,1)S(1)} %bitcast.65), channel_id=1, source_target_pairs={{0,1},{1,0},{2,3},{3,2},{4,5},{5,4},{6,7},{7,6},{8,9},{9,8},{10,11... | collective-permute-start | bytes 11010056 | tf_op jit(solution)/shard_map/ppermute | solution.py:22
  35.3 13.3 %collective-permute-start.10 = (bf16[80,3584]{1,0:T(8,128)(2,1)S(1)}, bf16[80,3584]{1,0:T(8,128)(2,1)S(1)}, u32[]{:S(2)}, u32[]{:S(2)}) collective-permute-start(bf16[80,3584]{1,0:T(8,128)(2,1)S(1)} %collective-permute-done.2), channel_id=1, source_target_pairs={{0,2},{1,3},{2,0},{3,1},{4,6},{5,7},{6,4},{7,5},{8,10},{9,11},{10,... | collective-permute-start | bytes 1720328 | tf_op jit(solution)/shard_map/ppermute | solution.py:22
  37.0 2.0 %copy-start.18 = (bf16[1,3584,512]{2,1,0:T(8,128)(2,1)S(1)}, bf16[1,3584,512]{2,1,0:T(8,128)(2,1)}, u32[]{:S(2)}) copy-start(bf16[1,3584,512]{2,1,0:T(8,128)(2,1)} %param.12) | copy-start | bytes 11010052
  40.8 13.4 %collective-permute-start.11 = (bf16[80,3584]{1,0:T(8,128)(2,1)S(1)}, bf16[80,3584]{1,0:T(8,128)(2,1)S(1)}, u32[]{:S(2)}, u32[]{:S(2)}) collective-permute-start(bf16[80,3584]{1,0:T(8,128)(2,1)S(1)} %get-tuple-element.20), channel_id=1, source_target_pairs={{0,4},{1,5},{2,6},{3,7},{4,8},{5,9},{6,10},{7,11},{8,12},{9,13},{1... | collective-permute-start | bytes 1720328 | tf_op jit(solution)/shard_map/ppermute | solution.py:22
  48.6 13.5 %collective-permute-start.12 = (bf16[80,3584]{1,0:T(8,128)(2,1)S(1)}, bf16[80,3584]{1,0:T(8,128)(2,1)S(1)}, u32[]{:S(2)}, u32[]{:S(2)}) collective-permute-start(bf16[80,3584]{1,0:T(8,128)(2,1)S(1)} %get-tuple-element.19), channel_id=1, source_target_pairs={{0,12},{1,13},{2,14},{3,15},{4,0},{5,1},{6,2},{7,3},{8,4},{9,5},{1... | collective-permute-start | bytes 1720328 | tf_op jit(solution)/shard_map/ppermute | solution.py:22
  74.2 24.0 %collective-permute-start.21 = (bf16[80,1792]{1,0:T(8,128)(2,1)}, bf16[80,1792]{1,0:T(8,128)(2,1)}, u32[]{:S(2)}, u32[]{:S(2)}) collective-permute-start(bf16[80,1792]{1,0:T(8,128)(2,1)} %get-tuple-element.39), channel_id=1, source_target_pairs={{0,2},{1,3},{2,0},{3,1},{4,6},{5,7},{6,4},{7,5},{8,10},{9,11},{10,... | collective-permute-start | bytes 860168 | tf_op jit(solution)/shard_map/ppermute | solution.py:22
  76.0 9.6 %collective-permute-start.23 = (bf16[80,1792]{1,0:T(8,128)(2,1)S(1)}, bf16[80,1792]{1,0:T(8,128)(2,1)S(1)}, u32[]{:S(2)}, u32[]{:S(2)}) collective-permute-start(bf16[80,1792]{1,0:T(8,128)(2,1)S(1)} %get-tuple-element.38), channel_id=1, source_target_pairs={{0,12},{1,13},{2,14},{3,15},{4,0},{5,1},{6,2},{7,3},{8,4},{9,5},{1... | collective-permute-start | bytes 860168 | tf_op jit(solution)/shard_map/ppermute | solution.py:22
  78.4 9.7 %collective-permute-start.24 = (bf16[80,1792]{1,0:T(8,128)(2,1)S(1)}, bf16[80,1792]{1,0:T(8,128)(2,1)S(1)}, u32[]{:S(2)}, u32[]{:S(2)}) collective-permute-start(bf16[80,1792]{1,0:T(8,128)(2,1)S(1)} %get-tuple-element.37), channel_id=1, source_target_pairs={{0,4},{1,5},{2,6},{3,7},{4,8},{5,9},{6,10},{7,11},{8,12},{9,13},{1... | collective-permute-start | bytes 860168 | tf_op jit(solution)/shard_map/ppermute | solution.py:22
  80.0 11.8 %collective-permute-start.15 = (bf16[80,1792]{1,0:T(8,128)(2,1)}, bf16[80,1792]{1,0:T(8,128)(2,1)}, u32[]{:S(2)}, u32[]{:S(2)}) collective-permute-start(bf16[80,1792]{1,0:T(8,128)(2,1)} %get-tuple-element.35), channel_id=1, source_target_pairs={{0,12},{1,13},{2,14},{3,15},{4,0},{5,1},{6,2},{7,3},{8,4},{9,5},{1... | collective-permute-start | bytes 860168 | tf_op jit(solution)/shard_map/ppermute | solution.py:22
  82.0 13.1 %collective-permute-start.16 = (bf16[80,1792]{1,0:T(8,128)(2,1)}, bf16[80,1792]{1,0:T(8,128)(2,1)}, u32[]{:S(2)}, u32[]{:S(2)}) collective-permute-start(bf16[80,1792]{1,0:T(8,128)(2,1)} %get-tuple-element.34), channel_id=1, source_target_pairs={{0,4},{1,5},{2,6},{3,7},{4,8},{5,9},{6,10},{7,11},{8,12},{9,13},{1... | collective-permute-start | bytes 860168 | tf_op jit(solution)/shard_map/ppermute | solution.py:22
  83.0 1.1 copy-start.9
  85.1 32.7 %copy-start.1 = (bf16[1,128,3584]{2,1,0:T(8,128)(2,1)S(1)}, bf16[1,128,3584]{2,1,0:T(8,128)(2,1)}, u32[]{:S(2)}) copy-start(bf16[1,128,3584]{2,1,0:T(8,128)(2,1)} %param.7) | copy-start | bytes 2752516
  85.5 2.6 %copy-start.14 = (bf16[80,1792]{1,0:T(8,128)(2,1)}, bf16[80,1792]{1,0:T(8,128)(2,1)S(1)}, u32[]{:S(2)}) copy-start(bf16[80,1792]{1,0:T(8,128)(2,1)S(1)} %collective-permute-done.23.refs_1_) | copy-start | bytes 860164
  85.5 26.1 %collective-permute-start.19 = (bf16[80,1792]{1,0:T(8,128)(2,1)S(1)}, bf16[80,1792]{1,0:T(8,128)(2,1)}, u32[]{:S(2)}, u32[]{:S(2)}) collective-permute-start(bf16[80,1792]{1,0:T(8,128)(2,1)S(1)} %get-tuple-element.30), channel_id=1, source_target_pairs={{0,12},{1,13},{2,14},{3,15},{4,0},{5,1},{6,2},{7,3},{8,4},{9,5},{1... | collective-permute-start | bytes 860168 | tf_op jit(solution)/shard_map/ppermute | solution.py:22
  88.1 0.7 copy-start.15
  88.1 23.9 %collective-permute-start.20 = (bf16[80,1792]{1,0:T(8,128)(2,1)S(1)}, bf16[80,1792]{1,0:T(8,128)(2,1)}, u32[]{:S(2)}, u32[]{:S(2)}) collective-permute-start(bf16[80,1792]{1,0:T(8,128)(2,1)S(1)} %get-tuple-element.29), channel_id=1, source_target_pairs={{0,4},{1,5},{2,6},{3,7},{4,8},{5,9},{6,10},{7,11},{8,12},{9,13},{1... | collective-permute-start | bytes 860168 | tf_op jit(solution)/shard_map/ppermute | solution.py:22
  91.8 19.8 %copy-start.10 = (bf16[128,1792]{1,0:T(8,128)(2,1)S(1)}, bf16[128,1792]{1,0:T(8,128)(2,1)}, u32[]{:S(2)}) copy-start(bf16[128,1792]{1,0:T(8,128)(2,1)} %mix.6) | copy-start | bytes 1376260
  91.9 37.5 %collective-permute-start.8 = (bf16[80,1792]{1,0:T(8,128)(2,1)}, bf16[80,1792]{1,0:T(8,128)(2,1)}, u32[]{:S(2)}, u32[]{:S(2)}) collective-permute-start(bf16[80,1792]{1,0:T(8,128)(2,1)} %get-tuple-element.26), channel_id=1, source_target_pairs={{0,12},{1,13},{2,14},{3,15},{4,0},{5,1},{6,2},{7,3},{8,4},{9,5},{1... | collective-permute-start | bytes 860168 | tf_op jit(solution)/shard_map/ppermute | solution.py:22
  95.2 34.2 %collective-permute-start.9 = (bf16[80,1792]{1,0:T(8,128)(2,1)}, bf16[80,1792]{1,0:T(8,128)(2,1)}, u32[]{:S(2)}, u32[]{:S(2)}) collective-permute-start(bf16[80,1792]{1,0:T(8,128)(2,1)} %get-tuple-element.25), channel_id=1, source_target_pairs={{0,4},{1,5},{2,6},{3,7},{4,8},{5,9},{6,10},{7,11},{8,12},{9,13},{1... | collective-permute-start | bytes 860168 | tf_op jit(solution)/shard_map/ppermute | solution.py:22
  98.2 6.8 %collective-permute-start.13 = (bf16[80,1792]{1,0:T(8,128)(2,1)}, bf16[80,1792]{1,0:T(8,128)(2,1)S(1)}, u32[]{:S(2)}, u32[]{:S(2)}) collective-permute-start(bf16[80,1792]{1,0:T(8,128)(2,1)} %get-tuple-element.36), channel_id=1, source_target_pairs={{0,2},{1,3},{2,0},{3,1},{4,6},{5,7},{6,4},{7,5},{8,10},{9,11},{10,... | collective-permute-start | bytes 860168 | tf_op jit(solution)/shard_map/ppermute | solution.py:22
  105.1 11.1 %collective-permute-start.22 = (bf16[80,1792]{1,0:T(8,128)(2,1)S(1)}, bf16[80,1792]{1,0:T(8,128)(2,1)S(1)}, u32[]{:S(2)}, u32[]{:S(2)}) collective-permute-start(bf16[80,1792]{1,0:T(8,128)(2,1)S(1)} %add_convert_fusion), channel_id=1, source_target_pairs={{0,8},{1,9},{2,10},{3,11},{4,12},{5,13},{6,14},{7,15},{8,0},{9,1},... | collective-permute-start | bytes 860168 | tf_op jit(solution)/shard_map/ppermute | solution.py:22
  111.6 11.5 %collective-permute-start.25 = (bf16[128,1792]{1,0:T(8,128)(2,1)S(1)}, bf16[128,1792]{1,0:T(8,128)(2,1)S(1)}, u32[]{:S(2)}, u32[]{:S(2)}) collective-permute-start(bf16[128,1792]{1,0:T(8,128)(2,1)S(1)} %copy-done.10), channel_id=1, source_target_pairs={{0,2},{1,3},{2,0},{3,1},{4,6},{5,7},{6,4},{7,5},{8,10},{9,11},{10,... | collective-permute-start | bytes 1376264 | tf_op jit(solution)/shard_map/ppermute | solution.py:22
  112.1 17.3 %collective-permute-start.14 = (bf16[80,1792]{1,0:T(8,128)(2,1)S(1)}, bf16[80,1792]{1,0:T(8,128)(2,1)S(1)}, u32[]{:S(2)}, u32[]{:S(2)}) collective-permute-start(bf16[80,1792]{1,0:T(8,128)(2,1)S(1)} %add_convert_fusion.1), channel_id=1, source_target_pairs={{0,8},{1,9},{2,10},{3,11},{4,12},{5,13},{6,14},{7,15},{8,0},{9,1},... | collective-permute-start | bytes 860168 | tf_op jit(solution)/shard_map/ppermute | solution.py:22
  116.1 7.0 %copy-start.16 = (bf16[80,1792]{1,0:T(8,128)(2,1)}, bf16[80,1792]{1,0:T(8,128)(2,1)S(1)}, u32[]{:S(2)}) copy-start(bf16[80,1792]{1,0:T(8,128)(2,1)S(1)} %collective-permute-done.22.refs_3_) | copy-start | bytes 860164
  116.1 26.6 %collective-permute-start.17 = (bf16[128,1792]{1,0:T(8,128)(2,1)}, bf16[128,1792]{1,0:T(8,128)(2,1)S(1)}, u32[]{:S(2)}, u32[]{:S(2)}) collective-permute-start(bf16[128,1792]{1,0:T(8,128)(2,1)} %mix.4), channel_id=1, source_target_pairs={{0,2},{1,3},{2,0},{3,1},{4,6},{5,7},{6,4},{7,5},{8,10},{9,11},{10,... | collective-permute-start | bytes 1376264 | tf_op jit(solution)/shard_map/ppermute | solution.py:22
  123.1 0.8 copy-start.12
  127.4 19.7 %collective-permute-start.26 = (bf16[128,1792]{1,0:T(8,128)(2,1)}, bf16[128,1792]{1,0:T(8,128)(2,1)S(1)}, u32[]{:S(2)}, u32[]{:S(2)}) collective-permute-start(bf16[128,1792]{1,0:T(8,128)(2,1)} %mix.7), channel_id=1, source_target_pairs={{0,16},{16,32},{32,48},{48,64},{64,80},{80,96},{96,112},{112,128},... | collective-permute-start | bytes 1376264 | tf_op jit(solution)/shard_map/ppermute | solution.py:27
  129.4 13.4 %copy-start.13 = (bf16[80,1792]{1,0:T(8,128)(2,1)}, bf16[80,1792]{1,0:T(8,128)(2,1)S(1)}, u32[]{:S(2)}) copy-start(bf16[80,1792]{1,0:T(8,128)(2,1)S(1)} %collective-permute-done.14.refs_3_) | copy-start | bytes 860164
  142.8 0.8 copy-start.11
  147.1 12.3 %collective-permute-start.18 = (bf16[128,1792]{1,0:T(8,128)(2,1)}, bf16[128,1792]{1,0:T(8,128)(2,1)S(1)}, u32[]{:S(2)}, u32[]{:S(2)}) collective-permute-start(bf16[128,1792]{1,0:T(8,128)(2,1)} %mix.5), channel_id=1, source_target_pairs={{0,16},{16,32},{32,48},{48,64},{64,80},{80,96},{96,112},{112,128},... | collective-permute-start | bytes 1376264 | tf_op jit(solution)/shard_map/ppermute | solution.py:27

commit v2 on v1

v2 whole, which is shorter than its diff:
```python
import functools

import jax
import jax.numpy as jnp
from jax import lax
from jax.experimental import pallas as pl
from jax.experimental.pallas import tpu as pltpu
from jax.sharding import PartitionSpec as P

EXPERTS = 4
CAP = 80
CHUNKS = 2
LAYERS = 8
TILE = 256
PACK = 128
FREE = pl.CostEstimate(flops=0, bytes_accessed=0, transcendentals=0)
F32 = jnp.float32
BF16 = jnp.bfloat16
VMEM = pl.BlockSpec(memory_space=pltpu.VMEM)
SMEM = pl.BlockSpec(memory_space=pltpu.SMEM)
ANY = pl.BlockSpec(memory_space=pl.ANY)
HBM = pl.BlockSpec(memory_space=pltpu.HBM)


def limit(mebibytes):
    return pltpu.CompilerParams(vmem_limit_bytes=mebibytes << 20)


def moved(value, dx, dy, dc):
    pairs = []
    for i in range(16):
        x, y, c = i // 4, (i // 2) % 2, i % 2
        pairs.append((i, ((x + dx) % 4) * 4 + ((y + dy) % 2) * 2 + (c + dc) % 2))
    return lax.ppermute(value, "expert", pairs)


def handed_on(value):
    pairs = []
    for s in range(16):
        for e in range(16):
            to = e ^ 2 if s % LAYERS == LAYERS - 1 else e
            pairs.append((s * 16 + e, ((s + 1) % 16) * 16 + to))
    return lax.ppermute(value, ("section", "expert"), pairs)


def first_route_kernel(column_ref, *refs):
    far, refs = refs[:4], refs[4:]
    *refs, sent_ref, gain_ref, ids_ref, gv_ref, sems = refs
    count, dim = far[0].shape
    near = (sent_ref.at[:, :dim], gain_ref, ids_ref, gv_ref)
    copies = [pltpu.make_async_copy(a, b, sems.at[i]) for i, (a, b) in enumerate(zip(far, near))]
    for copy in copies:
        copy.start()
    for copy in copies:
        copy.wait()
    ids, gv = ids_ref[...], gv_ref[...]
    high = gv.astype(BF16).astype(F32)
    middle = (gv - high).astype(BF16).astype(F32)
    low = gv - high - middle
    packed = jnp.concatenate([ids.astype(F32), high, middle, low], axis=0)
    packed = jnp.concatenate([packed, jnp.zeros((PACK - 8, count), F32)], axis=0)
    sent_ref[:, dim:] = packed.T.astype(BF16)
    route_kernel((0, 1, 2, 3), column_ref, sent_ref, gain_ref, ids, gv, *refs)


def second_route_kernel(column_ref, sent_ref, gain_ref, *refs):
    packed = sent_ref[:, gain_ref.shape[1] :].astype(F32).T
    ids = packed[0:2].astype(jnp.int32)
    gv = packed[2:4] + packed[4:6] + packed[6:8]
    route_kernel((0, 1, 3), column_ref, sent_ref, gain_ref, ids, gv, *refs)


def route_kernel(kinds, column_ref, tok_ref, gain_ref, ids, gv, *refs):
    w_ref = refs[-1]
    out_refs = dict(zip(kinds, refs[-1 - len(kinds) : -1]))
    wide = tok_ref[:, : gain_ref.shape[1]].astype(F32)
    scale = lax.rsqrt(jnp.mean(wide * wide, axis=-1, keepdims=True) + 1e-06)
    normed = (wide * scale * gain_ref[...]).astype(BF16)
    count = normed.shape[0]
    ids = jnp.bitwise_and(ids + (EXPERTS - column_ref[0]), EXPERTS - 1)
    first, second = ids[0:1, :], ids[1:2, :]
    kind = lax.broadcasted_iota(jnp.int32, (16, count), 0)
    chosen = (kind == first) | (kind == second)
    before = (
        lax.broadcasted_iota(jnp.int32, (count, count), 0)
        < lax.broadcasted_iota(jnp.int32, (count, count), 1)
    )
    place = jnp.dot(
        chosen.astype(F32).astype(BF16), before.astype(F32).astype(BF16), preferred_element_type=F32
    )
    weight = jnp.where(kind == first, gv[0:1, :], 0.0) + jnp.where(
        kind == second, gv[1:2, :], 0.0
    )
    slot = lax.broadcasted_iota(jnp.int32, (CAP, count), 0).astype(F32)
    for d in range(EXPERTS):
        spot = jnp.where(chosen[d : d + 1, :], place[d : d + 1, :], -1.0)
        hit = slot == spot
        pick = jnp.where(hit, 1.0, 0.0).astype(BF16)
        if d in out_refs:
            out_refs[d][...] = jnp.dot(pick, normed, preferred_element_type=F32).astype(BF16)
        full = jnp.where(hit, weight[d : d + 1, :], 0.0)
        high = full.astype(BF16)
        low = (full - high.astype(F32)).astype(BF16)
        w_ref[d] = jnp.concatenate([high, low], axis=1)


def route(first_set, column, tok, gain, choices, others):
    count, dim = tok.shape[0], gain.shape[1]
    blocks = 4 if first_set else 3
    out_shape = [jax.ShapeDtypeStruct((CAP, dim), BF16)] * blocks
    out_shape.append(jax.ShapeDtypeStruct((EXPERTS, CAP, 2 * count), BF16))
    kernel, scratch = second_route_kernel, []
    if first_set:
        kernel = first_route_kernel
        out_shape.append(jax.ShapeDtypeStruct((count, dim + PACK), BF16))
        scratch = [pltpu.VMEM(v.shape, v.dtype) for v in (gain, *choices)]
        scratch.append(pltpu.SemaphoreType.DMA((4,)))
    operands = (tok, gain, *choices)
    inner = 1 + len(operands)

    def body(*refs):
        kernel(*refs[:inner], *refs[inner + len(others) :])

    return pl.pallas_call(
        body,
        out_shape=out_shape,
        in_specs=[SMEM] + [HBM if first_set else VMEM] * len(operands) + [ANY] * len(others),
        out_specs=[VMEM] * len(out_shape),
        scratch_shapes=scratch,
        cost_estimate=FREE,
        compiler_params=limit(58 if first_set else 12),
        name="route",
    )(column, *operands, *others)


def hidden_tile(rows_ref, gate_ref, up_ref, hidden_ref, at, to):
    columns = pl.ds(at, TILE)
    gate = jnp.dot(rows_ref[...], gate_ref[:, columns], preferred_element_type=F32)
    upward = jnp.dot(rows_ref[...], up_ref[:, columns], preferred_element_type=F32)
    hidden_ref[:, pl.ds(to, TILE)] = (jax.nn.silu(gate) * upward).astype(BF16)


def down_chunk(hidden_ref, down_refs, chunk, width, out_refs):
    units = down_refs[0].shape[0]
    for at in range(0, width, TILE):
        columns = slice(chunk * width + at, chunk * width + at + TILE)
        total = jnp.dot(hidden_ref[:, :units], down_refs[0][:, columns], preferred_element_type=F32)
        total += jnp.dot(
            hidden_ref[:, units:], down_refs[1][:, columns], preferred_element_type=F32
        )
        for i, ref in enumerate(out_refs):
            ref[:, at : at + TILE] = total[i * CAP : (i + 1) * CAP].astype(BF16)


def expert_kernel(blocks, bring, *refs):
    rows_in, given = refs[:blocks], refs[blocks : blocks + 6]
    refs = refs[blocks + 6 :]
    outs, refs = refs[: blocks * CHUNKS], refs[blocks * CHUNKS :]
    near = given
    if bring:
        near, refs = refs[:6], refs[6:]
    rows_ref, hidden_ref = refs[:2]
    units = near[0].shape[1]
    width = outs[0].shape[1]
    copies = []

    def start(which, columns):
        if bring:
            copies.append(
                pltpu.make_async_copy(
                    given[which].at[:, columns], near[which].at[:, columns], refs[2].at[len(copies)]
                )
            )
            copies[-1].start()

    def arrived(step):
        if bring:
            copies[2 * step].wait()
            copies[2 * step + 1].wait()

    for half in range(2):
        for at in range(0, units, TILE):
            for which in (2 * half, 2 * half + 1):
                start(which, slice(at, at + TILE))
    for chunk in range(CHUNKS):
        for which in (4, 5):
            start(which, slice(chunk * width, (chunk + 1) * width))
    for i, ref in enumerate(rows_in):
        rows_ref[i * CAP : (i + 1) * CAP, :] = ref[...]
    step = 0
    for half in range(2):
        for at in range(0, units, TILE):
            arrived(step)
            hidden_tile(
                rows_ref, near[2 * half], near[2 * half + 1], hidden_ref, at, half * units + at
            )
            step += 1
    for chunk in range(CHUNKS):
        arrived(step)
        down_chunk(hidden_ref, near[4:], chunk, width, outs[chunk * blocks : (chunk + 1) * blocks])
        step += 1


def expert(rows, weights, width, bring, others=()):
    blocks, dim = len(rows), rows[0].shape[1]
    units = weights[0].shape[1]
    out_shape = [jax.ShapeDtypeStruct((CAP, width), BF16)] * (blocks * CHUNKS)
    scratch = [
        pltpu.VMEM((blocks * CAP, dim), BF16),
        pltpu.VMEM((blocks * CAP, 2 * units), BF16),
    ]
    if bring:
        out_shape += [jax.ShapeDtypeStruct(w.shape, BF16) for w in weights]
        scratch.append(pltpu.SemaphoreType.DMA((4 * (units // TILE) + 2 * CHUNKS,)))
    inner = blocks + 6

    def body(*refs):
        expert_kernel(blocks, bring, *refs[:inner], *refs[inner + len(others) :])

    outs = pl.pallas_call(
        body,
        out_shape=out_shape,
        in_specs=[VMEM] * blocks + [HBM if bring else VMEM] * 6 + [ANY] * len(others),
        out_specs=[VMEM] * len(out_shape),
        scratch_shapes=scratch,
        cost_estimate=FREE,
        compiler_params=limit(29 if bring else 12),
        name="expert",
    )(*rows, *weights, *others)
    chunks = [outs[k * blocks : (k + 1) * blocks] for k in range(CHUNKS)]
    return chunks, outs[blocks * CHUNKS :] if bring else weights


def after_kernel(*refs):
    pass


def after(values, others):
    return pl.pallas_call(
        after_kernel,
        out_shape=[jax.ShapeDtypeStruct(v.shape, v.dtype) for v in values],
        in_specs=[ANY] * (len(values) + len(others)),
        out_specs=[ANY] * len(values),
        input_output_aliases={i: i for i in range(len(values))},
        cost_estimate=FREE,
        compiler_params=limit(1),
        name="after",
    )(*values, *others)


def weighted(w_ref, kinds, refs):
    count = w_ref.shape[2] // 2
    weights = jnp.concatenate([w_ref[d] for d in kinds], axis=0)
    rows = jnp.concatenate([ref[...] for ref in refs], axis=0)
    both = lax.dot_general(weights, rows, (((0,), (0,)), ((), ())), preferred_element_type=F32)
    return both[:count] + both[count:]


def leave_kernel(swap_ref, w_own_ref, w_across_ref, *refs):
    own_refs, across_refs, out_ref = refs[:3], refs[3:6], refs[6]

    @pl.when(swap_ref[0] == 0)
    def _():
        out_ref[...] = weighted(w_across_ref, (0, 1, 3), across_refs).astype(BF16)

    @pl.when(swap_ref[0] != 0)
    def _():
        out_ref[...] = weighted(w_own_ref, (0, 1, 3), own_refs).astype(BF16)


def stay_kernel(chunk, swap_ref, w_own_ref, w_across_ref, *refs):
    own_refs, across_refs = refs[:3], refs[3:6]
    far_ref, mine_ref, tok_ref, tok_across_ref, out_ref = refs[6:]
    width = out_ref.shape[1]
    columns = slice(chunk * width, (chunk + 1) * width)

    @pl.when(swap_ref[0] == 0)
    def _():
        total = weighted(w_own_ref, (0, 1, 3, 2), (*own_refs, far_ref))
        out_ref[...] = (total + mine_ref[...].astype(F32) + tok_ref[:, columns].astype(F32)).astype(BF16)

    @pl.when(swap_ref[0] != 0)
    def _():
        total = weighted(w_across_ref, (0, 1, 3, 2), (*across_refs, far_ref))
        out_ref[...] = (
            total + mine_ref[...].astype(F32) + tok_across_ref[:, columns].astype(F32)
        ).astype(BF16)


def mix(kernel, name, swap, w_own, w_across, blocks):
    count, width = w_own.shape[2] // 2, blocks[0].shape[1]
    return pl.pallas_call(
        kernel,
        out_shape=jax.ShapeDtypeStruct((count, width), BF16),
        in_specs=[SMEM] + [VMEM] * (2 + len(blocks)),
        out_specs=VMEM,
        cost_estimate=FREE,
        compiler_params=limit(8),
        name=name,
    )(swap, w_own, w_across, *blocks)


def on_device(tokens, norm_gain, expert_ids, gate_values, gate_weight, up_weight, down_weight):
    tok = tokens[0]
    dim = tok.shape[1]
    column = lax.axis_index("expert") // 4
    swapped = lax.axis_index("section") % LAYERS == LAYERS - 1
    swap = swapped.astype(jnp.int32).reshape(1)
    column = column.astype(jnp.int32).reshape(1)
    ids = expert_ids[0].T
    gv = gate_values[0].T
    gates = (gate_weight[0], moved(gate_weight[0], 0, 0, 1))
    ups = (up_weight[0], moved(up_weight[0], 0, 0, 1))
    downs = (down_weight[0], moved(down_weight[0], 0, 0, 1))

    weights = (gates[0], ups[0], gates[1], ups[1], downs[0], downs[1])

    *own, w_own, sent = route(True, column, tok, norm_gain, (ids, gv), ())
    tok_across = moved(sent, 0, 1, 0)
    own_far = moved(own[2], 2, 0, 0)
    right_rows, left_rows = after((own[1], own[3]), (gates[1], ups[1], downs[1]))
    own_right = moved(right_rows, 1, 0, 0)
    own_left = moved(left_rows, -1, 0, 0)
    *across, w_across = route(
        False, column, tok_across, norm_gain, (), (right_rows, left_rows)
    )
    across_right = moved(across[1], 1, 0, 0)
    across_left = moved(across[2], -1, 0, 0)
    across_far = moved(own_far, 0, 1, 0)

    width = dim // CHUNKS
    first, kept = expert((own[0], own_far), weights, width, True)
    second, _ = expert((across[0], own_right, own_left, across_far), kept, width, False)
    third, _ = expert((across_right, across_left), kept, width, False, (second[-1][0],))
    outs = []
    for k in range(CHUNKS):
        own_out, far_out = first[k]
        across_out, right_out, left_out, far_late = second[k]
        right_late, left_late = third[k]
        far_in = moved(jnp.where(swapped, far_out, far_late), 0, 1, 0)
        far_kept = jnp.where(swapped, far_late, far_out)
        across_back = (across_out, moved(right_late, -1, 0, 0), moved(left_late, 1, 0, 0))
        own_back = (own_out, moved(right_out, -1, 0, 0), moved(left_out, 1, 0, 0))
        far_sum = (far_kept.astype(F32) + far_in.astype(F32)).astype(BF16)
        far_back = moved(far_sum, 2, 0, 0)
        leaving = mix(leave_kernel, "leave", swap, w_own, w_across, (*own_back, *across_back))
        mine = moved(leaving, 0, 1, 0)
        layer_out = mix(
            functools.partial(stay_kernel, k),
            "stay",
            swap,
            w_own,
            w_across,
            (*own_back, *across_back, far_back, mine, sent, tok_across),
        )
        outs.append(handed_on(layer_out))
    return jnp.concatenate(outs, axis=1)[None]


def solution(mesh):
    in_specs = (
        P("section", "expert", None),
        P("section", None),
        P("section", "expert", None),
        P("section", "expert", None),
        P("section", None, "expert"),
        P("section", None, "expert"),
        P("section", "expert", None),
    )
    out_specs = P("section", "expert", None)
    return jax.shard_map(
        on_device, mesh=mesh, in_specs=in_specs, out_specs=out_specs, check_vma=False
    )
```

time: 161 us -> 119 us (0.74)
  waiting for transfers between devices: 78.9 us -> 52.3 us
  matrix products: 17 us -> 0 us
  Pallas kernels: 15.2 us -> 29.3 us
  local copies, waits for them, and re-layouts: 11.5 us -> 0.84 us
  other arithmetic: 4.42 us -> 1.28 us
  starting transfers between devices: 32.9 us -> 34.6 us
    ppermute x25 -> x24, waiting for transfers between devices: 66.6 us -> 37.7 us  [moved(): return lax.ppermute(value, 'expert', pairs)]
    dot_general x16 -> x0, matrix products: 17 us -> none  [the longest x4 5.52 us: hidden_of(): upward = jnp.dot(rows, up_w, preferred_element_type=F32)]
    pallas_call x6 -> x10, Pallas kernels: 15.2 us -> 29.3 us  [the longest x3 21.7 us: expert(): pl.pallas_call(body, out_shape=out_shape, in_specs=[VMEM] * blocks + [HBM...]
    ppermute x2, starting transfers between devices: 1.92 us -> 7.72 us  [handed_on(): return lax.ppermute(value, ('section', 'expert'), pairs)]
    unnamed x44 -> x12, local copies, waits for them, and re-layouts: 6.55 us -> 0.84 us
    slice x5 -> x0, local copies, waits for them, and re-layouts: 4.68 us -> none  [the longest x2 1.96 us: on_device(): blocks = [early_out[i * CAP:(i + 1) * CAP] for i in range(5)]]
    ppermute x25 -> x24, starting transfers between devices: 31 us -> 26.9 us  [moved(): return lax.ppermute(value, 'expert', pairs)]
    convert_element_type x3 -> x2, other arithmetic: 2.75 us -> 0.23 us  [on_device(): far_sum = (far_kept.astype(F32) + far_in.astype(F32)).astype(BF16)]
  transfers between devices with their start and end apart: 27 -> 26, of which waited for: 12 -> 13; matrix products, arithmetic and copies ran while one was open for 13% -> 0% of each run, Pallas kernels for 9% -> 22%
where the time goes in v2:
time: 119 us; the launch traced here: 118 us
  waiting for transfers between devices  52.3 us (44%)
  starting transfers between devices  34.6 us (29%)
  Pallas kernels  29.3 us (25%)
  other arithmetic  1.28 us (1%)
    ppermute x24, waiting for transfers between devices, moved(): return lax.ppermute(value, 'expert', pairs)  37.7 us
    ppermute x24, starting transfers between devices, moved(): return lax.ppermute(value, 'expert', pairs)  26.9 us
    pallas_call x3, Pallas kernels, expert(): pl.pallas_call(body, out_shape=out_shape, in_specs=[VMEM] * blocks + [HBM...  21.7 us
    ppermute x2, waiting for transfers between devices, handed_on(): return lax.ppermute(value, ('section', 'expert'), pairs)  14.6 us
    ppermute x2, starting transfers between devices, handed_on(): return lax.ppermute(value, ('section', 'expert'), pairs)  7.72 us
    pallas_call x2, Pallas kernels, route(): pl.pallas_call(body, out_shape=out_shape, in_specs=[SMEM] + [HBM if first...  5.3 us
  transfers between devices with their start and end apart: 26, of which 13 were waited for; matrix products, arithmetic and copies ran while one was open for 0% of the time, Pallas kernels for 22%

profile of v2, /device:TPU:2, one launch (start us, length us, event | category | flops | bytes accessed | tf_op | source)
XLA Modules:
  0.0 118.5 jit_solution(8319610863386878145)
XLA Ops:
  0.0 0.5 collective-permute-start.2
  0.5 3.5 %route.2 = (bf16[80,3584]{1,0:T(8,128)(2,1)}, bf16[80,3584]{1,0:T(8,128)(2,1)}, bf16[80,3584]{1,0:T(8,128)(2,1)}, bf16[80,3584]{1,0:T(8,128)(2,1)}, bf16[4,80,25...) custom-call(s32[1]{0:T(128)} %bitcast.1.refs_0_, bf16[128,3584]{1,0:T(8,128)(2,1)} %bitcast.20, f32[1,3584]{1,0:T(1,128)} %refs_2_.3, ...), custom_call_target="tpu_custom_call" | custom-call | tf_op jit(solution)/shard_map/route/pallas_call | solution.py:124
  4.1 1.7 %collective-permute-start = (bf16[128,3712]{1,0:T(8,128)(2,1)}, bf16[128,3712]{1,0:T(8,128)(2,1)S(1)}, u32[]{:S(2)}, u32[]{:S(2)}) collective-permute-start(bf16[128,3712]{1,0:T(8,128)(2,1)} %get-tuple-element.40.refs_8_), channel_id=1, source_target_pairs={{0,2},{1,3},{2,0},{3,1},{4,6},{5,7},{6,4},{7,5},{8,10},{9,11},{10,... | collective-permute-start | bytes 2850824 | tf_op jit(solution)/shard_map/ppermute | solution.py:34
  5.7 2.1 %collective-permute-start.4 = (bf16[80,3584]{1,0:T(8,128)(2,1)}, bf16[80,3584]{1,0:T(8,128)(2,1)}, u32[]{:S(2)}, u32[]{:S(2)}) collective-permute-start(bf16[80,3584]{1,0:T(8,128)(2,1)} %get-tuple-element.47), channel_id=1, source_target_pairs={{0,8},{1,9},{2,10},{3,11},{4,12},{5,13},{6,14},{7,15},{8,0},{9,1},... | collective-permute-start | bytes 1720328 | tf_op jit(solution)/shard_map/ppermute | solution.py:34
  7.8 14.8 %collective-permute-done.4.refs_1_ = bf16[80,3584]{1,0:T(8,128)(2,1)} collective-permute-done((bf16[80,3584]{1,0:T(8,128)(2,1)}, bf16[80,3584]{1,0:T(8,128)(2,1)}, u32[]{:S(2)}, u32[]{:S(2)}) %collective-permute-start.4) | collective-permute-done | bytes 573472 | tf_op jit(solution)/shard_map/ppermute | solution.py:34
  22.6 0.5 collective-permute-start.7
  23.1 0.0 copy-start.5
  23.1 0.0 copy-start.2
  23.1 1.6 %collective-permute-start.5 = (bf16[80,3584]{1,0:T(8,128)(2,1)}, bf16[80,3584]{1,0:T(8,128)(2,1)}, u32[]{:S(2)}, u32[]{:S(2)}) collective-permute-start(bf16[80,3584]{1,0:T(8,128)(2,1)} %get-tuple-element.43.refs_3_), channel_id=1, source_target_pairs={{0,4},{1,5},{2,6},{3,7},{4,8},{5,9},{6,10},{7,11},{8,12},{9,13},{1... | collective-permute-start | bytes 1720328 | tf_op jit(solution)/shard_map/ppermute | solution.py:34
  24.7 0.9 collective-permute-start.6
  25.6 2.6 %collective-permute-done.refs_1_.refs_9_ = bf16[128,3712]{1,0:T(8,128)(2,1)S(1)} collective-permute-done((bf16[128,3712]{1,0:T(8,128)(2,1)}, bf16[128,3712]{1,0:T(8,128)(2,1)S(1)}, u32[]{:S(2)}, u32[]{:S(2)}) %collective-permute-start) | collective-permute-done | bytes 950304 | tf_op jit(solution)/shard_map/ppermute | solution.py:34
  28.2 1.8 %route.3 = (bf16[80,3584]{1,0:T(8,128)(2,1)S(1)}, bf16[80,3584]{1,0:T(8,128)(2,1)}, bf16[80,3584]{1,0:T(8,128)(2,1)}, bf16[4,80,256]{2,1,0:T(8,128)(2,1)S(1)}) custom-call(s32[1]{0:T(128)} %bitcast.1.refs_0_, bf16[128,3712]{1,0:T(8,128)(2,1)S(1)} %collective-permute-done.refs_1_.refs_9_, f32[1,3584]{1,0:T(1,128)S(1)} %copy-done.5, ...), custom_call_target="tpu_custom_call" | custom-call | tf_op jit(solution)/shard_map/route/pallas_call | solution.py:124
  30.0 0.8 copy-done.3
  30.8 1.5 %collective-permute-start.10 = (bf16[80,3584]{1,0:T(8,128)(2,1)}, bf16[80,3584]{1,0:T(8,128)(2,1)S(1)}, u32[]{:S(2)}, u32[]{:S(2)}) collective-permute-start(bf16[80,3584]{1,0:T(8,128)(2,1)} %get-tuple-element.59), channel_id=1, source_target_pairs={{0,4},{1,5},{2,6},{3,7},{4,8},{5,9},{6,10},{7,11},{8,12},{9,13},{1... | collective-permute-start | bytes 1720328 | tf_op jit(solution)/shard_map/ppermute | solution.py:34
  32.3 0.8 collective-permute-start.11
  33.1 9.4 %expert.3 = (bf16[80,1792]{1,0:T(8,128)(2,1)S(1)}, bf16[80,1792]{1,0:T(8,128)(2,1)S(1)}, bf16[80,1792]{1,0:T(8,128)(2,1)S(1)}, bf16[80,1792]{1,0:T(8,128)(2,1)S(...) custom-call(bf16[80,3584]{1,0:T(8,128)(2,1)S(1)} %copy-done.2, ...), custom_call_target="tpu_custom_call" | custom-call | tf_op jit(solution)/shard_map/expert/pallas_call | solution.py:220
  42.5 8.5 %expert.4 = (bf16[80,1792]{1,0:T(8,128)(2,1)S(1)}, bf16[80,1792]{1,0:T(8,128)(2,1)S(1)}, bf16[80,1792]{1,0:T(8,128)(2,1)S(1)}, bf16[80,1792]{1,0:T(8,128)(2,1)S(...) custom-call(bf16[80,3584]{1,0:T(8,128)(2,1)S(1)} %copy-done.4, ...), custom_call_target="tpu_custom_call" | custom-call | tf_op jit(solution)/shard_map/expert/pallas_call | solution.py:220
  51.0 3.8 %expert.5 = (bf16[80,1792]{1,0:T(8,128)(2,1)S(1)}, bf16[80,1792]{1,0:T(8,128)(2,1)S(1)}, bf16[80,1792]{1,0:T(8,128)(2,1)S(1)}, bf16[80,1792]{1,0:T(8,128)(2,1)S(1)}) custom-call(bf16[80,3584]{1,0:T(8,128)(2,1)S(1)} %collective-permute-done.10.refs_0_, bf16[80,3584]{1,0:T(8,128)(2,1)S(1)} %collective-permute-done.11.refs_1_, ...), custom_call_target="tpu_custom_call" | custom-call | tf_op jit(solution)/shard_map/expert/pallas_call | solution.py:220
  54.8 3.3 %collective-permute-start.12 = (bf16[80,1792]{1,0:T(8,128)(2,1)S(1)}, bf16[80,1792]{1,0:T(8,128)(2,1)S(1)}, u32[]{:S(2)}, u32[]{:S(2)}) collective-permute-start(bf16[80,1792]{1,0:T(8,128)(2,1)S(1)} %get-tuple-element.62), channel_id=1, source_target_pairs={{0,12},{1,13},{2,14},{3,15},{4,0},{5,1},{6,2},{7,3},{8,4},{9,5},{1... | collective-permute-start | bytes 860168 | tf_op jit(solution)/shard_map/ppermute | solution.py:34
  58.2 2.0 %collective-permute-start.8 = (bf16[80,1792]{1,0:T(8,128)(2,1)S(1)}, bf16[80,1792]{1,0:T(8,128)(2,1)S(1)}, u32[]{:S(2)}, u32[]{:S(2)}) collective-permute-start(bf16[80,1792]{1,0:T(8,128)(2,1)S(1)} %get-tuple-element.56), channel_id=1, source_target_pairs={{0,12},{1,13},{2,14},{3,15},{4,0},{5,1},{6,2},{7,3},{8,4},{9,5},{1... | collective-permute-start | bytes 860168 | tf_op jit(solution)/shard_map/ppermute | solution.py:34
  60.2 0.6 collective-permute-start.14
  60.9 4.5 %collective-permute-done.12.refs_4_ = bf16[80,1792]{1,0:T(8,128)(2,1)S(1)} collective-permute-done((bf16[80,1792]{1,0:T(8,128)(2,1)S(1)}, bf16[80,1792]{1,0:T(8,128)(2,1)S(1)}, u32[]{:S(2)}, u32[]{:S(2)}) %collective-permute-start.12) | collective-permute-done | bytes 286752 | tf_op jit(solution)/shard_map/ppermute | solution.py:34
  65.5 2.5 %collective-permute-start.20 = (bf16[80,1792]{1,0:T(8,128)(2,1)S(1)}, bf16[80,1792]{1,0:T(8,128)(2,1)S(1)}, u32[]{:S(2)}, u32[]{:S(2)}) collective-permute-start(bf16[80,1792]{1,0:T(8,128)(2,1)S(1)} %get-tuple-element.69), channel_id=1, source_target_pairs={{0,12},{1,13},{2,14},{3,15},{4,0},{5,1},{6,2},{7,3},{8,4},{9,5},{1... | collective-permute-start | bytes 860168 | tf_op jit(solution)/shard_map/ppermute | solution.py:34
  67.9 3.7 %collective-permute-done.8.refs_1_ = bf16[80,1792]{1,0:T(8,128)(2,1)S(1)} collective-permute-done((bf16[80,1792]{1,0:T(8,128)(2,1)S(1)}, bf16[80,1792]{1,0:T(8,128)(2,1)S(1)}, u32[]{:S(2)}, u32[]{:S(2)}) %collective-permute-start.8) | collective-permute-done | bytes 286752 | tf_op jit(solution)/shard_map/ppermute | solution.py:34
  71.6 2.5 %collective-permute-start.18 = (bf16[80,1792]{1,0:T(8,128)(2,1)S(1)}, bf16[80,1792]{1,0:T(8,128)(2,1)S(1)}, u32[]{:S(2)}, u32[]{:S(2)}) collective-permute-start(bf16[80,1792]{1,0:T(8,128)(2,1)S(1)} %get-tuple-element.67), channel_id=1, source_target_pairs={{0,12},{1,13},{2,14},{3,15},{4,0},{5,1},{6,2},{7,3},{8,4},{9,5},{1... | collective-permute-start | bytes 860168 | tf_op jit(solution)/shard_map/ppermute | solution.py:34
  74.1 0.5 leave.2
  74.6 0.6 collective-permute-start.22
  75.2 0.1 add_convert_fusion.1
  75.3 2.4 %collective-permute-done.20.refs_4_ = bf16[80,1792]{1,0:T(8,128)(2,1)S(1)} collective-permute-done((bf16[80,1792]{1,0:T(8,128)(2,1)S(1)}, bf16[80,1792]{1,0:T(8,128)(2,1)S(1)}, u32[]{:S(2)}, u32[]{:S(2)}) %collective-permute-start.20) | collective-permute-done | bytes 286752 | tf_op jit(solution)/shard_map/ppermute | solution.py:34
  77.7 0.7 collective-permute-start.16
  78.5 1.8 %collective-permute-done.21.refs_5_ = bf16[80,1792]{1,0:T(8,128)(2,1)S(1)} collective-permute-done((bf16[80,1792]{1,0:T(8,128)(2,1)S(1)}, bf16[80,1792]{1,0:T(8,128)(2,1)S(1)}, u32[]{:S(2)}, u32[]{:S(2)}) %collective-permute-start.21) | collective-permute-done | bytes 286752 | tf_op jit(solution)/shard_map/ppermute | solution.py:34
  80.2 2.6 %collective-permute-start.15 = (bf16[80,1792]{1,0:T(8,128)(2,1)S(1)}, bf16[80,1792]{1,0:T(8,128)(2,1)S(1)}, u32[]{:S(2)}, u32[]{:S(2)}) collective-permute-start(bf16[80,1792]{1,0:T(8,128)(2,1)S(1)} %add_convert_fusion.1), channel_id=1, source_target_pairs={{0,8},{1,9},{2,10},{3,11},{4,12},{5,13},{6,14},{7,15},{8,0},{9,1},... | collective-permute-start | bytes 860168 | tf_op jit(solution)/shard_map/ppermute | solution.py:34
  82.8 1.0 collective-permute-done.18.refs_1_
  83.9 2.5 %collective-permute-done.19.refs_2_ = bf16[80,1792]{1,0:T(8,128)(2,1)S(1)} collective-permute-done((bf16[80,1792]{1,0:T(8,128)(2,1)S(1)}, bf16[80,1792]{1,0:T(8,128)(2,1)S(1)}, u32[]{:S(2)}, u32[]{:S(2)}) %collective-permute-start.19) | collective-permute-done | bytes 286752 | tf_op jit(solution)/shard_map/ppermute | solution.py:34
  86.4 0.4 leave.3
  86.8 0.6 collective-permute-start.24
  87.5 0.1 add_convert_fusion
  87.6 1.9 %collective-permute-start.23 = (bf16[80,1792]{1,0:T(8,128)(2,1)S(1)}, bf16[80,1792]{1,0:T(8,128)(2,1)S(1)}, u32[]{:S(2)}, u32[]{:S(2)}) collective-permute-start(bf16[80,1792]{1,0:T(8,128)(2,1)S(1)} %add_convert_fusion), channel_id=1, source_target_pairs={{0,8},{1,9},{2,10},{3,11},{4,12},{5,13},{6,14},{7,15},{8,0},{9,1},... | collective-permute-start | bytes 860168 | tf_op jit(solution)/shard_map/ppermute | solution.py:34
  89.5 0.8 collective-permute-done.15.refs_6_
  90.2 3.0 %collective-permute-done.16.refs_7_ = bf16[128,1792]{1,0:T(8,128)(2,1)S(1)} collective-permute-done((bf16[128,1792]{1,0:T(8,128)(2,1)S(1)}, bf16[128,1792]{1,0:T(8,128)(2,1)S(1)}, u32[]{:S(2)}, u32[]{:S(2)}) %collective-permute-start.16) | collective-permute-done | bytes 458784 | tf_op jit(solution)/shard_map/ppermute | solution.py:34
  93.3 0.7 stay.2
  94.0 4.4 %collective-permute-start.17 = (bf16[128,1792]{1,0:T(8,128)(2,1)S(1)}, bf16[128,1792]{1,0:T(8,128)(2,1)S(1)}, u32[]{:S(2)}, u32[]{:S(2)}) collective-permute-start(bf16[128,1792]{1,0:T(8,128)(2,1)S(1)} %stay.2), channel_id=1, source_target_pairs={{0,16},{1,17},{2,18},{3,19},{4,20},{5,21},{6,22},{7,23},{8,24},{9,... | collective-permute-start | bytes 1376264 | tf_op jit(solution)/shard_map/ppermute | solution.py:43
  98.3 0.5 collective-permute-done.24.refs_7_
  98.9 0.7 stay.3
  99.6 3.4 %collective-permute-start.25 = (bf16[128,1792]{1,0:T(8,128)(2,1)S(1)}, bf16[128,1792]{1,0:T(8,128)(2,1)S(1)}, u32[]{:S(2)}, u32[]{:S(2)}) collective-permute-start(bf16[128,1792]{1,0:T(8,128)(2,1)S(1)} %stay.3), channel_id=1, source_target_pairs={{0,16},{1,17},{2,18},{3,19},{4,20},{5,21},{6,22},{7,23},{8,24},{9,... | collective-permute-start | bytes 1376264 | tf_op jit(solution)/shard_map/ppermute | solution.py:43
  102.9 9.7 %collective-permute-done.17 = bf16[128,1792]{1,0:T(8,128)(2,1)S(1)} collective-permute-done((bf16[128,1792]{1,0:T(8,128)(2,1)S(1)}, bf16[128,1792]{1,0:T(8,128)(2,1)S(1)}, u32[]{:S(2)}, u32[]{:S(2)}) %collective-permute-start.17) | collective-permute-done | bytes 458784 | tf_op jit(solution)/shard_map/ppermute | solution.py:43
  112.6 4.9 %collective-permute-done.25 = bf16[128,1792]{1,0:T(8,128)(2,1)S(1)} collective-permute-done((bf16[128,1792]{1,0:T(8,128)(2,1)S(1)}, bf16[128,1792]{1,0:T(8,128)(2,1)S(1)}, u32[]{:S(2)}, u32[]{:S(2)}) %collective-permute-start.25) | collective-permute-done | bytes 458784 | tf_op jit(solution)/shard_map/ppermute | solution.py:43
  117.5 1.0 maximum_bitcast_fusion
  (31 shorter events, 0.1 us)
Async XLA Ops:
  0.0 23.1 %collective-permute-start.1 = (bf16[3584,512]{1,0:T(8,128)(2,1)}, bf16[3584,512]{1,0:T(8,128)(2,1)}, u32[]{:S(2)}, u32[]{:S(2)}) collective-permute-start(bf16[3584,512]{1,0:T(8,128)(2,1)} %bitcast.14), channel_id=1, source_target_pairs={{0,1},{1,0},{2,3},{3,2},{4,5},{5,4},{6,7},{7,6},{8,9},{9,8},{10,11... | collective-permute-start | bytes 11010056 | tf_op jit(solution)/shard_map/ppermute | solution.py:34
  0.0 23.1 %collective-permute-start.2 = (bf16[3584,512]{1,0:T(8,128)(2,1)}, bf16[3584,512]{1,0:T(8,128)(2,1)}, u32[]{:S(2)}, u32[]{:S(2)}) collective-permute-start(bf16[3584,512]{1,0:T(8,128)(2,1)} %bitcast.16), channel_id=1, source_target_pairs={{0,1},{1,0},{2,3},{3,2},{4,5},{5,4},{6,7},{7,6},{8,9},{9,8},{10,11... | collective-permute-start | bytes 11010056 | tf_op jit(solution)/shard_map/ppermute | solution.py:34
  0.5 22.6 %collective-permute-start.3 = (bf16[512,3584]{1,0:T(8,128)(2,1)}, bf16[512,3584]{1,0:T(8,128)(2,1)}, u32[]{:S(2)}, u32[]{:S(2)}) collective-permute-start(bf16[512,3584]{1,0:T(8,128)(2,1)} %bitcast.18), channel_id=1, source_target_pairs={{0,1},{1,0},{2,3},{3,2},{4,5},{5,4},{6,7},{7,6},{8,9},{9,8},{10,11... | collective-permute-start | bytes 11010056 | tf_op jit(solution)/shard_map/ppermute | solution.py:34
  4.1 24.1 %collective-permute-start = (bf16[128,3712]{1,0:T(8,128)(2,1)}, bf16[128,3712]{1,0:T(8,128)(2,1)S(1)}, u32[]{:S(2)}, u32[]{:S(2)}) collective-permute-start(bf16[128,3712]{1,0:T(8,128)(2,1)} %get-tuple-element.40.refs_8_), channel_id=1, source_target_pairs={{0,2},{1,3},{2,0},{3,1},{4,6},{5,7},{6,4},{7,5},{8,10},{9,11},{10,... | collective-permute-start | bytes 2850824 | tf_op jit(solution)/shard_map/ppermute | solution.py:34
  5.7 16.9 %collective-permute-start.4 = (bf16[80,3584]{1,0:T(8,128)(2,1)}, bf16[80,3584]{1,0:T(8,128)(2,1)}, u32[]{:S(2)}, u32[]{:S(2)}) collective-permute-start(bf16[80,3584]{1,0:T(8,128)(2,1)} %get-tuple-element.47), channel_id=1, source_target_pairs={{0,8},{1,9},{2,10},{3,11},{4,12},{5,13},{6,14},{7,15},{8,0},{9,1},... | collective-permute-start | bytes 1720328 | tf_op jit(solution)/shard_map/ppermute | solution.py:34
  22.6 19.8 %collective-permute-start.7 = (bf16[80,3584]{1,0:T(8,128)(2,1)}, bf16[80,3584]{1,0:T(8,128)(2,1)S(1)}, u32[]{:S(2)}, u32[]{:S(2)}) collective-permute-start(bf16[80,3584]{1,0:T(8,128)(2,1)} %collective-permute-done.4.refs_1_), channel_id=1, source_target_pairs={{0,2},{1,3},{2,0},{3,1},{4,6},{5,7},{6,4},{7,5},{8,10},{9,11},{10,... | collective-permute-start | bytes 1720328 | tf_op jit(solution)/shard_map/ppermute | solution.py:34
  23.1 5.1 %copy-start.5 = (f32[1,3584]{1,0:T(1,128)S(1)}, f32[1,3584]{1,0:T(1,128)}, u32[]{:S(2)}) copy-start(f32[1,3584]{1,0:T(1,128)} %refs_2_.3) | copy-start | bytes 43012
  23.1 9.9 %copy-start.2 = (bf16[80,3584]{1,0:T(8,128)(2,1)S(1)}, bf16[80,3584]{1,0:T(8,128)(2,1)}, u32[]{:S(2)}) copy-start(bf16[80,3584]{1,0:T(8,128)(2,1)} %get-tuple-element.46.refs_0_) | copy-start | bytes 1720324
  23.1 19.3 %collective-permute-start.5 = (bf16[80,3584]{1,0:T(8,128)(2,1)}, bf16[80,3584]{1,0:T(8,128)(2,1)}, u32[]{:S(2)}, u32[]{:S(2)}) collective-permute-start(bf16[80,3584]{1,0:T(8,128)(2,1)} %get-tuple-element.43.refs_3_), channel_id=1, source_target_pairs={{0,4},{1,5},{2,6},{3,7},{4,8},{5,9},{6,10},{7,11},{8,12},{9,13},{1... | collective-permute-start | bytes 1720328 | tf_op jit(solution)/shard_map/ppermute | solution.py:34
  24.7 17.8 %collective-permute-start.6 = (bf16[80,3584]{1,0:T(8,128)(2,1)}, bf16[80,3584]{1,0:T(8,128)(2,1)}, u32[]{:S(2)}, u32[]{:S(2)}) collective-permute-start(bf16[80,3584]{1,0:T(8,128)(2,1)} %get-tuple-element.44.refs_4_), channel_id=1, source_target_pairs={{0,12},{1,13},{2,14},{3,15},{4,0},{5,1},{6,2},{7,3},{8,4},{9,5},{1... | collective-permute-start | bytes 1720328 | tf_op jit(solution)/shard_map/ppermute | solution.py:34
  30.0 0.8 copy-start.3
  30.8 20.2 %collective-permute-start.10 = (bf16[80,3584]{1,0:T(8,128)(2,1)}, bf16[80,3584]{1,0:T(8,128)(2,1)S(1)}, u32[]{:S(2)}, u32[]{:S(2)}) collective-permute-start(bf16[80,3584]{1,0:T(8,128)(2,1)} %get-tuple-element.59), channel_id=1, source_target_pairs={{0,4},{1,5},{2,6},{3,7},{4,8},{5,9},{6,10},{7,11},{8,12},{9,13},{1... | collective-permute-start | bytes 1720328 | tf_op jit(solution)/shard_map/ppermute | solution.py:34
  32.3 18.8 %collective-permute-start.11 = (bf16[80,3584]{1,0:T(8,128)(2,1)}, bf16[80,3584]{1,0:T(8,128)(2,1)S(1)}, u32[]{:S(2)}, u32[]{:S(2)}) collective-permute-start(bf16[80,3584]{1,0:T(8,128)(2,1)} %get-tuple-element.60), channel_id=1, source_target_pairs={{0,12},{1,13},{2,14},{3,15},{4,0},{5,1},{6,2},{7,3},{8,4},{9,5},{1... | collective-permute-start | bytes 1720328 | tf_op jit(solution)/shard_map/ppermute | solution.py:34
  33.1 9.5 %copy-start.4 = (bf16[80,3584]{1,0:T(8,128)(2,1)S(1)}, bf16[80,3584]{1,0:T(8,128)(2,1)}, u32[]{:S(2)}) copy-start(bf16[80,3584]{1,0:T(8,128)(2,1)} %copy-done.3) | copy-start | bytes 1720324
  51.0 23.1 %copy-start.1 = (bf16[4,80,256]{2,1,0:T(8,128)(2,1)S(1)}, bf16[4,80,256]{2,1,0:T(8,128)(2,1)}, u32[]{:S(2)}) copy-start(bf16[4,80,256]{2,1,0:T(8,128)(2,1)} %get-tuple-element.39.w_own_ref) | copy-start | bytes 491524
  54.8 10.6 %collective-permute-start.12 = (bf16[80,1792]{1,0:T(8,128)(2,1)S(1)}, bf16[80,1792]{1,0:T(8,128)(2,1)S(1)}, u32[]{:S(2)}, u32[]{:S(2)}) collective-permute-start(bf16[80,1792]{1,0:T(8,128)(2,1)S(1)} %get-tuple-element.62), channel_id=1, source_target_pairs={{0,12},{1,13},{2,14},{3,15},{4,0},{5,1},{6,2},{7,3},{8,4},{9,5},{1... | collective-permute-start | bytes 860168 | tf_op jit(solution)/shard_map/ppermute | solution.py:34
  58.2 9.8 %collective-permute-start.13 = (bf16[80,1792]{1,0:T(8,128)(2,1)S(1)}, bf16[80,1792]{1,0:T(8,128)(2,1)S(1)}, u32[]{:S(2)}, u32[]{:S(2)}) collective-permute-start(bf16[80,1792]{1,0:T(8,128)(2,1)S(1)} %get-tuple-element.63), channel_id=1, source_target_pairs={{0,4},{1,5},{2,6},{3,7},{4,8},{5,9},{6,10},{7,11},{8,12},{9,13},{1... | collective-permute-start | bytes 860168 | tf_op jit(solution)/shard_map/ppermute | solution.py:34
  58.2 13.4 %collective-permute-start.8 = (bf16[80,1792]{1,0:T(8,128)(2,1)S(1)}, bf16[80,1792]{1,0:T(8,128)(2,1)S(1)}, u32[]{:S(2)}, u32[]{:S(2)}) collective-permute-start(bf16[80,1792]{1,0:T(8,128)(2,1)S(1)} %get-tuple-element.56), channel_id=1, source_target_pairs={{0,12},{1,13},{2,14},{3,15},{4,0},{5,1},{6,2},{7,3},{8,4},{9,5},{1... | collective-permute-start | bytes 860168 | tf_op jit(solution)/shard_map/ppermute | solution.py:34
  60.2 13.9 %collective-permute-start.9 = (bf16[80,1792]{1,0:T(8,128)(2,1)S(1)}, bf16[80,1792]{1,0:T(8,128)(2,1)S(1)}, u32[]{:S(2)}, u32[]{:S(2)}) collective-permute-start(bf16[80,1792]{1,0:T(8,128)(2,1)S(1)} %get-tuple-element.57), channel_id=1, source_target_pairs={{0,4},{1,5},{2,6},{3,7},{4,8},{5,9},{6,10},{7,11},{8,12},{9,13},{1... | collective-permute-start | bytes 860168 | tf_op jit(solution)/shard_map/ppermute | solution.py:34
  60.2 14.3 %collective-permute-start.14 = (bf16[80,1792]{1,0:T(8,128)(2,1)S(1)}, bf16[80,1792]{1,0:T(8,128)(2,1)S(1)}, u32[]{:S(2)}, u32[]{:S(2)}) collective-permute-start(bf16[80,1792]{1,0:T(8,128)(2,1)S(1)} %broadcast_select_fusion.1), channel_id=1, source_target_pairs={{0,2},{1,3},{2,0},{3,1},{4,6},{5,7},{6,4},{7,5},{8,10},{9,11},{10,... | collective-permute-start | bytes 860168 | tf_op jit(solution)/shard_map/ppermute | solution.py:34
  60.9 32.4 %copy-start = (bf16[128,3712]{1,0:T(8,128)(2,1)S(1)}, bf16[128,3712]{1,0:T(8,128)(2,1)}, u32[]{:S(2)}) copy-start(bf16[128,3712]{1,0:T(8,128)(2,1)} %get-tuple-element.40.refs_8_) | copy-start | bytes 2850820
  65.5 12.3 %collective-permute-start.20 = (bf16[80,1792]{1,0:T(8,128)(2,1)S(1)}, bf16[80,1792]{1,0:T(8,128)(2,1)S(1)}, u32[]{:S(2)}, u32[]{:S(2)}) collective-permute-start(bf16[80,1792]{1,0:T(8,128)(2,1)S(1)} %get-tuple-element.69), channel_id=1, source_target_pairs={{0,12},{1,13},{2,14},{3,15},{4,0},{5,1},{6,2},{7,3},{8,4},{9,5},{1... | collective-permute-start | bytes 860168 | tf_op jit(solution)/shard_map/ppermute | solution.py:34
  67.9 12.3 %collective-permute-start.21 = (bf16[80,1792]{1,0:T(8,128)(2,1)S(1)}, bf16[80,1792]{1,0:T(8,128)(2,1)S(1)}, u32[]{:S(2)}, u32[]{:S(2)}) collective-permute-start(bf16[80,1792]{1,0:T(8,128)(2,1)S(1)} %get-tuple-element.70), channel_id=1, source_target_pairs={{0,4},{1,5},{2,6},{3,7},{4,8},{5,9},{6,10},{7,11},{8,12},{9,13},{1... | collective-permute-start | bytes 860168 | tf_op jit(solution)/shard_map/ppermute | solution.py:34
  71.6 12.3 %collective-permute-start.18 = (bf16[80,1792]{1,0:T(8,128)(2,1)S(1)}, bf16[80,1792]{1,0:T(8,128)(2,1)S(1)}, u32[]{:S(2)}, u32[]{:S(2)}) collective-permute-start(bf16[80,1792]{1,0:T(8,128)(2,1)S(1)} %get-tuple-element.67), channel_id=1, source_target_pairs={{0,12},{1,13},{2,14},{3,15},{4,0},{5,1},{6,2},{7,3},{8,4},{9,5},{1... | collective-permute-start | bytes 860168 | tf_op jit(solution)/shard_map/ppermute | solution.py:34
  74.1 12.3 %collective-permute-start.19 = (bf16[80,1792]{1,0:T(8,128)(2,1)S(1)}, bf16[80,1792]{1,0:T(8,128)(2,1)S(1)}, u32[]{:S(2)}, u32[]{:S(2)}) collective-permute-start(bf16[80,1792]{1,0:T(8,128)(2,1)S(1)} %get-tuple-element.68), channel_id=1, source_target_pairs={{0,4},{1,5},{2,6},{3,7},{4,8},{5,9},{6,10},{7,11},{8,12},{9,13},{1... | collective-permute-start | bytes 860168 | tf_op jit(solution)/shard_map/ppermute | solution.py:34
  74.6 12.9 %collective-permute-start.22 = (bf16[80,1792]{1,0:T(8,128)(2,1)S(1)}, bf16[80,1792]{1,0:T(8,128)(2,1)S(1)}, u32[]{:S(2)}, u32[]{:S(2)}) collective-permute-start(bf16[80,1792]{1,0:T(8,128)(2,1)S(1)} %broadcast_select_fusion), channel_id=1, source_target_pairs={{0,2},{1,3},{2,0},{3,1},{4,6},{5,7},{6,4},{7,5},{8,10},{9,11},{10,... | collective-permute-start | bytes 860168 | tf_op jit(solution)/shard_map/ppermute | solution.py:34
  77.7 15.5 %collective-permute-start.16 = (bf16[128,1792]{1,0:T(8,128)(2,1)S(1)}, bf16[128,1792]{1,0:T(8,128)(2,1)S(1)}, u32[]{:S(2)}, u32[]{:S(2)}) collective-permute-start(bf16[128,1792]{1,0:T(8,128)(2,1)S(1)} %leave.2), channel_id=1, source_target_pairs={{0,2},{1,3},{2,0},{3,1},{4,6},{5,7},{6,4},{7,5},{8,10},{9,11},{10,... | collective-permute-start | bytes 1376264 | tf_op jit(solution)/shard_map/ppermute | solution.py:34
  80.2 10.0 %collective-permute-start.15 = (bf16[80,1792]{1,0:T(8,128)(2,1)S(1)}, bf16[80,1792]{1,0:T(8,128)(2,1)S(1)}, u32[]{:S(2)}, u32[]{:S(2)}) collective-permute-start(bf16[80,1792]{1,0:T(8,128)(2,1)S(1)} %add_convert_fusion.1), channel_id=1, source_target_pairs={{0,8},{1,9},{2,10},{3,11},{4,12},{5,13},{6,14},{7,15},{8,0},{9,1},... | collective-permute-start | bytes 860168 | tf_op jit(solution)/shard_map/ppermute | solution.py:34
  86.8 12.0 %collective-permute-start.24 = (bf16[128,1792]{1,0:T(8,128)(2,1)S(1)}, bf16[128,1792]{1,0:T(8,128)(2,1)S(1)}, u32[]{:S(2)}, u32[]{:S(2)}) collective-permute-start(bf16[128,1792]{1,0:T(8,128)(2,1)S(1)} %leave.3), channel_id=1, source_target_pairs={{0,2},{1,3},{2,0},{3,1},{4,6},{5,7},{6,4},{7,5},{8,10},{9,11},{10,... | collective-permute-start | bytes 1376264 | tf_op jit(solution)/shard_map/ppermute | solution.py:34
  87.6 10.8 %collective-permute-start.23 = (bf16[80,1792]{1,0:T(8,128)(2,1)S(1)}, bf16[80,1792]{1,0:T(8,128)(2,1)S(1)}, u32[]{:S(2)}, u32[]{:S(2)}) collective-permute-start(bf16[80,1792]{1,0:T(8,128)(2,1)S(1)} %add_convert_fusion), channel_id=1, source_target_pairs={{0,8},{1,9},{2,10},{3,11},{4,12},{5,13},{6,14},{7,15},{8,0},{9,1},... | collective-permute-start | bytes 860168 | tf_op jit(solution)/shard_map/ppermute | solution.py:34
  94.0 18.6 %collective-permute-start.17 = (bf16[128,1792]{1,0:T(8,128)(2,1)S(1)}, bf16[128,1792]{1,0:T(8,128)(2,1)S(1)}, u32[]{:S(2)}, u32[]{:S(2)}) collective-permute-start(bf16[128,1792]{1,0:T(8,128)(2,1)S(1)} %stay.2), channel_id=1, source_target_pairs={{0,16},{1,17},{2,18},{3,19},{4,20},{5,21},{6,22},{7,23},{8,24},{9,... | collective-permute-start | bytes 1376264 | tf_op jit(solution)/shard_map/ppermute | solution.py:43
  99.6 17.9 %collective-permute-start.25 = (bf16[128,1792]{1,0:T(8,128)(2,1)S(1)}, bf16[128,1792]{1,0:T(8,128)(2,1)S(1)}, u32[]{:S(2)}, u32[]{:S(2)}) collective-permute-start(bf16[128,1792]{1,0:T(8,128)(2,1)S(1)} %stay.3), channel_id=1, source_target_pairs={{0,16},{1,17},{2,18},{3,19},{4,20},{5,21},{6,22},{7,23},{8,24},{9,... | collective-permute-start | bytes 1376264 | tf_op jit(solution)/shard_map/ppermute | solution.py:43

commit v3 on v2

v3 whole, which is shorter than its diff:
```python
import functools

import jax
import jax.numpy as jnp
from jax import lax
from jax.experimental import pallas as pl
from jax.experimental.pallas import tpu as pltpu
from jax.sharding import PartitionSpec as P

EXPERTS = 4
CAP = 80
PARTS = (1792, 1792)
LAYERS = 8
TILE = 256
PACK = 128
LOAD = 46
BRING = 34
FREE = pl.CostEstimate(flops=0, bytes_accessed=0, transcendentals=0)
F32 = jnp.float32
BF16 = jnp.bfloat16
VMEM = pl.BlockSpec(memory_space=pltpu.VMEM)
SMEM = pl.BlockSpec(memory_space=pltpu.SMEM)
ANY = pl.BlockSpec(memory_space=pl.ANY)
HBM = pl.BlockSpec(memory_space=pltpu.HBM)


def limit(mebibytes):
    return pltpu.CompilerParams(vmem_limit_bytes=mebibytes << 20)


def moved(value, dx, dy, dc):
    pairs = []
    for i in range(16):
        x, y, c = i // 4, (i // 2) % 2, i % 2
        pairs.append((i, ((x + dx) % 4) * 4 + ((y + dy) % 2) * 2 + (c + dc) % 2))
    return lax.ppermute(value, "expert", pairs)


def handed_on(value):
    pairs = []
    for s in range(16):
        for e in range(16):
            to = e ^ 2 if s % LAYERS == LAYERS - 1 else e
            pairs.append((s * 16 + e, ((s + 1) % 16) * 16 + to))
    return lax.ppermute(value, ("section", "expert"), pairs)


def first_route_kernel(flags_ref, *refs):
    far, refs = refs[:4], refs[4:]
    *refs, sent_ref, gain_ref, ids_ref, gv_ref, sems = refs
    count, dim = far[0].shape
    near = (sent_ref.at[:, :dim], gain_ref, ids_ref, gv_ref)
    copies = [pltpu.make_async_copy(a, b, sems.at[i]) for i, (a, b) in enumerate(zip(far, near))]
    for copy in copies:
        copy.start()
    for copy in copies:
        copy.wait()
    ids, gv = ids_ref[...], gv_ref[...]
    high = gv.astype(BF16).astype(F32)
    middle = (gv - high).astype(BF16).astype(F32)
    low = gv - high - middle
    packed = jnp.concatenate([ids.astype(F32), high, middle, low], axis=0)
    packed = jnp.concatenate([packed, jnp.zeros((PACK - 8, count), F32)], axis=0)
    sent_ref[:, dim:] = packed.T.astype(BF16)
    route_kernel((0, 1, 2, 3), flags_ref, sent_ref, gain_ref, ids, gv, *refs)


def second_route_kernel(flags_ref, sent_ref, gain_ref, *refs):
    packed = sent_ref[:, gain_ref.shape[1] :].astype(F32).T
    ids = packed[0:2].astype(jnp.int32)
    gv = packed[2:4] + packed[4:6] + packed[6:8]
    route_kernel((0, 1, 3), flags_ref, sent_ref, gain_ref, ids, gv, *refs)


def route_kernel(kinds, flags_ref, tok_ref, gain_ref, ids, gv, *refs):
    w_ref = refs[-1]
    out_refs = dict(zip(kinds, refs[-1 - len(kinds) : -1]))
    wide = tok_ref[:, : gain_ref.shape[1]].astype(F32)
    scale = lax.rsqrt(jnp.mean(wide * wide, axis=-1, keepdims=True) + 1e-06)
    normed = (wide * scale * gain_ref[...]).astype(BF16)
    count = normed.shape[0]
    ids = jnp.bitwise_and(ids + (EXPERTS - flags_ref[0]), EXPERTS - 1)
    first, second = ids[0:1, :], ids[1:2, :]
    kind = lax.broadcasted_iota(jnp.int32, (16, count), 0)
    chosen = (kind == first) | (kind == second)
    before = (
        lax.broadcasted_iota(jnp.int32, (count, count), 0)
        < lax.broadcasted_iota(jnp.int32, (count, count), 1)
    )
    place = jnp.dot(
        chosen.astype(F32).astype(BF16), before.astype(F32).astype(BF16), preferred_element_type=F32
    )
    weight = jnp.where(kind == first, gv[0:1, :], 0.0) + jnp.where(
        kind == second, gv[1:2, :], 0.0
    )
    slot = lax.broadcasted_iota(jnp.int32, (CAP, count), 0).astype(F32)
    for d in range(EXPERTS):
        spot = jnp.where(chosen[d : d + 1, :], place[d : d + 1, :], -1.0)
        hit = slot == spot
        pick = jnp.where(hit, 1.0, 0.0).astype(BF16)
        if d in out_refs:
            out_refs[d][...] = jnp.dot(pick, normed, preferred_element_type=F32).astype(BF16)
        full = jnp.where(hit, weight[d : d + 1, :], 0.0)
        high = full.astype(BF16)
        low = (full - high.astype(F32)).astype(BF16)
        w_ref[d] = jnp.concatenate([high, low], axis=1)


def route(first_set, flags, tok, gain, choices, others):
    count, dim = tok.shape[0], gain.shape[1]
    blocks = 4 if first_set else 3
    out_shape = [jax.ShapeDtypeStruct((CAP, dim), BF16)] * blocks
    out_shape.append(jax.ShapeDtypeStruct((EXPERTS, CAP, 2 * count), BF16))
    kernel, scratch = second_route_kernel, []
    if first_set:
        kernel = first_route_kernel
        out_shape.append(jax.ShapeDtypeStruct((count, dim + PACK), BF16))
        scratch = [pltpu.VMEM(v.shape, v.dtype) for v in (gain, *choices)]
        scratch.append(pltpu.SemaphoreType.DMA((4,)))
    operands = (tok, gain, *choices)
    inner = 1 + len(operands)

    def body(*refs):
        kernel(*refs[:inner], *refs[inner + len(others) :])

    return pl.pallas_call(
        body,
        out_shape=out_shape,
        in_specs=[SMEM] + [HBM if first_set else VMEM] * len(operands) + [ANY] * len(others),
        out_specs=[VMEM] * len(out_shape),
        scratch_shapes=scratch,
        cost_estimate=FREE,
        compiler_params=limit(58 if first_set else 12),
        name="route",
    )(flags, *operands, *others)


def hidden_tile(rows_ref, gate_ref, up_ref, hidden_ref, at, to):
    columns = pl.ds(at, TILE)
    gate = jnp.dot(rows_ref[...], gate_ref[:, columns], preferred_element_type=F32)
    upward = jnp.dot(rows_ref[...], up_ref[:, columns], preferred_element_type=F32)
    hidden_ref[:, pl.ds(to, TILE)] = (jax.nn.silu(gate) * upward).astype(BF16)


def load_kernel(count, *refs):
    sems = refs[-1]
    copies = [
        pltpu.make_async_copy(refs[i], refs[i - 1 - count], sems.at[i]) for i in range(count)
    ]
    for copy in copies:
        copy.start()
    for copy in copies:
        copy.wait()


def load(weights, others, room):
    count = len(weights)
    return pl.pallas_call(
        functools.partial(load_kernel, count),
        out_shape=[jax.ShapeDtypeStruct(w.shape, BF16) for w in weights],
        in_specs=[HBM] * count + [ANY] * len(others),
        out_specs=[VMEM] * count,
        scratch_shapes=[pltpu.SemaphoreType.DMA((count,))],
        cost_estimate=FREE,
        compiler_params=limit(room),
        name="load",
    )(*weights, *others)


def expert_kernel(splits, far, flags_ref, *refs):
    blocks = len(splits)
    rows_in, weights, refs = refs[:blocks], refs[blocks : blocks + 6], refs[blocks + 6 :]
    far_refs, refs = refs[:far], refs[far:]
    *outs, rows_ref, hidden_ref = refs
    dim, units = weights[0].shape
    for i, ref in enumerate(rows_in):
        rows_ref[i * CAP : (i + 1) * CAP, :] = ref[...]
    for half in range(2):
        for at in range(0, units, TILE):
            hidden_tile(
                rows_ref, weights[3 * half], weights[3 * half + 1], hidden_ref, at, half * units + at
            )
    for at in range(0, dim, TILE):
        columns = slice(at, at + TILE)
        total = jnp.dot(
            hidden_ref[:, :units], weights[2][:, columns], preferred_element_type=F32
        ) + jnp.dot(hidden_ref[:, units:], weights[5][:, columns], preferred_element_type=F32)
        first = 0
        for i, split in enumerate(splits):
            part = total[i * CAP : (i + 1) * CAP].astype(BF16)
            chunk = sum(1 for k in range(len(split)) if at >= sum(split[: k + 1]))
            to = at - sum(split[:chunk])
            outs[first + chunk][:, to : to + TILE] = part
            first += len(split)
    if far:
        far_ref, cross_ref, kept_ref = far_refs[0], outs[0], outs[-1]

        @pl.when(flags_ref[1] == 0)
        def _():
            kept_ref[...] = far_ref[...]

        @pl.when(flags_ref[1] != 0)
        def _():
            kept_ref[...] = cross_ref[...]
            cross_ref[...] = far_ref[...]


def expert(flags, rows, weights, splits, far=(), others=()):
    blocks, dim = len(rows), rows[0].shape[1]
    units = weights[0].shape[1]
    inner = 1 + blocks + 6 + len(far)
    out_shape = [
        jax.ShapeDtypeStruct((CAP, width), BF16) for split in splits for width in split
    ] + [jax.ShapeDtypeStruct((CAP, dim), BF16)] * len(far)
    scratch = [
        pltpu.VMEM((blocks * CAP, dim), BF16),
        pltpu.VMEM((blocks * CAP, 2 * units), BF16),
    ]

    def body(*refs):
        expert_kernel(splits, len(far), *refs[:inner], *refs[inner + len(others) :])

    outs = pl.pallas_call(
        body,
        out_shape=out_shape,
        in_specs=[SMEM]
        + [VMEM] * (blocks + 6 + len(far))
        + [ANY] * len(others),
        out_specs=[VMEM] * len(out_shape),
        scratch_shapes=scratch,
        cost_estimate=FREE,
        compiler_params=limit(10),
        name="expert",
    )(flags, *rows, *weights, *far, *others)
    grouped, first = [], 0
    for split in splits:
        group = outs[first : first + len(split)]
        grouped.append(group if len(split) > 1 else group[0])
        first += len(split)
    return grouped, list(outs[first:])


def add_kernel(a_ref, b_ref, *out_refs):
    at = 0
    for ref in out_refs:
        columns = slice(at, at + ref.shape[1])
        ref[...] = (a_ref[:, columns].astype(F32) + b_ref[:, columns].astype(F32)).astype(BF16)
        at += ref.shape[1]


def added(a, b):
    return pl.pallas_call(
        add_kernel,
        out_shape=[jax.ShapeDtypeStruct((a.shape[0], width), a.dtype) for width in PARTS],
        in_specs=[VMEM] * 2,
        out_specs=[VMEM] * len(PARTS),
        cost_estimate=FREE,
        compiler_params=limit(2),
        name="add",
    )(a, b)


def after_kernel(*refs):
    pass


def after(values, others):
    return pl.pallas_call(
        after_kernel,
        out_shape=[jax.ShapeDtypeStruct(v.shape, v.dtype) for v in values],
        in_specs=[ANY] * (len(values) + len(others)),
        out_specs=[ANY] * len(values),
        input_output_aliases={i: i for i in range(len(values))},
        cost_estimate=FREE,
        compiler_params=limit(1),
        name="after",
    )(*values, *others)


def weighted(w_ref, kinds, refs, columns):
    count = w_ref.shape[2] // 2
    weights = jnp.concatenate([w_ref[d] for d in kinds], axis=0)
    width = columns.stop - columns.start
    rows = jnp.concatenate(
        [ref[...] if ref.shape[1] == width else ref[:, columns] for ref in refs], axis=0
    )
    both = lax.dot_general(weights, rows, (((0,), (0,)), ((), ())), preferred_element_type=F32)
    return both[:count] + both[count:]


def leave_kernel(columns, flags_ref, w_own_ref, w_across_ref, *refs):
    own_refs, across_refs, out_ref = refs[:3], refs[3:6], refs[6]

    @pl.when(flags_ref[1] == 0)
    def _():
        out_ref[...] = weighted(w_across_ref, (0, 1, 3), across_refs, columns).astype(BF16)

    @pl.when(flags_ref[1] != 0)
    def _():
        out_ref[...] = weighted(w_own_ref, (0, 1, 3), own_refs, columns).astype(BF16)


def stay_kernel(columns, flags_ref, w_own_ref, w_across_ref, *refs):
    own_refs, across_refs = refs[:3], refs[3:6]
    far_ref, mine_ref, tok_ref, tok_across_ref, out_ref = refs[6:]

    def finish(w_ref, near, home_ref):
        total = weighted(w_ref, (0, 1, 3, 2), (*near, far_ref), columns)
        total += mine_ref[...].astype(F32) + home_ref[:, columns].astype(F32)
        out_ref[...] = total.astype(BF16)

    @pl.when(flags_ref[1] == 0)
    def _():
        finish(w_own_ref, own_refs, tok_ref)

    @pl.when(flags_ref[1] != 0)
    def _():
        finish(w_across_ref, across_refs, tok_across_ref)


def mix(chunk, kernel, name, flags, w_own, w_across, blocks):
    count, width = w_own.shape[2] // 2, PARTS[chunk]
    begin = sum(PARTS[:chunk])
    return pl.pallas_call(
        functools.partial(kernel, slice(begin, begin + width)),
        out_shape=jax.ShapeDtypeStruct((count, width), BF16),
        in_specs=[SMEM] + [VMEM] * (2 + len(blocks)),
        out_specs=VMEM,
        cost_estimate=FREE,
        compiler_params=limit(8),
        name=name,
    )(flags, w_own, w_across, *blocks)


def on_device(tokens, norm_gain, expert_ids, gate_values, gate_weight, up_weight, down_weight):
    tok = tokens[0]
    dim = tok.shape[1]
    column = lax.axis_index("expert") // 4
    swapped = lax.axis_index("section") % LAYERS == LAYERS - 1
    flags = jnp.stack([column.astype(jnp.int32), swapped.astype(jnp.int32)])
    ids = expert_ids[0].T
    gv = gate_values[0].T
    gates = (gate_weight[0], moved(gate_weight[0], 0, 0, 1))
    ups = (up_weight[0], moved(up_weight[0], 0, 0, 1))
    downs = (down_weight[0], moved(down_weight[0], 0, 0, 1))

    *own, w_own, sent = route(True, flags, tok, norm_gain, (ids, gv), ())
    tok_across = moved(sent, 0, 1, 0)
    own_far = moved(own[2], 2, 0, 0)
    held = load((gates[0], ups[0], downs[0]), (sent,), LOAD)
    right_rows, left_rows = after((own[1], own[3]), (gates[1], ups[1], downs[1], held[0]))
    own_right = moved(right_rows, 1, 0, 0)
    own_left = moved(left_rows, -1, 0, 0)
    held_more = load((gates[1], ups[1], downs[1]), (own_far,), BRING)
    (own_far,) = after((own_far,), (right_rows, left_rows, tok_across))
    across_far = moved(own_far, 0, 1, 0)
    kept = (*held, *held_more)
    whole, split = (dim,), PARTS
    *across, w_across = route(False, flags, tok_across, norm_gain, (), (kept[3],))
    (own_out, far_out, right_out, left_out), _ = expert(
        flags, (own[0], own_far, own_right, own_left), kept, (whole,) * 4
    )
    across_right = moved(across[1], 1, 0, 0)
    across_left = moved(across[2], -1, 0, 0)
    (far_cross, across_out), (far_kept,) = expert(
        flags, (across_far, across[0]), kept, (whole,) * 2, (far_out,)
    )
    (right_late, left_late), _ = expert(
        flags, (across_right, across_left), kept, (split,) * 2, others=(far_cross,)
    )
    my_right = moved(right_out, -1, 0, 0)
    my_left = moved(left_out, 1, 0, 0)
    far_in = moved(far_cross, 0, 1, 0)
    sums = added(far_kept, far_in)
    outs = []
    for k in range(len(PARTS)):
        right_rows, left_rows = right_late[k], left_late[k]
        if k > 0:
            right_rows, left_rows = after((right_rows, left_rows), (my_right, my_left))
        own_back = (own_out, my_right, my_left)
        across_back = (across_out, moved(right_rows, -1, 0, 0), moved(left_rows, 1, 0, 0))
        far_back = moved(sums[k], 2, 0, 0)
        leaving = mix(k, leave_kernel, "leave", flags, w_own, w_across, (*own_back, *across_back))
        if k > 0:
            (leaving,) = after((leaving,), (arrived,))
        mine, arrived = moved(leaving, 0, 1, 0), far_back
        layer_out = mix(
            k,
            stay_kernel,
            "stay",
            flags,
            w_own,
            w_across,
            (*own_back, *across_back, far_back, mine, sent, tok_across),
        )
        outs.append(handed_on(layer_out))
    return jnp.concatenate(outs, axis=1)[None]


def solution(mesh):
    in_specs = (
        P("section", "expert", None),
        P("section", None),
        P("section", "expert", None),
        P("section", "expert", None),
        P("section", None, "expert"),
        P("section", None, "expert"),
        P("section", "expert", None),
    )
    out_specs = P("section", "expert", None)
    return jax.shard_map(
        on_device, mesh=mesh, in_specs=in_specs, out_specs=out_specs, check_vma=False
    )
```

time: 119 us -> 111 us (0.933)
  waiting for transfers between devices: 52.3 us -> 41.3 us
  Pallas kernels: 29.3 us -> 37.3 us
  starting transfers between devices: 34.6 us -> 29.7 us
    ppermute x24 -> x21, waiting for transfers between devices: 37.7 us -> 25.2 us  [moved(): return lax.ppermute(value, 'expert', pairs)]
    pallas_call x7 -> x10, Pallas kernels: 24 us -> 31.7 us  [the longest x3 16.6 us: expert(): pl.pallas_call(body, out_shape=out_shape, in_specs=[SMEM] + [VMEM] * (blo...]
    ppermute x2, starting transfers between devices: 7.72 us -> 3.07 us  [handed_on(): return lax.ppermute(value, ('section', 'expert'), pairs)]
    ppermute x2, waiting for transfers between devices: 14.6 us -> 16.1 us  [handed_on(): return lax.ppermute(value, ('section', 'expert'), pairs)]
    ppermute x24 -> x21, starting transfers between devices: 26.9 us -> 26.6 us  [moved(): return lax.ppermute(value, 'expert', pairs)]
  transfers between devices with their start and end apart: 26 -> 23, of which waited for: 13 -> 13; matrix products, arithmetic and copies ran while one was open for 0% -> 1% of each run, Pallas kernels for 22% -> 34%
where the time goes in v3:
time: 111 us
  waiting for transfers between devices  41.3 us (37%)
  Pallas kernels  37.3 us (34%)
  starting transfers between devices  29.7 us (27%)
  other arithmetic  1.54 us (1%)
  local copies, waits for them, and re-layouts  1.22 us (1%)
    ppermute x21, starting transfers between devices, moved(): return lax.ppermute(value, 'expert', pairs)  26.6 us
    ppermute x21, waiting for transfers between devices, moved(): return lax.ppermute(value, 'expert', pairs)  25.2 us
    pallas_call x3, Pallas kernels, expert(): pl.pallas_call(body, out_shape=out_shape, in_specs=[SMEM] + [VMEM] * (blo...  16.6 us
    ppermute x2, waiting for transfers between devices, handed_on(): return lax.ppermute(value, ('section', 'expert'), pairs)  16.1 us
    pallas_call x2, Pallas kernels, load(): pl.pallas_call(functools.partial(load_kernel, count), out_shape=[jax.Shap...  10.4 us
    pallas_call x2, Pallas kernels, route(): pl.pallas_call(body, out_shape=out_shape, in_specs=[SMEM] + [HBM if first...  5.65 us
    pallas_call x4, Pallas kernels, mix(): pl.pallas_call(functools.partial(kernel, slice(begin, begin + width)), ou...  4.46 us
    ppermute x2, starting transfers between devices, handed_on(): return lax.ppermute(value, ('section', 'expert'), pairs)  3.07 us
  transfers between devices with their start and end apart: 23, of which 13 were waited for; matrix products, arithmetic and copies ran while one was open for 1% of the time, Pallas kernels for 34%

profile of v3, /device:TPU:2, one launch (start us, length us, event | category | flops | bytes accessed | tf_op | source)
XLA Modules:
  0.0 111.2 jit_solution(16900507505705162942)
XLA Ops:
  0.0 0.5 collective-permute-start.2
  0.5 0.6 pad_add_fusion.refs_0_.flags_ref
  1.1 4.2 %route.2 = (bf16[80,3584]{1,0:T(8,128)(2,1)}, bf16[80,3584]{1,0:T(8,128)(2,1)}, bf16[80,3584]{1,0:T(8,128)(2,1)}, bf16[80,3584]{1,0:T(8,128)(2,1)}, bf16[4,80,25...) custom-call(s32[2]{0:T(128)} %pad_add_fusion.refs_0_.flags_ref, bf16[128,3584]{1,0:T(8,128)(2,1)} %bitcast.20, ...), custom_call_target="tpu_custom_call" | custom-call | tf_op jit(solution)/shard_map/route/pallas_call | solution.py:126
  5.3 1.7 %collective-permute-start = (bf16[128,3712]{1,0:T(8,128)(2,1)}, bf16[128,3712]{1,0:T(8,128)(2,1)S(1)}, u32[]{:S(2)}, u32[]{:S(2)}) collective-permute-start(bf16[128,3712]{1,0:T(8,128)(2,1)} %get-tuple-element.39.refs_3_.refs_8_), channel_id=1, source_target_pairs={{0,2},{1,3},{2,0},{3,1},{4,6},{5,7},{6,4},{7,5},{8,10},{9,11},{10,... | collective-permute-start | bytes 2850824 | tf_op jit(solution)/shard_map/ppermute | solution.py:36
  7.0 2.1 %collective-permute-start.4 = (bf16[80,3584]{1,0:T(8,128)(2,1)}, bf16[80,3584]{1,0:T(8,128)(2,1)S(1)}, u32[]{:S(2)}, u32[]{:S(2)}) collective-permute-start(bf16[80,3584]{1,0:T(8,128)(2,1)} %get-tuple-element.40), channel_id=1, source_target_pairs={{0,8},{1,9},{2,10},{3,11},{4,12},{5,13},{6,14},{7,15},{8,0},{9,1},... | collective-permute-start | bytes 1720328 | tf_op jit(solution)/shard_map/ppermute | solution.py:36
  9.1 1.2 %copy-done.1 = bf16[128,3712]{1,0:T(8,128)(2,1)S(1)} copy-done((bf16[128,3712]{1,0:T(8,128)(2,1)S(1)}, bf16[128,3712]{1,0:T(8,128)(2,1)}, u32[]{:S(2)}) %copy-start.1) | copy-done | bytes 950296
  10.3 6.2 %load.3 = (bf16[3584,512]{1,0:T(8,128)(2,1)S(1)}, bf16[3584,512]{1,0:T(8,128)(2,1)S(1)}, bf16[512,3584]{1,0:T(8,128)(2,1)}) custom-call(bf16[3584,512]{1,0:T(8,128)(2,1)} %bitcast.15, bf16[3584,512]{1,0:T(8,128)(2,1)} %bitcast.17, bf16[512,3584]{1,0:T(8,128)(2,1)} %bitcast.19, bf16[128,3712]{1,0:T(8,128)(2,1)S(1)} %copy-done.1), custom_call_target="tpu_custom_call" | custom-call | tf_op jit(solution)/shard_map/load/pallas_call | solution.py:158
  16.5 0.7 collective-permute-done.3.refs_2_.refs_4_
  17.3 1.5 %collective-permute-start.5 = (bf16[80,3584]{1,0:T(8,128)(2,1)S(1)}, bf16[80,3584]{1,0:T(8,128)(2,1)S(1)}, u32[]{:S(2)}, u32[]{:S(2)}) collective-permute-start(bf16[80,3584]{1,0:T(8,128)(2,1)S(1)} %get-tuple-element.47.refs_1_), channel_id=1, source_target_pairs={{0,4},{1,5},{2,6},{3,7},{4,8},{5,9},{6,10},{7,11},{8,12},{9,13},{1... | collective-permute-start | bytes 1720328 | tf_op jit(solution)/shard_map/ppermute | solution.py:36
  18.8 0.9 collective-permute-start.6
  19.6 4.9 %collective-permute-done.4.refs_3_.refs_0_ = bf16[80,3584]{1,0:T(8,128)(2,1)S(1)} collective-permute-done((bf16[80,3584]{1,0:T(8,128)(2,1)}, bf16[80,3584]{1,0:T(8,128)(2,1)S(1)}, u32[]{:S(2)}, u32[]{:S(2)}) %collective-permute-start.4) | collective-permute-done | bytes 573472 | tf_op jit(solution)/shard_map/ppermute | solution.py:36
  24.5 4.2 %load.2 = (bf16[3584,512]{1,0:T(8,128)(2,1)S(1)}, bf16[3584,512]{1,0:T(8,128)(2,1)S(1)}, bf16[512,3584]{1,0:T(8,128)(2,1)S(1)}) custom-call(bf16[3584,512]{1,0:T(8,128)(2,1)} %collective-permute-done.1.refs_0_.refs_2_, bf16[3584,512]{1,0:T(8,128)(2,1)} %collective-permute-done.2.refs_1_.refs_3_, bf16[512,3584]{1,0:T(8,128)(2,1)} %collective-permute-done.3.refs_2_.refs_4_, ...), custom_call_target="tpu_custom_call" | custom-call | tf_op jit(solution)/shard_map/load/pallas_call | solution.py:158
  28.8 0.3 collective-permute-done.refs_1_.refs_3_.refs_9_
  29.1 1.6 %collective-permute-start.9 = (bf16[80,3584]{1,0:T(8,128)(2,1)S(1)}, bf16[80,3584]{1,0:T(8,128)(2,1)S(1)}, u32[]{:S(2)}, u32[]{:S(2)}) collective-permute-start(bf16[80,3584]{1,0:T(8,128)(2,1)S(1)} %after.5.refs_2_), channel_id=1, source_target_pairs={{0,2},{1,3},{2,0},{3,1},{4,6},{5,7},{6,4},{7,5},{8,10},{9,11},{10,... | collective-permute-start | bytes 1720328 | tf_op jit(solution)/shard_map/ppermute | solution.py:36
  30.6 1.4 %route.3 = (bf16[80,3584]{1,0:T(8,128)(2,1)S(1)}, bf16[80,3584]{1,0:T(8,128)(2,1)S(1)}, bf16[80,3584]{1,0:T(8,128)(2,1)S(1)}, bf16[4,80,256]{2,1,0:T(8,128)(2,1)S(1)}) custom-call(s32[2]{0:T(128)S(1)} %copy-done.8, bf16[128,3712]{1,0:T(8,128)(2,1)S(1)} %collective-permute-done.refs_1_.refs_3_.refs_9_, f32[1,3584]{1,0:T(1,128)S(1)} %copy-done.7, ...), custom_call_target="tpu_custom_call" | custom-call | tf_op jit(solution)/shard_map/route/pallas_call | solution.py:126
  32.1 1.6 %collective-permute-start.10 = (bf16[80,3584]{1,0:T(8,128)(2,1)S(1)}, bf16[80,3584]{1,0:T(8,128)(2,1)S(1)}, u32[]{:S(2)}, u32[]{:S(2)}) collective-permute-start(bf16[80,3584]{1,0:T(8,128)(2,1)S(1)} %get-tuple-element.59), channel_id=1, source_target_pairs={{0,4},{1,5},{2,6},{3,7},{4,8},{5,9},{6,10},{7,11},{8,12},{9,13},{1... | collective-permute-start | bytes 1720328 | tf_op jit(solution)/shard_map/ppermute | solution.py:36
  33.7 0.5 collective-permute-start.11
  34.2 2.7 %collective-permute-done.5.refs_3_ = bf16[80,3584]{1,0:T(8,128)(2,1)S(1)} collective-permute-done((bf16[80,3584]{1,0:T(8,128)(2,1)S(1)}, bf16[80,3584]{1,0:T(8,128)(2,1)S(1)}, u32[]{:S(2)}, u32[]{:S(2)}) %collective-permute-start.5) | collective-permute-done | bytes 573472 | tf_op jit(solution)/shard_map/ppermute | solution.py:36
  36.9 7.8 %expert.3 = (bf16[80,3584]{1,0:T(8,128)(2,1)S(1)}, bf16[80,3584]{1,0:T(8,128)(2,1)S(1)}, bf16[80,3584]{1,0:T(8,128)(2,1)S(1)}, bf16[80,3584]{1,0:T(8,128)(2,1)S(1)}) custom-call(s32[2]{0:T(128)S(1)} %copy-done.8, bf16[80,3584]{1,0:T(8,128)(2,1)S(1)} %copy-done.6, bf16[80,3584]{1,0:T(8,128)(2,1)S(1)} %after.5.refs_2_, ...), custom_call_target="tpu_custom_call" | custom-call | tf_op jit(solution)/shard_map/expert/pallas_call | solution.py:223
  44.7 0.6 collective-permute-start.7
  45.3 1.5 %collective-permute-start.8 = (bf16[80,3584]{1,0:T(8,128)(2,1)S(1)}, bf16[80,3584]{1,0:T(8,128)(2,1)S(1)}, u32[]{:S(2)}, u32[]{:S(2)}) collective-permute-start(bf16[80,3584]{1,0:T(8,128)(2,1)S(1)} %get-tuple-element.55), channel_id=1, source_target_pairs={{0,4},{1,5},{2,6},{3,7},{4,8},{5,9},{6,10},{7,11},{8,12},{9,13},{1... | collective-permute-start | bytes 1720328 | tf_op jit(solution)/shard_map/ppermute | solution.py:36
  46.8 4.4 %expert.4 = (bf16[80,3584]{1,0:T(8,128)(2,1)S(1)}, bf16[80,3584]{1,0:T(8,128)(2,1)S(1)}, bf16[80,3584]{1,0:T(8,128)(2,1)S(1)}) custom-call(s32[2]{0:T(128)S(1)} %copy-done.8, bf16[80,3584]{1,0:T(8,128)(2,1)S(1)} %collective-permute-done.9.refs_1_, bf16[80,3584]{1,0:T(8,128)(2,1)S(1)} %get-tuple-element.56.refs_2_, ...), custom_call_target="tpu_custom_call" | custom-call | tf_op jit(solution)/shard_map/expert/pallas_call | solution.py:223
  51.2 0.7 collective-permute-start.14
  52.0 4.4 %expert.5 = (bf16[80,1792]{1,0:T(8,128)(2,1)S(1)}, bf16[80,1792]{1,0:T(8,128)(2,1)S(1)}, bf16[80,1792]{1,0:T(8,128)(2,1)S(1)}, bf16[80,1792]{1,0:T(8,128)(2,1)S(1)}) custom-call(s32[2]{0:T(128)S(1)} %copy-done.8, bf16[80,3584]{1,0:T(8,128)(2,1)S(1)} %collective-permute-done.10.refs_1_, bf16[80,3584]{1,0:T(8,128)(2,1)S(1)} %collective-permute-done.11.refs_2_, ...), custom_call_target="tpu_custom_call" | custom-call | tf_op jit(solution)/shard_map/expert/pallas_call | solution.py:223
  56.4 1.7 %collective-permute-start.12 = (bf16[80,1792]{1,0:T(8,128)(2,1)S(1)}, bf16[80,1792]{1,0:T(8,128)(2,1)S(1)}, u32[]{:S(2)}, u32[]{:S(2)}) collective-permute-start(bf16[80,1792]{1,0:T(8,128)(2,1)S(1)} %get-tuple-element.62), channel_id=1, source_target_pairs={{0,12},{1,13},{2,14},{3,15},{4,0},{5,1},{6,2},{7,3},{8,4},{9,5},{1... | collective-permute-start | bytes 860168 | tf_op jit(solution)/shard_map/ppermute | solution.py:36
  58.0 0.4 collective-permute-start.13
  58.5 3.4 %collective-permute-done.7.refs_1_.refs_2_ = bf16[80,3584]{1,0:T(8,128)(2,1)S(1)} collective-permute-done((bf16[80,3584]{1,0:T(8,128)(2,1)S(1)}, bf16[80,3584]{1,0:T(8,128)(2,1)S(1)}, u32[]{:S(2)}, u32[]{:S(2)}) %collective-permute-start.7) | collective-permute-done | bytes 573472 | tf_op jit(solution)/shard_map/ppermute | solution.py:36
  61.9 0.8 collective-permute-start.18
  62.7 1.2 %collective-permute-start.19 = (bf16[80,1792]{1,0:T(8,128)(2,1)S(1)}, bf16[80,1792]{1,0:T(8,128)(2,1)S(1)}, u32[]{:S(2)}, u32[]{:S(2)}) collective-permute-start(bf16[80,1792]{1,0:T(8,128)(2,1)S(1)} %get-tuple-element.69), channel_id=1, source_target_pairs={{0,4},{1,5},{2,6},{3,7},{4,8},{5,9},{6,10},{7,11},{8,12},{9,13},{1... | collective-permute-start | bytes 860168 | tf_op jit(solution)/shard_map/ppermute | solution.py:36
  63.9 1.2 %collective-permute-done.14.b_ref = bf16[80,3584]{1,0:T(8,128)(2,1)S(1)} collective-permute-done((bf16[80,3584]{1,0:T(8,128)(2,1)S(1)}, bf16[80,3584]{1,0:T(8,128)(2,1)S(1)}, u32[]{:S(2)}, u32[]{:S(2)}) %collective-permute-start.14) | collective-permute-done | bytes 573472 | tf_op jit(solution)/shard_map/ppermute | solution.py:36
  65.2 3.0 %collective-permute-start.15 = (bf16[80,1792]{1,0:T(8,128)(2,1)S(1)}, bf16[80,1792]{1,0:T(8,128)(2,1)S(1)}, u32[]{:S(2)}, u32[]{:S(2)}) collective-permute-start(bf16[80,1792]{1,0:T(8,128)(2,1)S(1)} %get-tuple-element.65), channel_id=1, source_target_pairs={{0,8},{1,9},{2,10},{3,11},{4,12},{5,13},{6,14},{7,15},{8,0},{9,1},... | collective-permute-start | bytes 860168 | tf_op jit(solution)/shard_map/ppermute | solution.py:36
  68.2 1.0 leave.2
  69.2 1.4 %collective-permute-start.16 = (bf16[128,1792]{1,0:T(8,128)(2,1)S(1)}, bf16[128,1792]{1,0:T(8,128)(2,1)S(1)}, u32[]{:S(2)}, u32[]{:S(2)}) collective-permute-start(bf16[128,1792]{1,0:T(8,128)(2,1)S(1)} %leave.2), channel_id=1, source_target_pairs={{0,2},{1,3},{2,0},{3,1},{4,6},{5,7},{6,4},{7,5},{8,10},{9,11},{10,... | collective-permute-start | bytes 1376264 | tf_op jit(solution)/shard_map/ppermute | solution.py:36
  70.6 3.0 %collective-permute-done.18.refs_4_ = bf16[80,1792]{1,0:T(8,128)(2,1)S(1)} collective-permute-done((bf16[80,1792]{1,0:T(8,128)(2,1)S(1)}, bf16[80,1792]{1,0:T(8,128)(2,1)S(1)}, u32[]{:S(2)}, u32[]{:S(2)}) %collective-permute-start.18) | collective-permute-done | bytes 286752 | tf_op jit(solution)/shard_map/ppermute | solution.py:36
  73.7 0.7 collective-permute-done.19.refs_5_
  74.4 1.0 leave.3.refs_0_
  75.4 3.7 %collective-permute-done.15.refs_6_.refs_1_ = bf16[80,1792]{1,0:T(8,128)(2,1)S(1)} collective-permute-done((bf16[80,1792]{1,0:T(8,128)(2,1)S(1)}, bf16[80,1792]{1,0:T(8,128)(2,1)S(1)}, u32[]{:S(2)}, u32[]{:S(2)}) %collective-permute-start.15) | collective-permute-done | bytes 286752 | tf_op jit(solution)/shard_map/ppermute | solution.py:36
  79.1 0.9 collective-permute-start.21
  80.0 4.1 %collective-permute-start.20 = (bf16[80,1792]{1,0:T(8,128)(2,1)S(1)}, bf16[80,1792]{1,0:T(8,128)(2,1)S(1)}, u32[]{:S(2)}, u32[]{:S(2)}) collective-permute-start(bf16[80,1792]{1,0:T(8,128)(2,1)S(1)} %get-tuple-element.70), channel_id=1, source_target_pairs={{0,8},{1,9},{2,10},{3,11},{4,12},{5,13},{6,14},{7,15},{8,0},{9,1},... | collective-permute-start | bytes 860168 | tf_op jit(solution)/shard_map/ppermute | solution.py:36
  84.0 1.2 %stay.2 = bf16[128,1792]{1,0:T(8,128)(2,1)S(1)} custom-call(s32[2]{0:T(128)S(1)} %copy-done.8, bf16[4,80,256]{2,1,0:T(8,128)(2,1)S(1)} %copy-done.3, bf16[4,80,256]{2,1,0:T(8,128)(2,1)S(1)} %get-tuple-element.42.w_across_ref, bf16[80,3584]{1,0:T(8,128)(2,1)S(1)} %get-tuple-element.53.refs_0_, bf16[80,3584]{1,0:T(8,128)(2,1)S(1)} %collective-permute-done.7.refs_1_.refs_2_, ...), custom_call_target="tpu_custom_call" | custom-call | tf_op jit(solution)/shard_map/stay/pallas_call | solution.py:324
  85.3 1.1 collective-permute-start.17
  86.4 2.5 %collective-permute-done.20.refs_6_ = bf16[80,1792]{1,0:T(8,128)(2,1)S(1)} collective-permute-done((bf16[80,1792]{1,0:T(8,128)(2,1)S(1)}, bf16[80,1792]{1,0:T(8,128)(2,1)S(1)}, u32[]{:S(2)}, u32[]{:S(2)}) %collective-permute-start.20) | collective-permute-done | bytes 286752 | tf_op jit(solution)/shard_map/ppermute | solution.py:36
  88.9 2.0 %collective-permute-done.21.refs_7_ = bf16[128,1792]{1,0:T(8,128)(2,1)S(1)} collective-permute-done((bf16[128,1792]{1,0:T(8,128)(2,1)S(1)}, bf16[128,1792]{1,0:T(8,128)(2,1)S(1)}, u32[]{:S(2)}, u32[]{:S(2)}) %collective-permute-start.21) | collective-permute-done | bytes 458784 | tf_op jit(solution)/shard_map/ppermute | solution.py:36
  90.9 1.2 %stay.3 = bf16[128,1792]{1,0:T(8,128)(2,1)S(1)} custom-call(s32[2]{0:T(128)S(1)} %copy-done.8, bf16[4,80,256]{2,1,0:T(8,128)(2,1)S(1)} %copy-done.3, bf16[4,80,256]{2,1,0:T(8,128)(2,1)S(1)} %get-tuple-element.42.w_across_ref, bf16[80,3584]{1,0:T(8,128)(2,1)S(1)} %get-tuple-element.53.refs_0_, bf16[80,3584]{1,0:T(8,128)(2,1)S(1)} %collective-permute-done.7.refs_1_.refs_2_, ...), custom_call_target="tpu_custom_call" | custom-call | tf_op jit(solution)/shard_map/stay/pallas_call | solution.py:324
  92.1 2.0 %collective-permute-start.22 = (bf16[128,1792]{1,0:T(8,128)(2,1)S(1)}, bf16[128,1792]{1,0:T(8,128)(2,1)S(1)}, u32[]{:S(2)}, u32[]{:S(2)}) collective-permute-start(bf16[128,1792]{1,0:T(8,128)(2,1)S(1)} %stay.3), channel_id=1, source_target_pairs={{0,16},{1,17},{2,18},{3,19},{4,20},{5,21},{6,22},{7,23},{8,24},{9,... | collective-permute-start | bytes 1376264 | tf_op jit(solution)/shard_map/ppermute | solution.py:45
  94.1 8.0 %collective-permute-done.17 = bf16[128,1792]{1,0:T(8,128)(2,1)S(1)} collective-permute-done((bf16[128,1792]{1,0:T(8,128)(2,1)S(1)}, bf16[128,1792]{1,0:T(8,128)(2,1)S(1)}, u32[]{:S(2)}, u32[]{:S(2)}) %collective-permute-start.17) | collective-permute-done | bytes 458784 | tf_op jit(solution)/shard_map/ppermute | solution.py:45
  102.1 8.1 %collective-permute-done.22 = bf16[128,1792]{1,0:T(8,128)(2,1)S(1)} collective-permute-done((bf16[128,1792]{1,0:T(8,128)(2,1)S(1)}, bf16[128,1792]{1,0:T(8,128)(2,1)S(1)}, u32[]{:S(2)}, u32[]{:S(2)}) %collective-permute-start.22) | collective-permute-done | bytes 458784 | tf_op jit(solution)/shard_map/ppermute | solution.py:45
  110.2 1.0 maximum_bitcast_fusion
  (34 shorter events, 0.2 us)
Async XLA Ops:
  0.0 16.5 %collective-permute-start.1 = (bf16[3584,512]{1,0:T(8,128)(2,1)}, bf16[3584,512]{1,0:T(8,128)(2,1)}, u32[]{:S(2)}, u32[]{:S(2)}) collective-permute-start(bf16[3584,512]{1,0:T(8,128)(2,1)} %bitcast.14), channel_id=1, source_target_pairs={{0,1},{1,0},{2,3},{3,2},{4,5},{5,4},{6,7},{7,6},{8,9},{9,8},{10,11... | collective-permute-start | bytes 11010056 | tf_op jit(solution)/shard_map/ppermute | solution.py:36
  0.0 16.5 %collective-permute-start.2 = (bf16[3584,512]{1,0:T(8,128)(2,1)}, bf16[3584,512]{1,0:T(8,128)(2,1)}, u32[]{:S(2)}, u32[]{:S(2)}) collective-permute-start(bf16[3584,512]{1,0:T(8,128)(2,1)} %bitcast.16), channel_id=1, source_target_pairs={{0,1},{1,0},{2,3},{3,2},{4,5},{5,4},{6,7},{7,6},{8,9},{9,8},{10,11... | collective-permute-start | bytes 11010056 | tf_op jit(solution)/shard_map/ppermute | solution.py:36
  0.5 16.7 %collective-permute-start.3 = (bf16[512,3584]{1,0:T(8,128)(2,1)}, bf16[512,3584]{1,0:T(8,128)(2,1)}, u32[]{:S(2)}, u32[]{:S(2)}) collective-permute-start(bf16[512,3584]{1,0:T(8,128)(2,1)} %bitcast.18), channel_id=1, source_target_pairs={{0,1},{1,0},{2,3},{3,2},{4,5},{5,4},{6,7},{7,6},{8,9},{9,8},{10,11... | collective-permute-start | bytes 11010056 | tf_op jit(solution)/shard_map/ppermute | solution.py:36
  5.3 23.8 %collective-permute-start = (bf16[128,3712]{1,0:T(8,128)(2,1)}, bf16[128,3712]{1,0:T(8,128)(2,1)S(1)}, u32[]{:S(2)}, u32[]{:S(2)}) collective-permute-start(bf16[128,3712]{1,0:T(8,128)(2,1)} %get-tuple-element.39.refs_3_.refs_8_), channel_id=1, source_target_pairs={{0,2},{1,3},{2,0},{3,1},{4,6},{5,7},{6,4},{7,5},{8,10},{9,11},{10,... | collective-permute-start | bytes 2850824 | tf_op jit(solution)/shard_map/ppermute | solution.py:36
  7.0 17.6 %collective-permute-start.4 = (bf16[80,3584]{1,0:T(8,128)(2,1)}, bf16[80,3584]{1,0:T(8,128)(2,1)S(1)}, u32[]{:S(2)}, u32[]{:S(2)}) collective-permute-start(bf16[80,3584]{1,0:T(8,128)(2,1)} %get-tuple-element.40), channel_id=1, source_target_pairs={{0,8},{1,9},{2,10},{3,11},{4,12},{5,13},{6,14},{7,15},{8,0},{9,1},... | collective-permute-start | bytes 1720328 | tf_op jit(solution)/shard_map/ppermute | solution.py:36
  9.1 1.2 %copy-start.1 = (bf16[128,3712]{1,0:T(8,128)(2,1)S(1)}, bf16[128,3712]{1,0:T(8,128)(2,1)}, u32[]{:S(2)}) copy-start(bf16[128,3712]{1,0:T(8,128)(2,1)} %get-tuple-element.39.refs_3_.refs_8_) | copy-start | bytes 2850820
  10.3 7.0 %copy-start.4 = (bf16[80,3584]{1,0:T(8,128)(2,1)S(1)}, bf16[80,3584]{1,0:T(8,128)(2,1)}, u32[]{:S(2)}) copy-start(bf16[80,3584]{1,0:T(8,128)(2,1)} %get-tuple-element.44.refs_0_) | copy-start | bytes 1720324
  10.3 7.0 %copy-start.5 = (bf16[80,3584]{1,0:T(8,128)(2,1)S(1)}, bf16[80,3584]{1,0:T(8,128)(2,1)}, u32[]{:S(2)}) copy-start(bf16[80,3584]{1,0:T(8,128)(2,1)} %get-tuple-element.45.refs_1_) | copy-start | bytes 1720324
  17.3 19.6 %collective-permute-start.5 = (bf16[80,3584]{1,0:T(8,128)(2,1)S(1)}, bf16[80,3584]{1,0:T(8,128)(2,1)S(1)}, u32[]{:S(2)}, u32[]{:S(2)}) collective-permute-start(bf16[80,3584]{1,0:T(8,128)(2,1)S(1)} %get-tuple-element.47.refs_1_), channel_id=1, source_target_pairs={{0,4},{1,5},{2,6},{3,7},{4,8},{5,9},{6,10},{7,11},{8,12},{9,13},{1... | collective-permute-start | bytes 1720328 | tf_op jit(solution)/shard_map/ppermute | solution.py:36
  18.7 11.9 %copy-start.7 = (f32[1,3584]{1,0:T(1,128)S(1)}, f32[1,3584]{1,0:T(1,128)}, u32[]{:S(2)}) copy-start(f32[1,3584]{1,0:T(1,128)} %refs_2_.3) | copy-start | bytes 43012
  18.8 11.9 %copy-start.8 = (s32[2]{0:T(128)S(1)}, s32[2]{0:T(128)}, u32[]{:S(2)}) copy-start(s32[2]{0:T(128)} %pad_add_fusion.refs_0_.flags_ref) | copy-start | bytes 28
  18.8 18.1 %collective-permute-start.6 = (bf16[80,3584]{1,0:T(8,128)(2,1)S(1)}, bf16[80,3584]{1,0:T(8,128)(2,1)S(1)}, u32[]{:S(2)}, u32[]{:S(2)}) collective-permute-start(bf16[80,3584]{1,0:T(8,128)(2,1)S(1)} %get-tuple-element.48.refs_2_), channel_id=1, source_target_pairs={{0,12},{1,13},{2,14},{3,15},{4,0},{5,1},{6,2},{7,3},{8,4},{9,5},{1... | collective-permute-start | bytes 1720328 | tf_op jit(solution)/shard_map/ppermute | solution.py:36
  28.8 8.1 %copy-start = (bf16[512,3584]{1,0:T(8,128)(2,1)S(1)}, bf16[512,3584]{1,0:T(8,128)(2,1)}, u32[]{:S(2)}) copy-start(bf16[512,3584]{1,0:T(8,128)(2,1)} %get-tuple-element.50.refs_7_.refs_5_) | copy-start | bytes 11010052
  28.8 8.1 %copy-start.6 = (bf16[80,3584]{1,0:T(8,128)(2,1)S(1)}, bf16[80,3584]{1,0:T(8,128)(2,1)}, u32[]{:S(2)}) copy-start(bf16[80,3584]{1,0:T(8,128)(2,1)} %get-tuple-element.43.refs_1_) | copy-start | bytes 1720324
  29.1 17.7 %collective-permute-start.9 = (bf16[80,3584]{1,0:T(8,128)(2,1)S(1)}, bf16[80,3584]{1,0:T(8,128)(2,1)S(1)}, u32[]{:S(2)}, u32[]{:S(2)}) collective-permute-start(bf16[80,3584]{1,0:T(8,128)(2,1)S(1)} %after.5.refs_2_), channel_id=1, source_target_pairs={{0,2},{1,3},{2,0},{3,1},{4,6},{5,7},{6,4},{7,5},{8,10},{9,11},{10,... | collective-permute-start | bytes 1720328 | tf_op jit(solution)/shard_map/ppermute | solution.py:36
  32.1 19.9 %collective-permute-start.10 = (bf16[80,3584]{1,0:T(8,128)(2,1)S(1)}, bf16[80,3584]{1,0:T(8,128)(2,1)S(1)}, u32[]{:S(2)}, u32[]{:S(2)}) collective-permute-start(bf16[80,3584]{1,0:T(8,128)(2,1)S(1)} %get-tuple-element.59), channel_id=1, source_target_pairs={{0,4},{1,5},{2,6},{3,7},{4,8},{5,9},{6,10},{7,11},{8,12},{9,13},{1... | collective-permute-start | bytes 1720328 | tf_op jit(solution)/shard_map/ppermute | solution.py:36
  33.7 18.3 %collective-permute-start.11 = (bf16[80,3584]{1,0:T(8,128)(2,1)S(1)}, bf16[80,3584]{1,0:T(8,128)(2,1)S(1)}, u32[]{:S(2)}, u32[]{:S(2)}) collective-permute-start(bf16[80,3584]{1,0:T(8,128)(2,1)S(1)} %get-tuple-element.60), channel_id=1, source_target_pairs={{0,12},{1,13},{2,14},{3,15},{4,0},{5,1},{6,2},{7,3},{8,4},{9,5},{1... | collective-permute-start | bytes 1720328 | tf_op jit(solution)/shard_map/ppermute | solution.py:36
  44.7 17.2 %collective-permute-start.7 = (bf16[80,3584]{1,0:T(8,128)(2,1)S(1)}, bf16[80,3584]{1,0:T(8,128)(2,1)S(1)}, u32[]{:S(2)}, u32[]{:S(2)}) collective-permute-start(bf16[80,3584]{1,0:T(8,128)(2,1)S(1)} %get-tuple-element.54), channel_id=1, source_target_pairs={{0,12},{1,13},{2,14},{3,15},{4,0},{5,1},{6,2},{7,3},{8,4},{9,5},{1... | collective-permute-start | bytes 1720328 | tf_op jit(solution)/shard_map/ppermute | solution.py:36
  45.3 16.6 %collective-permute-start.8 = (bf16[80,3584]{1,0:T(8,128)(2,1)S(1)}, bf16[80,3584]{1,0:T(8,128)(2,1)S(1)}, u32[]{:S(2)}, u32[]{:S(2)}) collective-permute-start(bf16[80,3584]{1,0:T(8,128)(2,1)S(1)} %get-tuple-element.55), channel_id=1, source_target_pairs={{0,4},{1,5},{2,6},{3,7},{4,8},{5,9},{6,10},{7,11},{8,12},{9,13},{1... | collective-permute-start | bytes 1720328 | tf_op jit(solution)/shard_map/ppermute | solution.py:36
  51.2 17.0 %copy-start.3 = (bf16[4,80,256]{2,1,0:T(8,128)(2,1)S(1)}, bf16[4,80,256]{2,1,0:T(8,128)(2,1)}, u32[]{:S(2)}) copy-start(bf16[4,80,256]{2,1,0:T(8,128)(2,1)} %get-tuple-element.38.w_own_ref) | copy-start | bytes 491524
  51.2 13.9 %collective-permute-start.14 = (bf16[80,3584]{1,0:T(8,128)(2,1)S(1)}, bf16[80,3584]{1,0:T(8,128)(2,1)S(1)}, u32[]{:S(2)}, u32[]{:S(2)}) collective-permute-start(bf16[80,3584]{1,0:T(8,128)(2,1)S(1)} %get-tuple-element.61.refs_9_), channel_id=1, source_target_pairs={{0,2},{1,3},{2,0},{3,1},{4,6},{5,7},{6,4},{7,5},{8,10},{9,11},{10,... | collective-permute-start | bytes 1720328 | tf_op jit(solution)/shard_map/ppermute | solution.py:36
  56.4 11.8 %collective-permute-start.12 = (bf16[80,1792]{1,0:T(8,128)(2,1)S(1)}, bf16[80,1792]{1,0:T(8,128)(2,1)S(1)}, u32[]{:S(2)}, u32[]{:S(2)}) collective-permute-start(bf16[80,1792]{1,0:T(8,128)(2,1)S(1)} %get-tuple-element.62), channel_id=1, source_target_pairs={{0,12},{1,13},{2,14},{3,15},{4,0},{5,1},{6,2},{7,3},{8,4},{9,5},{1... | collective-permute-start | bytes 860168 | tf_op jit(solution)/shard_map/ppermute | solution.py:36
  58.0 10.2 %collective-permute-start.13 = (bf16[80,1792]{1,0:T(8,128)(2,1)S(1)}, bf16[80,1792]{1,0:T(8,128)(2,1)S(1)}, u32[]{:S(2)}, u32[]{:S(2)}) collective-permute-start(bf16[80,1792]{1,0:T(8,128)(2,1)S(1)} %get-tuple-element.63), channel_id=1, source_target_pairs={{0,4},{1,5},{2,6},{3,7},{4,8},{5,9},{6,10},{7,11},{8,12},{9,13},{1... | collective-permute-start | bytes 860168 | tf_op jit(solution)/shard_map/ppermute | solution.py:36
  61.9 11.8 %collective-permute-start.18 = (bf16[80,1792]{1,0:T(8,128)(2,1)S(1)}, bf16[80,1792]{1,0:T(8,128)(2,1)S(1)}, u32[]{:S(2)}, u32[]{:S(2)}) collective-permute-start(bf16[80,1792]{1,0:T(8,128)(2,1)S(1)} %get-tuple-element.68), channel_id=1, source_target_pairs={{0,12},{1,13},{2,14},{3,15},{4,0},{5,1},{6,2},{7,3},{8,4},{9,5},{1... | collective-permute-start | bytes 860168 | tf_op jit(solution)/shard_map/ppermute | solution.py:36
  62.7 11.7 %collective-permute-start.19 = (bf16[80,1792]{1,0:T(8,128)(2,1)S(1)}, bf16[80,1792]{1,0:T(8,128)(2,1)S(1)}, u32[]{:S(2)}, u32[]{:S(2)}) collective-permute-start(bf16[80,1792]{1,0:T(8,128)(2,1)S(1)} %get-tuple-element.69), channel_id=1, source_target_pairs={{0,4},{1,5},{2,6},{3,7},{4,8},{5,9},{6,10},{7,11},{8,12},{9,13},{1... | collective-permute-start | bytes 860168 | tf_op jit(solution)/shard_map/ppermute | solution.py:36
  65.2 13.9 %collective-permute-start.15 = (bf16[80,1792]{1,0:T(8,128)(2,1)S(1)}, bf16[80,1792]{1,0:T(8,128)(2,1)S(1)}, u32[]{:S(2)}, u32[]{:S(2)}) collective-permute-start(bf16[80,1792]{1,0:T(8,128)(2,1)S(1)} %get-tuple-element.65), channel_id=1, source_target_pairs={{0,8},{1,9},{2,10},{3,11},{4,12},{5,13},{6,14},{7,15},{8,0},{9,1},... | collective-permute-start | bytes 860168 | tf_op jit(solution)/shard_map/ppermute | solution.py:36
  68.2 15.8 %copy-start.2 = (bf16[128,3712]{1,0:T(8,128)(2,1)S(1)}, bf16[128,3712]{1,0:T(8,128)(2,1)}, u32[]{:S(2)}) copy-start(bf16[128,3712]{1,0:T(8,128)(2,1)} %get-tuple-element.39.refs_3_.refs_8_) | copy-start | bytes 2850820
  69.2 14.8 %collective-permute-start.16 = (bf16[128,1792]{1,0:T(8,128)(2,1)S(1)}, bf16[128,1792]{1,0:T(8,128)(2,1)S(1)}, u32[]{:S(2)}, u32[]{:S(2)}) collective-permute-start(bf16[128,1792]{1,0:T(8,128)(2,1)S(1)} %leave.2), channel_id=1, source_target_pairs={{0,2},{1,3},{2,0},{3,1},{4,6},{5,7},{6,4},{7,5},{8,10},{9,11},{10,... | collective-permute-start | bytes 1376264 | tf_op jit(solution)/shard_map/ppermute | solution.py:36
  79.1 11.8 %collective-permute-start.21 = (bf16[128,1792]{1,0:T(8,128)(2,1)S(1)}, bf16[128,1792]{1,0:T(8,128)(2,1)S(1)}, u32[]{:S(2)}, u32[]{:S(2)}) collective-permute-start(bf16[128,1792]{1,0:T(8,128)(2,1)S(1)} %after.7), channel_id=1, source_target_pairs={{0,2},{1,3},{2,0},{3,1},{4,6},{5,7},{6,4},{7,5},{8,10},{9,11},{10,... | collective-permute-start | bytes 1376264 | tf_op jit(solution)/shard_map/ppermute | solution.py:36
  80.0 8.9 %collective-permute-start.20 = (bf16[80,1792]{1,0:T(8,128)(2,1)S(1)}, bf16[80,1792]{1,0:T(8,128)(2,1)S(1)}, u32[]{:S(2)}, u32[]{:S(2)}) collective-permute-start(bf16[80,1792]{1,0:T(8,128)(2,1)S(1)} %get-tuple-element.70), channel_id=1, source_target_pairs={{0,8},{1,9},{2,10},{3,11},{4,12},{5,13},{6,14},{7,15},{8,0},{9,1},... | collective-permute-start | bytes 860168 | tf_op jit(solution)/shard_map/ppermute | solution.py:36
  85.3 16.9 %collective-permute-start.17 = (bf16[128,1792]{1,0:T(8,128)(2,1)S(1)}, bf16[128,1792]{1,0:T(8,128)(2,1)S(1)}, u32[]{:S(2)}, u32[]{:S(2)}) collective-permute-start(bf16[128,1792]{1,0:T(8,128)(2,1)S(1)} %stay.2), channel_id=1, source_target_pairs={{0,16},{1,17},{2,18},{3,19},{4,20},{5,21},{6,22},{7,23},{8,24},{9,... | collective-permute-start | bytes 1376264 | tf_op jit(solution)/shard_map/ppermute | solution.py:45
  92.1 18.1 %collective-permute-start.22 = (bf16[128,1792]{1,0:T(8,128)(2,1)S(1)}, bf16[128,1792]{1,0:T(8,128)(2,1)S(1)}, u32[]{:S(2)}, u32[]{:S(2)}) collective-permute-start(bf16[128,1792]{1,0:T(8,128)(2,1)S(1)} %stay.3), channel_id=1, source_target_pairs={{0,16},{1,17},{2,18},{3,19},{4,20},{5,21},{6,22},{7,23},{8,24},{9,... | collective-permute-start | bytes 1376264 | tf_op jit(solution)/shard_map/ppermute | solution.py:45

commit v4 on v3

--- a/solution.py
+++ b/solution.py
@@ -19,13 +19,20 @@
 F32 = jnp.float32
 BF16 = jnp.bfloat16
 VMEM = pl.BlockSpec(memory_space=pltpu.VMEM)
-SMEM = pl.BlockSpec(memory_space=pltpu.SMEM)
 ANY = pl.BlockSpec(memory_space=pl.ANY)
 HBM = pl.BlockSpec(memory_space=pltpu.HBM)
 
 
 def limit(mebibytes):
     return pltpu.CompilerParams(vmem_limit_bytes=mebibytes << 20)
+
+
+def column():
+    return lax.axis_index("expert") // 4
+
+
+def swapped():
+    return lax.axis_index("section") % LAYERS == LAYERS - 1
 
 
 def moved(value, dx, dy, dc):
@@ -45,7 +52,7 @@
     return lax.ppermute(value, ("section", "expert"), pairs)
 
 
-def first_route_kernel(flags_ref, *refs):
+def first_route_kernel(*refs):
     far, refs = refs[:4], refs[4:]
     *refs, sent_ref, gain_ref, ids_ref, gv_ref, sems = refs
     count, dim = far[0].shape
@@ -62,24 +69,24 @@
     packed = jnp.concatenate([ids.astype(F32), high, middle, low], axis=0)
     packed = jnp.concatenate([packed, jnp.zeros((PACK - 8, count), F32)], axis=0)
     sent_ref[:, dim:] = packed.T.astype(BF16)
-    route_kernel((0, 1, 2, 3), flags_ref, sent_ref, gain_ref, ids, gv, *refs)
-
-
-def second_route_kernel(flags_ref, sent_ref, gain_ref, *refs):
+    route_kernel((0, 1, 2, 3), sent_ref, gain_ref, ids, gv, *refs)
+
+
+def second_route_kernel(sent_ref, gain_ref, *refs):
     packed = sent_ref[:, gain_ref.shape[1] :].astype(F32).T
     ids = packed[0:2].astype(jnp.int32)
     gv = packed[2:4] + packed[4:6] + packed[6:8]
-    route_kernel((0, 1, 3), flags_ref, sent_ref, gain_ref, ids, gv, *refs)
-
-
-def route_kernel(kinds, flags_ref, tok_ref, gain_ref, ids, gv, *refs):
+    route_kernel((0, 1, 3), sent_ref, gain_ref, ids, gv, *refs)
+
+
+def route_kernel(kinds, tok_ref, gain_ref, ids, gv, *refs):
     w_ref = refs[-1]
     out_refs = dict(zip(kinds, refs[-1 - len(kinds) : -1]))
     wide = tok_ref[:, : gain_ref.shape[1]].astype(F32)
     scale = lax.rsqrt(jnp.mean(wide * wide, axis=-1, keepdims=True) + 1e-06)
     normed = (wide * scale * gain_ref[...]).astype(BF16)
     count = normed.shape[0]
-    ids = jnp.bitwise_and(ids + (EXPERTS - flags_ref[0]), EXPERTS - 1)
+    ids = jnp.bitwise_and(ids + (EXPERTS - column()), EXPERTS - 1)
     first, second = ids[0:1, :], ids[1:2, :]
     kind = lax.broadcasted_iota(jnp.int32, (16, count), 0)
     chosen = (kind == first) | (kind == second)
@@ -106,7 +113,7 @@
         w_ref[d] = jnp.concatenate([high, low], axis=1)
 
 
-def route(first_set, flags, tok, gain, choices, others):
+def route(first_set, tok, gain, choices, others):
     count, dim = tok.shape[0], gain.shape[1]
     blocks = 4 if first_set else 3
     out_shape = [jax.ShapeDtypeStruct((CAP, dim), BF16)] * blocks
@@ -118,7 +125,7 @@
         scratch = [pltpu.VMEM(v.shape, v.dtype) for v in (gain, *choices)]
         scratch.append(pltpu.SemaphoreType.DMA((4,)))
     operands = (tok, gain, *choices)
-    inner = 1 + len(operands)
+    inner = len(operands)
 
     def body(*refs):
         kernel(*refs[:inner], *refs[inner + len(others) :])
@@ -126,13 +133,13 @@
     return pl.pallas_call(
         body,
         out_shape=out_shape,
-        in_specs=[SMEM] + [HBM if first_set else VMEM] * len(operands) + [ANY] * len(others),
+        in_specs=[HBM if first_set else VMEM] * len(operands) + [ANY] * len(others),
         out_specs=[VMEM] * len(out_shape),
         scratch_shapes=scratch,
         cost_estimate=FREE,
         compiler_params=limit(58 if first_set else 12),
         name="route",
-    )(flags, *operands, *others)
+    )(*operands, *others)
 
 
 def hidden_tile(rows_ref, gate_ref, up_ref, hidden_ref, at, to):
@@ -167,7 +174,7 @@
     )(*weights, *others)
 
 
-def expert_kernel(splits, far, flags_ref, *refs):
+def expert_kernel(splits, far, *refs):
     blocks = len(splits)
     rows_in, weights, refs = refs[:blocks], refs[blocks : blocks + 6], refs[blocks + 6 :]
     far_refs, refs = refs[:far], refs[far:]
@@ -195,20 +202,20 @@
     if far:
         far_ref, cross_ref, kept_ref = far_refs[0], outs[0], outs[-1]
 
-        @pl.when(flags_ref[1] == 0)
+        @pl.when(jnp.logical_not(swapped()))
         def _():
             kept_ref[...] = far_ref[...]
 
-        @pl.when(flags_ref[1] != 0)
+        @pl.when(swapped())
         def _():
             kept_ref[...] = cross_ref[...]
             cross_ref[...] = far_ref[...]
 
 
-def expert(flags, rows, weights, splits, far=(), others=()):
+def expert(rows, weights, splits, far=(), others=()):
     blocks, dim = len(rows), rows[0].shape[1]
     units = weights[0].shape[1]
-    inner = 1 + blocks + 6 + len(far)
+    inner = blocks + 6 + len(far)
     out_shape = [
         jax.ShapeDtypeStruct((CAP, width), BF16) for split in splits for width in split
     ] + [jax.ShapeDtypeStruct((CAP, dim), BF16)] * len(far)
@@ -223,15 +230,14 @@
     outs = pl.pallas_call(
         body,
         out_shape=out_shape,
-        in_specs=[SMEM]
-        + [VMEM] * (blocks + 6 + len(far))
+        in_specs=[VMEM] * inner
         + [ANY] * len(others),
         out_specs=[VMEM] * len(out_shape),
         scratch_shapes=scratch,
         cost_estimate=FREE,
         compiler_params=limit(10),
         name="expert",
-    )(flags, *rows, *weights, *far, *others)
+    )(*rows, *weights, *far, *others)
     grouped, first = [], 0
     for split in splits:
         group = outs[first : first + len(split)]
@@ -288,19 +294,19 @@
     return both[:count] + both[count:]
 
 
-def leave_kernel(columns, flags_ref, w_own_ref, w_across_ref, *refs):
+def leave_kernel(columns, w_own_ref, w_across_ref, *refs):
     own_refs, across_refs, out_ref = refs[:3], refs[3:6], refs[6]
 
-    @pl.when(flags_ref[1] == 0)
+    @pl.when(jnp.logical_not(swapped()))
     def _():
         out_ref[...] = weighted(w_across_ref, (0, 1, 3), across_refs, columns).astype(BF16)
 
-    @pl.when(flags_ref[1] != 0)
+    @pl.when(swapped())
     def _():
         out_ref[...] = weighted(w_own_ref, (0, 1, 3), own_refs, columns).astype(BF16)
 
 
-def stay_kernel(columns, flags_ref, w_own_ref, w_across_ref, *refs):
+def stay_kernel(columns, w_own_ref, w_across_ref, *refs):
     own_refs, across_refs = refs[:3], refs[3:6]
     far_ref, mine_ref, tok_ref, tok_across_ref, out_ref = refs[6:]
 
@@ -309,42 +315,39 @@
         total += mine_ref[...].astype(F32) + home_ref[:, columns].astype(F32)
         out_ref[...] = total.astype(BF16)
 
-    @pl.when(flags_ref[1] == 0)
+    @pl.when(jnp.logical_not(swapped()))
     def _():
         finish(w_own_ref, own_refs, tok_ref)
 
-    @pl.when(flags_ref[1] != 0)
+    @pl.when(swapped())
     def _():
         finish(w_across_ref, across_refs, tok_across_ref)
 
 
-def mix(chunk, kernel, name, flags, w_own, w_across, blocks):
+def mix(chunk, kernel, name, w_own, w_across, blocks):
     count, width = w_own.shape[2] // 2, PARTS[chunk]
     begin = sum(PARTS[:chunk])
     return pl.pallas_call(
         functools.partial(kernel, slice(begin, begin + width)),
         out_shape=jax.ShapeDtypeStruct((count, width), BF16),
-        in_specs=[SMEM] + [VMEM] * (2 + len(blocks)),
+        in_specs=[VMEM] * (2 + len(blocks)),
         out_specs=VMEM,
         cost_estimate=FREE,
         compiler_params=limit(8),
         name=name,
-    )(flags, w_own, w_across, *blocks)
+    )(w_own, w_across, *blocks)
 
 
 def on_device(tokens, norm_gain, expert_ids, gate_values, gate_weight, up_weight, down_weight):
     tok = tokens[0]
     dim = tok.shape[1]
-    column = lax.axis_index("expert") // 4
-    swapped = lax.axis_index("section") % LAYERS == LAYERS - 1
-    flags = jnp.stack([column.astype(jnp.int32), swapped.astype(jnp.int32)])
     ids = expert_ids[0].T
     gv = gate_values[0].T
     gates = (gate_weight[0], moved(gate_weight[0], 0, 0, 1))
     ups = (up_weight[0], moved(up_weight[0], 0, 0, 1))
     downs = (down_weight[0], moved(down_weight[0], 0, 0, 1))
 
-    *own, w_own, sent = route(True, flags, tok, norm_gain, (ids, gv), ())
+    *own, w_own, sent = route(True, tok, norm_gain, (ids, gv), ())
     tok_across = moved(sent, 0, 1, 0)
     own_far = moved(own[2], 2, 0, 0)
     held = load((gates[0], ups[0], downs[0]), (sent,), LOAD)
@@ -356,17 +359,17 @@
     across_far = moved(own_far, 0, 1, 0)
     kept = (*held, *held_more)
     whole, split = (dim,), PARTS
-    *across, w_across = route(False, flags, tok_across, norm_gain, (), (kept[3],))
+    *across, w_across = route(False, tok_across, norm_gain, (), (kept[3],))
     (own_out, far_out, right_out, left_out), _ = expert(
-        flags, (own[0], own_far, own_right, own_left), kept, (whole,) * 4
+        (own[0], own_far, own_right, own_left), kept, (whole,) * 4
     )
     across_right = moved(across[1], 1, 0, 0)
     across_left = moved(across[2], -1, 0, 0)
     (far_cross, across_out), (far_kept,) = expert(
-        flags, (across_far, across[0]), kept, (whole,) * 2, (far_out,)
+        (across_far, across[0]), kept, (whole,) * 2, (far_out,)
     )
     (right_late, left_late), _ = expert(
-        flags, (across_right, across_left), kept, (split,) * 2, others=(far_cross,)
+        (across_right, across_left), kept, (split,) * 2, others=(far_cross,)
     )
     my_right = moved(right_out, -1, 0, 0)
     my_left = moved(left_out, 1, 0, 0)
@@ -380,7 +383,7 @@
         own_back = (own_out, my_right, my_left)
         across_back = (across_out, moved(right_rows, -1, 0, 0), moved(left_rows, 1, 0, 0))
         far_back = moved(sums[k], 2, 0, 0)
-        leaving = mix(k, leave_kernel, "leave", flags, w_own, w_across, (*own_back, *across_back))
+        leaving = mix(k, leave_kernel, "leave", w_own, w_across, (*own_back, *across_back))
         if k > 0:
             (leaving,) = after((leaving,), (arrived,))
         mine, arrived = moved(leaving, 0, 1, 0), far_back
@@ -388,7 +391,6 @@
             k,
             stay_kernel,
             "stay",
-            flags,
             w_own,
             w_across,
             (*own_back, *across_back, far_back, mine, sent, tok_across),

time: 111 us -> 110 us (level)
  Pallas kernels: 37.3 us -> 32.1 us
  waiting for transfers between devices: 41.3 us -> 46.1 us
    ppermute x21, waiting for transfers between devices: 25.2 us -> 29 us  [moved(): return lax.ppermute(value, 'expert', pairs)]
    pallas_call x5, Pallas kernels: 22.3 us -> 19.3 us  [the longest x3 14.9 us: expert(): pl.pallas_call(body, out_shape=out_shape, in_specs=[VMEM] * inner + [ANY]...]
    pallas_call x4, Pallas kernels: 4.46 us -> 2.26 us  [mix(): pl.pallas_call(functools.partial(kernel, slice(begin, begin + width)), ou...]
  transfers between devices with their start and end apart: 23 -> 23, of which waited for: 13 -> 14; matrix products, arithmetic and copies ran while one was open for 1% -> 0% of each run, Pallas kernels for 34% -> 29%
where the time goes in v4:
time: 110 us
  waiting for transfers between devices  46.1 us (42%)
  Pallas kernels  32.1 us (29%)
  starting transfers between devices  29.3 us (27%)
  local copies, waits for them, and re-layouts  1.22 us (1%)
    ppermute x21, waiting for transfers between devices, moved(): return lax.ppermute(value, 'expert', pairs)  29 us
    ppermute x21, starting transfers between devices, moved(): return lax.ppermute(value, 'expert', pairs)  25.9 us
    ppermute x2, waiting for transfers between devices, handed_on(): return lax.ppermute(value, ('section', 'expert'), pairs)  17.1 us
    pallas_call x3, Pallas kernels, expert(): pl.pallas_call(body, out_shape=out_shape, in_specs=[VMEM] * inner + [ANY]...  14.9 us
    pallas_call x2, Pallas kernels, load(): pl.pallas_call(functools.partial(load_kernel, count), out_shape=[jax.Shap...  10.4 us
    pallas_call x2, Pallas kernels, route(): pl.pallas_call(body, out_shape=out_shape, in_specs=[HBM if first_set else...  4.44 us
    ppermute x2, starting transfers between devices, handed_on(): return lax.ppermute(value, ('section', 'expert'), pairs)  3.36 us
    pallas_call x4, Pallas kernels, mix(): pl.pallas_call(functools.partial(kernel, slice(begin, begin + width)), ou...  2.26 us
  transfers between devices with their start and end apart: 23, of which 14 were waited for; matrix products, arithmetic and copies ran while one was open for 0% of the time, Pallas kernels for 29%

profile of v4, /device:TPU:2, one launch (start us, length us, event | category | flops | bytes accessed | tf_op | source)
XLA Modules:
  0.0 109.8 jit_solution(6658462207993949610)
XLA Ops:
  0.0 0.5 collective-permute-start.2
  0.5 3.5 %route.2 = (bf16[80,3584]{1,0:T(8,128)(2,1)}, bf16[80,3584]{1,0:T(8,128)(2,1)}, bf16[80,3584]{1,0:T(8,128)(2,1)}, bf16[80,3584]{1,0:T(8,128)(2,1)}, bf16[4,80,25...) custom-call(bf16[128,3584]{1,0:T(8,128)(2,1)} %bitcast.18, f32[1,3584]{1,0:T(1,128)} %refs_1_.3, s32[2,128]{1,0:T(2,128)} %bitcast.19, ...), custom_call_target="tpu_custom_call" | custom-call | tf_op jit(solution)/shard_map/route/pallas_call | solution.py:133
  4.1 1.7 %collective-permute-start = (bf16[128,3712]{1,0:T(8,128)(2,1)}, bf16[128,3712]{1,0:T(8,128)(2,1)S(1)}, u32[]{:S(2)}, u32[]{:S(2)}) collective-permute-start(bf16[128,3712]{1,0:T(8,128)(2,1)} %get-tuple-element.39.refs_3_.refs_8_), channel_id=1, source_target_pairs={{0,2},{1,3},{2,0},{3,1},{4,6},{5,7},{6,4},{7,5},{8,10},{9,11},{10,... | collective-permute-start | bytes 2850824 | tf_op jit(solution)/shard_map/ppermute | solution.py:43
  5.7 2.1 %collective-permute-start.4 = (bf16[80,3584]{1,0:T(8,128)(2,1)}, bf16[80,3584]{1,0:T(8,128)(2,1)S(1)}, u32[]{:S(2)}, u32[]{:S(2)}) collective-permute-start(bf16[80,3584]{1,0:T(8,128)(2,1)} %get-tuple-element.40), channel_id=1, source_target_pairs={{0,8},{1,9},{2,10},{3,11},{4,12},{5,13},{6,14},{7,15},{8,0},{9,1},... | collective-permute-start | bytes 1720328 | tf_op jit(solution)/shard_map/ppermute | solution.py:43
  7.8 1.2 %copy-done.1 = bf16[128,3712]{1,0:T(8,128)(2,1)S(1)} copy-done((bf16[128,3712]{1,0:T(8,128)(2,1)S(1)}, bf16[128,3712]{1,0:T(8,128)(2,1)}, u32[]{:S(2)}) %copy-start.1) | copy-done | bytes 950296
  9.0 6.2 %load.3 = (bf16[3584,512]{1,0:T(8,128)(2,1)S(1)}, bf16[3584,512]{1,0:T(8,128)(2,1)S(1)}, bf16[512,3584]{1,0:T(8,128)(2,1)}) custom-call(bf16[3584,512]{1,0:T(8,128)(2,1)} %bitcast.13, bf16[3584,512]{1,0:T(8,128)(2,1)} %bitcast.15, bf16[512,3584]{1,0:T(8,128)(2,1)} %bitcast.17, bf16[128,3712]{1,0:T(8,128)(2,1)S(1)} %copy-done.1), custom_call_target="tpu_custom_call" | custom-call | tf_op jit(solution)/shard_map/load/pallas_call | solution.py:165
  15.3 2.0 %collective-permute-done.3.refs_2_.refs_4_ = bf16[512,3584]{1,0:T(8,128)(2,1)} collective-permute-done((bf16[512,3584]{1,0:T(8,128)(2,1)}, bf16[512,3584]{1,0:T(8,128)(2,1)}, u32[]{:S(2)}, u32[]{:S(2)}) %collective-permute-start.3) | collective-permute-done | bytes 3670048 | tf_op jit(solution)/shard_map/ppermute | solution.py:43
  17.3 1.5 %collective-permute-start.5 = (bf16[80,3584]{1,0:T(8,128)(2,1)S(1)}, bf16[80,3584]{1,0:T(8,128)(2,1)S(1)}, u32[]{:S(2)}, u32[]{:S(2)}) collective-permute-start(bf16[80,3584]{1,0:T(8,128)(2,1)S(1)} %get-tuple-element.47.refs_1_), channel_id=1, source_target_pairs={{0,4},{1,5},{2,6},{3,7},{4,8},{5,9},{6,10},{7,11},{8,12},{9,13},{1... | collective-permute-start | bytes 1720328 | tf_op jit(solution)/shard_map/ppermute | solution.py:43
  18.8 0.9 collective-permute-start.6
  19.6 3.1 %collective-permute-done.4.refs_3_.refs_0_ = bf16[80,3584]{1,0:T(8,128)(2,1)S(1)} collective-permute-done((bf16[80,3584]{1,0:T(8,128)(2,1)}, bf16[80,3584]{1,0:T(8,128)(2,1)S(1)}, u32[]{:S(2)}, u32[]{:S(2)}) %collective-permute-start.4) | collective-permute-done | bytes 573472 | tf_op jit(solution)/shard_map/ppermute | solution.py:43
  22.7 4.2 %load.2 = (bf16[3584,512]{1,0:T(8,128)(2,1)S(1)}, bf16[3584,512]{1,0:T(8,128)(2,1)S(1)}, bf16[512,3584]{1,0:T(8,128)(2,1)S(1)}) custom-call(bf16[3584,512]{1,0:T(8,128)(2,1)} %collective-permute-done.1.refs_0_.refs_2_, bf16[3584,512]{1,0:T(8,128)(2,1)} %collective-permute-done.2.refs_1_.refs_3_, bf16[512,3584]{1,0:T(8,128)(2,1)} %collective-permute-done.3.refs_2_.refs_4_, ...), custom_call_target="tpu_custom_call" | custom-call | tf_op jit(solution)/shard_map/load/pallas_call | solution.py:165
  27.0 0.8 collective-permute-done.refs_0_.refs_3_.refs_9_
  27.8 1.6 %collective-permute-start.9 = (bf16[80,3584]{1,0:T(8,128)(2,1)S(1)}, bf16[80,3584]{1,0:T(8,128)(2,1)S(1)}, u32[]{:S(2)}, u32[]{:S(2)}) collective-permute-start(bf16[80,3584]{1,0:T(8,128)(2,1)S(1)} %after.5.refs_1_), channel_id=1, source_target_pairs={{0,2},{1,3},{2,0},{3,1},{4,6},{5,7},{6,4},{7,5},{8,10},{9,11},{10,... | collective-permute-start | bytes 1720328 | tf_op jit(solution)/shard_map/ppermute | solution.py:43
  29.4 0.9 route.3
  30.3 1.6 %collective-permute-start.10 = (bf16[80,3584]{1,0:T(8,128)(2,1)S(1)}, bf16[80,3584]{1,0:T(8,128)(2,1)S(1)}, u32[]{:S(2)}, u32[]{:S(2)}) collective-permute-start(bf16[80,3584]{1,0:T(8,128)(2,1)S(1)} %get-tuple-element.59), channel_id=1, source_target_pairs={{0,4},{1,5},{2,6},{3,7},{4,8},{5,9},{6,10},{7,11},{8,12},{9,13},{1... | collective-permute-start | bytes 1720328 | tf_op jit(solution)/shard_map/ppermute | solution.py:43
  31.9 0.5 collective-permute-start.11
  32.4 3.2 %collective-permute-done.5.refs_2_ = bf16[80,3584]{1,0:T(8,128)(2,1)S(1)} collective-permute-done((bf16[80,3584]{1,0:T(8,128)(2,1)S(1)}, bf16[80,3584]{1,0:T(8,128)(2,1)S(1)}, u32[]{:S(2)}, u32[]{:S(2)}) %collective-permute-start.5) | collective-permute-done | bytes 573472 | tf_op jit(solution)/shard_map/ppermute | solution.py:43
  35.6 7.3 %expert.3 = (bf16[80,3584]{1,0:T(8,128)(2,1)S(1)}, bf16[80,3584]{1,0:T(8,128)(2,1)S(1)}, bf16[80,3584]{1,0:T(8,128)(2,1)S(1)}, bf16[80,3584]{1,0:T(8,128)(2,1)S(1)}) custom-call(bf16[80,3584]{1,0:T(8,128)(2,1)S(1)} %copy-done.6, bf16[80,3584]{1,0:T(8,128)(2,1)S(1)} %after.5.refs_1_, bf16[80,3584]{1,0:T(8,128)(2,1)S(1)} %collective-permute-done.5.refs_2_, ...), custom_call_target="tpu_custom_call" | custom-call | tf_op jit(solution)/shard_map/expert/pallas_call | solution.py:230
  42.9 1.0 collective-permute-start.7
  43.9 1.1 collective-permute-start.8
  45.0 3.8 %expert.4 = (bf16[80,3584]{1,0:T(8,128)(2,1)S(1)}, bf16[80,3584]{1,0:T(8,128)(2,1)S(1)}, bf16[80,3584]{1,0:T(8,128)(2,1)S(1)}) custom-call(bf16[80,3584]{1,0:T(8,128)(2,1)S(1)} %collective-permute-done.9.refs_0_, bf16[80,3584]{1,0:T(8,128)(2,1)S(1)} %get-tuple-element.56.refs_1_, bf16[3584,512]{1,0:T(8,128)(2,1)S(1)} %get-tuple-element.46.refs_5_.refs_4_.refs_2_, ...), custom_call_target="tpu_custom_call" | custom-call | tf_op jit(solution)/shard_map/expert/pallas_call | solution.py:230
  48.8 0.9 collective-permute-start.14
  49.7 3.8 %expert.5 = (bf16[80,1792]{1,0:T(8,128)(2,1)S(1)}, bf16[80,1792]{1,0:T(8,128)(2,1)S(1)}, bf16[80,1792]{1,0:T(8,128)(2,1)S(1)}, bf16[80,1792]{1,0:T(8,128)(2,1)S(1)}) custom-call(bf16[80,3584]{1,0:T(8,128)(2,1)S(1)} %collective-permute-done.10.refs_0_, bf16[80,3584]{1,0:T(8,128)(2,1)S(1)} %collective-permute-done.11.refs_1_, ...), custom_call_target="tpu_custom_call" | custom-call | tf_op jit(solution)/shard_map/expert/pallas_call | solution.py:230
  53.5 1.6 %collective-permute-start.12 = (bf16[80,1792]{1,0:T(8,128)(2,1)S(1)}, bf16[80,1792]{1,0:T(8,128)(2,1)S(1)}, u32[]{:S(2)}, u32[]{:S(2)}) collective-permute-start(bf16[80,1792]{1,0:T(8,128)(2,1)S(1)} %get-tuple-element.62), channel_id=1, source_target_pairs={{0,12},{1,13},{2,14},{3,15},{4,0},{5,1},{6,2},{7,3},{8,4},{9,5},{1... | collective-permute-start | bytes 860168 | tf_op jit(solution)/shard_map/ppermute | solution.py:43
  55.1 0.5 collective-permute-start.13
  55.6 4.5 %collective-permute-done.7.refs_1_.refs_2_ = bf16[80,3584]{1,0:T(8,128)(2,1)S(1)} collective-permute-done((bf16[80,3584]{1,0:T(8,128)(2,1)S(1)}, bf16[80,3584]{1,0:T(8,128)(2,1)S(1)}, u32[]{:S(2)}, u32[]{:S(2)}) %collective-permute-start.7) | collective-permute-done | bytes 573472 | tf_op jit(solution)/shard_map/ppermute | solution.py:43
  60.1 0.8 collective-permute-done.8.refs_2_.refs_3_
  60.9 1.5 %collective-permute-start.18 = (bf16[80,1792]{1,0:T(8,128)(2,1)S(1)}, bf16[80,1792]{1,0:T(8,128)(2,1)S(1)}, u32[]{:S(2)}, u32[]{:S(2)}) collective-permute-start(bf16[80,1792]{1,0:T(8,128)(2,1)S(1)} %get-tuple-element.68), channel_id=1, source_target_pairs={{0,12},{1,13},{2,14},{3,15},{4,0},{5,1},{6,2},{7,3},{8,4},{9,5},{1... | collective-permute-start | bytes 860168 | tf_op jit(solution)/shard_map/ppermute | solution.py:43
  62.5 0.5 collective-permute-start.19
  63.1 3.5 %collective-permute-start.15 = (bf16[80,1792]{1,0:T(8,128)(2,1)S(1)}, bf16[80,1792]{1,0:T(8,128)(2,1)S(1)}, u32[]{:S(2)}, u32[]{:S(2)}) collective-permute-start(bf16[80,1792]{1,0:T(8,128)(2,1)S(1)} %get-tuple-element.65), channel_id=1, source_target_pairs={{0,8},{1,9},{2,10},{3,11},{4,12},{5,13},{6,14},{7,15},{8,0},{9,1},... | collective-permute-start | bytes 860168 | tf_op jit(solution)/shard_map/ppermute | solution.py:43
  66.6 0.5 collective-permute-done.13.refs_5_
  67.1 0.4 leave.2
  67.5 1.1 collective-permute-start.16
  68.6 4.4 %collective-permute-done.18.refs_4_ = bf16[80,1792]{1,0:T(8,128)(2,1)S(1)} collective-permute-done((bf16[80,1792]{1,0:T(8,128)(2,1)S(1)}, bf16[80,1792]{1,0:T(8,128)(2,1)S(1)}, u32[]{:S(2)}, u32[]{:S(2)}) %collective-permute-start.18) | collective-permute-done | bytes 286752 | tf_op jit(solution)/shard_map/ppermute | solution.py:43
  73.0 0.2 collective-permute-done.19.refs_5_
  73.2 0.4 leave.3.refs_0_
  73.7 4.2 %collective-permute-done.15.refs_6_.refs_1_ = bf16[80,1792]{1,0:T(8,128)(2,1)S(1)} collective-permute-done((bf16[80,1792]{1,0:T(8,128)(2,1)S(1)}, bf16[80,1792]{1,0:T(8,128)(2,1)S(1)}, u32[]{:S(2)}, u32[]{:S(2)}) %collective-permute-start.15) | collective-permute-done | bytes 286752 | tf_op jit(solution)/shard_map/ppermute | solution.py:43
  77.8 0.9 collective-permute-start.21
  78.7 3.0 %collective-permute-start.20 = (bf16[80,1792]{1,0:T(8,128)(2,1)S(1)}, bf16[80,1792]{1,0:T(8,128)(2,1)S(1)}, u32[]{:S(2)}, u32[]{:S(2)}) collective-permute-start(bf16[80,1792]{1,0:T(8,128)(2,1)S(1)} %get-tuple-element.70), channel_id=1, source_target_pairs={{0,8},{1,9},{2,10},{3,11},{4,12},{5,13},{6,14},{7,15},{8,0},{9,1},... | collective-permute-start | bytes 860168 | tf_op jit(solution)/shard_map/ppermute | solution.py:43
  81.7 0.7 stay.2
  82.4 1.4 %collective-permute-start.17 = (bf16[128,1792]{1,0:T(8,128)(2,1)S(1)}, bf16[128,1792]{1,0:T(8,128)(2,1)S(1)}, u32[]{:S(2)}, u32[]{:S(2)}) collective-permute-start(bf16[128,1792]{1,0:T(8,128)(2,1)S(1)} %stay.2), channel_id=1, source_target_pairs={{0,16},{1,17},{2,18},{3,19},{4,20},{5,21},{6,22},{7,23},{8,24},{9,... | collective-permute-start | bytes 1376264 | tf_op jit(solution)/shard_map/ppermute | solution.py:52
  83.8 3.9 %collective-permute-done.20.refs_6_ = bf16[80,1792]{1,0:T(8,128)(2,1)S(1)} collective-permute-done((bf16[80,1792]{1,0:T(8,128)(2,1)S(1)}, bf16[80,1792]{1,0:T(8,128)(2,1)S(1)}, u32[]{:S(2)}, u32[]{:S(2)}) %collective-permute-start.20) | collective-permute-done | bytes 286752 | tf_op jit(solution)/shard_map/ppermute | solution.py:43
  87.7 1.4 %collective-permute-done.21.refs_7_ = bf16[128,1792]{1,0:T(8,128)(2,1)S(1)} collective-permute-done((bf16[128,1792]{1,0:T(8,128)(2,1)S(1)}, bf16[128,1792]{1,0:T(8,128)(2,1)S(1)}, u32[]{:S(2)}, u32[]{:S(2)}) %collective-permute-start.21) | collective-permute-done | bytes 458784 | tf_op jit(solution)/shard_map/ppermute | solution.py:43
  89.1 0.7 stay.3
  89.8 2.0 %collective-permute-start.22 = (bf16[128,1792]{1,0:T(8,128)(2,1)S(1)}, bf16[128,1792]{1,0:T(8,128)(2,1)S(1)}, u32[]{:S(2)}, u32[]{:S(2)}) collective-permute-start(bf16[128,1792]{1,0:T(8,128)(2,1)S(1)} %stay.3), channel_id=1, source_target_pairs={{0,16},{1,17},{2,18},{3,19},{4,20},{5,21},{6,22},{7,23},{8,24},{9,... | collective-permute-start | bytes 1376264 | tf_op jit(solution)/shard_map/ppermute | solution.py:52
  91.8 9.2 %collective-permute-done.17 = bf16[128,1792]{1,0:T(8,128)(2,1)S(1)} collective-permute-done((bf16[128,1792]{1,0:T(8,128)(2,1)S(1)}, bf16[128,1792]{1,0:T(8,128)(2,1)S(1)}, u32[]{:S(2)}, u32[]{:S(2)}) %collective-permute-start.17) | collective-permute-done | bytes 458784 | tf_op jit(solution)/shard_map/ppermute | solution.py:52
  100.9 7.9 %collective-permute-done.22 = bf16[128,1792]{1,0:T(8,128)(2,1)S(1)} collective-permute-done((bf16[128,1792]{1,0:T(8,128)(2,1)S(1)}, bf16[128,1792]{1,0:T(8,128)(2,1)S(1)}, u32[]{:S(2)}, u32[]{:S(2)}) %collective-permute-start.22) | collective-permute-done | bytes 458784 | tf_op jit(solution)/shard_map/ppermute | solution.py:52
  108.9 1.0 maximum_bitcast_fusion
  (31 shorter events, 0.2 us)
Async XLA Ops:
  0.0 15.3 %collective-permute-start.1 = (bf16[3584,512]{1,0:T(8,128)(2,1)}, bf16[3584,512]{1,0:T(8,128)(2,1)}, u32[]{:S(2)}, u32[]{:S(2)}) collective-permute-start(bf16[3584,512]{1,0:T(8,128)(2,1)} %bitcast.12), channel_id=1, source_target_pairs={{0,1},{1,0},{2,3},{3,2},{4,5},{5,4},{6,7},{7,6},{8,9},{9,8},{10,11... | collective-permute-start | bytes 11010056 | tf_op jit(solution)/shard_map/ppermute | solution.py:43
  0.0 15.3 %collective-permute-start.2 = (bf16[3584,512]{1,0:T(8,128)(2,1)}, bf16[3584,512]{1,0:T(8,128)(2,1)}, u32[]{:S(2)}, u32[]{:S(2)}) collective-permute-start(bf16[3584,512]{1,0:T(8,128)(2,1)} %bitcast.14), channel_id=1, source_target_pairs={{0,1},{1,0},{2,3},{3,2},{4,5},{5,4},{6,7},{7,6},{8,9},{9,8},{10,11... | collective-permute-start | bytes 11010056 | tf_op jit(solution)/shard_map/ppermute | solution.py:43
  0.5 16.7 %collective-permute-start.3 = (bf16[512,3584]{1,0:T(8,128)(2,1)}, bf16[512,3584]{1,0:T(8,128)(2,1)}, u32[]{:S(2)}, u32[]{:S(2)}) collective-permute-start(bf16[512,3584]{1,0:T(8,128)(2,1)} %bitcast.16), channel_id=1, source_target_pairs={{0,1},{1,0},{2,3},{3,2},{4,5},{5,4},{6,7},{7,6},{8,9},{9,8},{10,11... | collective-permute-start | bytes 11010056 | tf_op jit(solution)/shard_map/ppermute | solution.py:43
  4.1 23.8 %collective-permute-start = (bf16[128,3712]{1,0:T(8,128)(2,1)}, bf16[128,3712]{1,0:T(8,128)(2,1)S(1)}, u32[]{:S(2)}, u32[]{:S(2)}) collective-permute-start(bf16[128,3712]{1,0:T(8,128)(2,1)} %get-tuple-element.39.refs_3_.refs_8_), channel_id=1, source_target_pairs={{0,2},{1,3},{2,0},{3,1},{4,6},{5,7},{6,4},{7,5},{8,10},{9,11},{10,... | collective-permute-start | bytes 2850824 | tf_op jit(solution)/shard_map/ppermute | solution.py:43
  5.7 17.0 %collective-permute-start.4 = (bf16[80,3584]{1,0:T(8,128)(2,1)}, bf16[80,3584]{1,0:T(8,128)(2,1)S(1)}, u32[]{:S(2)}, u32[]{:S(2)}) collective-permute-start(bf16[80,3584]{1,0:T(8,128)(2,1)} %get-tuple-element.40), channel_id=1, source_target_pairs={{0,8},{1,9},{2,10},{3,11},{4,12},{5,13},{6,14},{7,15},{8,0},{9,1},... | collective-permute-start | bytes 1720328 | tf_op jit(solution)/shard_map/ppermute | solution.py:43
  7.8 1.2 %copy-start.1 = (bf16[128,3712]{1,0:T(8,128)(2,1)S(1)}, bf16[128,3712]{1,0:T(8,128)(2,1)}, u32[]{:S(2)}) copy-start(bf16[128,3712]{1,0:T(8,128)(2,1)} %get-tuple-element.39.refs_3_.refs_8_) | copy-start | bytes 2850820
  9.0 8.2 %copy-start.4 = (bf16[80,3584]{1,0:T(8,128)(2,1)S(1)}, bf16[80,3584]{1,0:T(8,128)(2,1)}, u32[]{:S(2)}) copy-start(bf16[80,3584]{1,0:T(8,128)(2,1)} %get-tuple-element.44.refs_0_) | copy-start | bytes 1720324
  9.0 8.2 %copy-start.5 = (bf16[80,3584]{1,0:T(8,128)(2,1)S(1)}, bf16[80,3584]{1,0:T(8,128)(2,1)}, u32[]{:S(2)}) copy-start(bf16[80,3584]{1,0:T(8,128)(2,1)} %get-tuple-element.45.refs_1_) | copy-start | bytes 1720324
  17.3 18.4 %collective-permute-start.5 = (bf16[80,3584]{1,0:T(8,128)(2,1)S(1)}, bf16[80,3584]{1,0:T(8,128)(2,1)S(1)}, u32[]{:S(2)}, u32[]{:S(2)}) collective-permute-start(bf16[80,3584]{1,0:T(8,128)(2,1)S(1)} %get-tuple-element.47.refs_1_), channel_id=1, source_target_pairs={{0,4},{1,5},{2,6},{3,7},{4,8},{5,9},{6,10},{7,11},{8,12},{9,13},{1... | collective-permute-start | bytes 1720328 | tf_op jit(solution)/shard_map/ppermute | solution.py:43
  18.7 10.7 %copy-start.7 = (f32[1,3584]{1,0:T(1,128)S(1)}, f32[1,3584]{1,0:T(1,128)}, u32[]{:S(2)}) copy-start(f32[1,3584]{1,0:T(1,128)} %refs_1_.3) | copy-start | bytes 43012
  18.8 16.9 %collective-permute-start.6 = (bf16[80,3584]{1,0:T(8,128)(2,1)S(1)}, bf16[80,3584]{1,0:T(8,128)(2,1)S(1)}, u32[]{:S(2)}, u32[]{:S(2)}) collective-permute-start(bf16[80,3584]{1,0:T(8,128)(2,1)S(1)} %get-tuple-element.48.refs_2_), channel_id=1, source_target_pairs={{0,12},{1,13},{2,14},{3,15},{4,0},{5,1},{6,2},{7,3},{8,4},{9,5},{1... | collective-permute-start | bytes 1720328 | tf_op jit(solution)/shard_map/ppermute | solution.py:43
  27.0 8.7 %copy-start = (bf16[512,3584]{1,0:T(8,128)(2,1)S(1)}, bf16[512,3584]{1,0:T(8,128)(2,1)}, u32[]{:S(2)}) copy-start(bf16[512,3584]{1,0:T(8,128)(2,1)} %get-tuple-element.50.refs_6_.refs_4_) | copy-start | bytes 11010052
  27.0 8.7 %copy-start.6 = (bf16[80,3584]{1,0:T(8,128)(2,1)S(1)}, bf16[80,3584]{1,0:T(8,128)(2,1)}, u32[]{:S(2)}) copy-start(bf16[80,3584]{1,0:T(8,128)(2,1)} %get-tuple-element.43.refs_0_) | copy-start | bytes 1720324
  27.8 17.2 %collective-permute-start.9 = (bf16[80,3584]{1,0:T(8,128)(2,1)S(1)}, bf16[80,3584]{1,0:T(8,128)(2,1)S(1)}, u32[]{:S(2)}, u32[]{:S(2)}) collective-permute-start(bf16[80,3584]{1,0:T(8,128)(2,1)S(1)} %after.5.refs_1_), channel_id=1, source_target_pairs={{0,2},{1,3},{2,0},{3,1},{4,6},{5,7},{6,4},{7,5},{8,10},{9,11},{10,... | collective-permute-start | bytes 1720328 | tf_op jit(solution)/shard_map/ppermute | solution.py:43
  30.3 19.4 %collective-permute-start.10 = (bf16[80,3584]{1,0:T(8,128)(2,1)S(1)}, bf16[80,3584]{1,0:T(8,128)(2,1)S(1)}, u32[]{:S(2)}, u32[]{:S(2)}) collective-permute-start(bf16[80,3584]{1,0:T(8,128)(2,1)S(1)} %get-tuple-element.59), channel_id=1, source_target_pairs={{0,4},{1,5},{2,6},{3,7},{4,8},{5,9},{6,10},{7,11},{8,12},{9,13},{1... | collective-permute-start | bytes 1720328 | tf_op jit(solution)/shard_map/ppermute | solution.py:43
  31.9 17.8 %collective-permute-start.11 = (bf16[80,3584]{1,0:T(8,128)(2,1)S(1)}, bf16[80,3584]{1,0:T(8,128)(2,1)S(1)}, u32[]{:S(2)}, u32[]{:S(2)}) collective-permute-start(bf16[80,3584]{1,0:T(8,128)(2,1)S(1)} %get-tuple-element.60), channel_id=1, source_target_pairs={{0,12},{1,13},{2,14},{3,15},{4,0},{5,1},{6,2},{7,3},{8,4},{9,5},{1... | collective-permute-start | bytes 1720328 | tf_op jit(solution)/shard_map/ppermute | solution.py:43
  42.9 17.2 %collective-permute-start.7 = (bf16[80,3584]{1,0:T(8,128)(2,1)S(1)}, bf16[80,3584]{1,0:T(8,128)(2,1)S(1)}, u32[]{:S(2)}, u32[]{:S(2)}) collective-permute-start(bf16[80,3584]{1,0:T(8,128)(2,1)S(1)} %get-tuple-element.54), channel_id=1, source_target_pairs={{0,12},{1,13},{2,14},{3,15},{4,0},{5,1},{6,2},{7,3},{8,4},{9,5},{1... | collective-permute-start | bytes 1720328 | tf_op jit(solution)/shard_map/ppermute | solution.py:43
  43.9 17.0 %collective-permute-start.8 = (bf16[80,3584]{1,0:T(8,128)(2,1)S(1)}, bf16[80,3584]{1,0:T(8,128)(2,1)S(1)}, u32[]{:S(2)}, u32[]{:S(2)}) collective-permute-start(bf16[80,3584]{1,0:T(8,128)(2,1)S(1)} %get-tuple-element.55), channel_id=1, source_target_pairs={{0,4},{1,5},{2,6},{3,7},{4,8},{5,9},{6,10},{7,11},{8,12},{9,13},{1... | collective-permute-start | bytes 1720328 | tf_op jit(solution)/shard_map/ppermute | solution.py:43
  48.8 18.3 %copy-start.3 = (bf16[4,80,256]{2,1,0:T(8,128)(2,1)S(1)}, bf16[4,80,256]{2,1,0:T(8,128)(2,1)}, u32[]{:S(2)}) copy-start(bf16[4,80,256]{2,1,0:T(8,128)(2,1)} %get-tuple-element.38.w_own_ref) | copy-start | bytes 491524
  48.8 14.1 %collective-permute-start.14 = (bf16[80,3584]{1,0:T(8,128)(2,1)S(1)}, bf16[80,3584]{1,0:T(8,128)(2,1)S(1)}, u32[]{:S(2)}, u32[]{:S(2)}) collective-permute-start(bf16[80,3584]{1,0:T(8,128)(2,1)S(1)} %get-tuple-element.61.refs_8_), channel_id=1, source_target_pairs={{0,2},{1,3},{2,0},{3,1},{4,6},{5,7},{6,4},{7,5},{8,10},{9,11},{10,... | collective-permute-start | bytes 1720328 | tf_op jit(solution)/shard_map/ppermute | solution.py:43
  53.5 13.1 %collective-permute-start.12 = (bf16[80,1792]{1,0:T(8,128)(2,1)S(1)}, bf16[80,1792]{1,0:T(8,128)(2,1)S(1)}, u32[]{:S(2)}, u32[]{:S(2)}) collective-permute-start(bf16[80,1792]{1,0:T(8,128)(2,1)S(1)} %get-tuple-element.62), channel_id=1, source_target_pairs={{0,12},{1,13},{2,14},{3,15},{4,0},{5,1},{6,2},{7,3},{8,4},{9,5},{1... | collective-permute-start | bytes 860168 | tf_op jit(solution)/shard_map/ppermute | solution.py:43
  55.1 12.0 %collective-permute-start.13 = (bf16[80,1792]{1,0:T(8,128)(2,1)S(1)}, bf16[80,1792]{1,0:T(8,128)(2,1)S(1)}, u32[]{:S(2)}, u32[]{:S(2)}) collective-permute-start(bf16[80,1792]{1,0:T(8,128)(2,1)S(1)} %get-tuple-element.63), channel_id=1, source_target_pairs={{0,4},{1,5},{2,6},{3,7},{4,8},{5,9},{6,10},{7,11},{8,12},{9,13},{1... | collective-permute-start | bytes 860168 | tf_op jit(solution)/shard_map/ppermute | solution.py:43
  60.9 12.1 %collective-permute-start.18 = (bf16[80,1792]{1,0:T(8,128)(2,1)S(1)}, bf16[80,1792]{1,0:T(8,128)(2,1)S(1)}, u32[]{:S(2)}, u32[]{:S(2)}) collective-permute-start(bf16[80,1792]{1,0:T(8,128)(2,1)S(1)} %get-tuple-element.68), channel_id=1, source_target_pairs={{0,12},{1,13},{2,14},{3,15},{4,0},{5,1},{6,2},{7,3},{8,4},{9,5},{1... | collective-permute-start | bytes 860168 | tf_op jit(solution)/shard_map/ppermute | solution.py:43
  62.5 10.8 %collective-permute-start.19 = (bf16[80,1792]{1,0:T(8,128)(2,1)S(1)}, bf16[80,1792]{1,0:T(8,128)(2,1)S(1)}, u32[]{:S(2)}, u32[]{:S(2)}) collective-permute-start(bf16[80,1792]{1,0:T(8,128)(2,1)S(1)} %get-tuple-element.69), channel_id=1, source_target_pairs={{0,4},{1,5},{2,6},{3,7},{4,8},{5,9},{6,10},{7,11},{8,12},{9,13},{1... | collective-permute-start | bytes 860168 | tf_op jit(solution)/shard_map/ppermute | solution.py:43
  63.1 14.7 %collective-permute-start.15 = (bf16[80,1792]{1,0:T(8,128)(2,1)S(1)}, bf16[80,1792]{1,0:T(8,128)(2,1)S(1)}, u32[]{:S(2)}, u32[]{:S(2)}) collective-permute-start(bf16[80,1792]{1,0:T(8,128)(2,1)S(1)} %get-tuple-element.65), channel_id=1, source_target_pairs={{0,8},{1,9},{2,10},{3,11},{4,12},{5,13},{6,14},{7,15},{8,0},{9,1},... | collective-permute-start | bytes 860168 | tf_op jit(solution)/shard_map/ppermute | solution.py:43
  67.1 14.6 %copy-start.2 = (bf16[128,3712]{1,0:T(8,128)(2,1)S(1)}, bf16[128,3712]{1,0:T(8,128)(2,1)}, u32[]{:S(2)}) copy-start(bf16[128,3712]{1,0:T(8,128)(2,1)} %get-tuple-element.39.refs_3_.refs_8_) | copy-start | bytes 2850820
  67.5 14.2 %collective-permute-start.16 = (bf16[128,1792]{1,0:T(8,128)(2,1)S(1)}, bf16[128,1792]{1,0:T(8,128)(2,1)S(1)}, u32[]{:S(2)}, u32[]{:S(2)}) collective-permute-start(bf16[128,1792]{1,0:T(8,128)(2,1)S(1)} %leave.2), channel_id=1, source_target_pairs={{0,2},{1,3},{2,0},{3,1},{4,6},{5,7},{6,4},{7,5},{8,10},{9,11},{10,... | collective-permute-start | bytes 1376264 | tf_op jit(solution)/shard_map/ppermute | solution.py:43
  77.8 11.2 %collective-permute-start.21 = (bf16[128,1792]{1,0:T(8,128)(2,1)S(1)}, bf16[128,1792]{1,0:T(8,128)(2,1)S(1)}, u32[]{:S(2)}, u32[]{:S(2)}) collective-permute-start(bf16[128,1792]{1,0:T(8,128)(2,1)S(1)} %after.7), channel_id=1, source_target_pairs={{0,2},{1,3},{2,0},{3,1},{4,6},{5,7},{6,4},{7,5},{8,10},{9,11},{10,... | collective-permute-start | bytes 1376264 | tf_op jit(solution)/shard_map/ppermute | solution.py:43
  78.7 9.0 %collective-permute-start.20 = (bf16[80,1792]{1,0:T(8,128)(2,1)S(1)}, bf16[80,1792]{1,0:T(8,128)(2,1)S(1)}, u32[]{:S(2)}, u32[]{:S(2)}) collective-permute-start(bf16[80,1792]{1,0:T(8,128)(2,1)S(1)} %get-tuple-element.70), channel_id=1, source_target_pairs={{0,8},{1,9},{2,10},{3,11},{4,12},{5,13},{6,14},{7,15},{8,0},{9,1},... | collective-permute-start | bytes 860168 | tf_op jit(solution)/shard_map/ppermute | solution.py:43
  82.4 18.5 %collective-permute-start.17 = (bf16[128,1792]{1,0:T(8,128)(2,1)S(1)}, bf16[128,1792]{1,0:T(8,128)(2,1)S(1)}, u32[]{:S(2)}, u32[]{:S(2)}) collective-permute-start(bf16[128,1792]{1,0:T(8,128)(2,1)S(1)} %stay.2), channel_id=1, source_target_pairs={{0,16},{1,17},{2,18},{3,19},{4,20},{5,21},{6,22},{7,23},{8,24},{9,... | collective-permute-start | bytes 1376264 | tf_op jit(solution)/shard_map/ppermute | solution.py:52
  89.8 19.1 %collective-permute-start.22 = (bf16[128,1792]{1,0:T(8,128)(2,1)S(1)}, bf16[128,1792]{1,0:T(8,128)(2,1)S(1)}, u32[]{:S(2)}, u32[]{:S(2)}) collective-permute-start(bf16[128,1792]{1,0:T(8,128)(2,1)S(1)} %stay.3), channel_id=1, source_target_pairs={{0,16},{1,17},{2,18},{3,19},{4,20},{5,21},{6,22},{7,23},{8,24},{9,... | collective-permute-start | bytes 1376264 | tf_op jit(solution)/shard_map/ppermute | solution.py:52

commit v5 on v4

--- a/solution.py
+++ b/solution.py
@@ -382,10 +382,11 @@
             right_rows, left_rows = after((right_rows, left_rows), (my_right, my_left))
         own_back = (own_out, my_right, my_left)
         across_back = (across_out, moved(right_rows, -1, 0, 0), moved(left_rows, 1, 0, 0))
-        far_back = moved(sums[k], 2, 0, 0)
+        far_rows = sums[k]
+        if k > 0:
+            (far_rows,) = after((far_rows,), (arrived,))
+        far_back = moved(far_rows, 2, 0, 0)
         leaving = mix(k, leave_kernel, "leave", w_own, w_across, (*own_back, *across_back))
-        if k > 0:
-            (leaving,) = after((leaving,), (arrived,))
         mine, arrived = moved(leaving, 0, 1, 0), far_back
         layer_out = mix(
             k,

time: 110 us -> 109 us (level)
  waiting for transfers between devices: 46.1 us -> 44.2 us
    ppermute x21, waiting for transfers between devices: 29 us -> 26.6 us  [moved(): return lax.ppermute(value, 'expert', pairs)]
where the time goes in v5:
time: 109 us
  waiting for transfers between devices  44.2 us (41%)
  Pallas kernels  32.1 us (29%)
  starting transfers between devices  30.4 us (28%)
  local copies, waits for them, and re-layouts  1.22 us (1%)
    ppermute x21, starting transfers between devices, moved(): return lax.ppermute(value, 'expert', pairs)  27 us
    ppermute x21, waiting for transfers between devices, moved(): return lax.ppermute(value, 'expert', pairs)  26.6 us
    ppermute x2, waiting for transfers between devices, handed_on(): return lax.ppermute(value, ('section', 'expert'), pairs)  17.5 us
    pallas_call x3, Pallas kernels, expert(): pl.pallas_call(body, out_shape=out_shape, in_specs=[VMEM] * inner + [ANY]...  14.9 us
    pallas_call x2, Pallas kernels, load(): pl.pallas_call(functools.partial(load_kernel, count), out_shape=[jax.Shap...  10.4 us
    pallas_call x2, Pallas kernels, route(): pl.pallas_call(body, out_shape=out_shape, in_specs=[HBM if first_set else...  4.44 us
    ppermute x2, starting transfers between devices, handed_on(): return lax.ppermute(value, ('section', 'expert'), pairs)  3.38 us
    pallas_call x4, Pallas kernels, mix(): pl.pallas_call(functools.partial(kernel, slice(begin, begin + width)), ou...  2.26 us
  transfers between devices with their start and end apart: 23, of which 14 were waited for; matrix products, arithmetic and copies ran while one was open for 0% of the time, Pallas kernels for 29%

profile of v5, /device:TPU:2, one launch (start us, length us, event | category | flops | bytes accessed | tf_op | source)
XLA Modules:
  0.0 109.1 jit_solution(151562728924429510)
XLA Ops:
  0.0 0.5 collective-permute-start.2
  0.5 3.5 %route.2 = (bf16[80,3584]{1,0:T(8,128)(2,1)}, bf16[80,3584]{1,0:T(8,128)(2,1)}, bf16[80,3584]{1,0:T(8,128)(2,1)}, bf16[80,3584]{1,0:T(8,128)(2,1)}, bf16[4,80,25...) custom-call(bf16[128,3584]{1,0:T(8,128)(2,1)} %bitcast.18, f32[1,3584]{1,0:T(1,128)} %refs_1_.3, s32[2,128]{1,0:T(2,128)} %bitcast.19, ...), custom_call_target="tpu_custom_call" | custom-call | tf_op jit(solution)/shard_map/route/pallas_call | solution.py:133
  4.1 1.7 %collective-permute-start = (bf16[128,3712]{1,0:T(8,128)(2,1)}, bf16[128,3712]{1,0:T(8,128)(2,1)S(1)}, u32[]{:S(2)}, u32[]{:S(2)}) collective-permute-start(bf16[128,3712]{1,0:T(8,128)(2,1)} %get-tuple-element.39.refs_3_.refs_8_), channel_id=1, source_target_pairs={{0,2},{1,3},{2,0},{3,1},{4,6},{5,7},{6,4},{7,5},{8,10},{9,11},{10,... | collective-permute-start | bytes 2850824 | tf_op jit(solution)/shard_map/ppermute | solution.py:43
  5.7 2.1 %collective-permute-start.4 = (bf16[80,3584]{1,0:T(8,128)(2,1)}, bf16[80,3584]{1,0:T(8,128)(2,1)S(1)}, u32[]{:S(2)}, u32[]{:S(2)}) collective-permute-start(bf16[80,3584]{1,0:T(8,128)(2,1)} %get-tuple-element.40), channel_id=1, source_target_pairs={{0,8},{1,9},{2,10},{3,11},{4,12},{5,13},{6,14},{7,15},{8,0},{9,1},... | collective-permute-start | bytes 1720328 | tf_op jit(solution)/shard_map/ppermute | solution.py:43
  7.8 1.2 %copy-done.1 = bf16[128,3712]{1,0:T(8,128)(2,1)S(1)} copy-done((bf16[128,3712]{1,0:T(8,128)(2,1)S(1)}, bf16[128,3712]{1,0:T(8,128)(2,1)}, u32[]{:S(2)}) %copy-start.1) | copy-done | bytes 950296
  9.0 6.2 %load.3 = (bf16[3584,512]{1,0:T(8,128)(2,1)S(1)}, bf16[3584,512]{1,0:T(8,128)(2,1)S(1)}, bf16[512,3584]{1,0:T(8,128)(2,1)}) custom-call(bf16[3584,512]{1,0:T(8,128)(2,1)} %bitcast.13, bf16[3584,512]{1,0:T(8,128)(2,1)} %bitcast.15, bf16[512,3584]{1,0:T(8,128)(2,1)} %bitcast.17, bf16[128,3712]{1,0:T(8,128)(2,1)S(1)} %copy-done.1), custom_call_target="tpu_custom_call" | custom-call | tf_op jit(solution)/shard_map/load/pallas_call | solution.py:165
  15.3 2.0 %collective-permute-done.3.refs_2_.refs_4_ = bf16[512,3584]{1,0:T(8,128)(2,1)} collective-permute-done((bf16[512,3584]{1,0:T(8,128)(2,1)}, bf16[512,3584]{1,0:T(8,128)(2,1)}, u32[]{:S(2)}, u32[]{:S(2)}) %collective-permute-start.3) | collective-permute-done | bytes 3670048 | tf_op jit(solution)/shard_map/ppermute | solution.py:43
  17.3 1.5 %collective-permute-start.5 = (bf16[80,3584]{1,0:T(8,128)(2,1)S(1)}, bf16[80,3584]{1,0:T(8,128)(2,1)S(1)}, u32[]{:S(2)}, u32[]{:S(2)}) collective-permute-start(bf16[80,3584]{1,0:T(8,128)(2,1)S(1)} %get-tuple-element.47.refs_1_), channel_id=1, source_target_pairs={{0,4},{1,5},{2,6},{3,7},{4,8},{5,9},{6,10},{7,11},{8,12},{9,13},{1... | collective-permute-start | bytes 1720328 | tf_op jit(solution)/shard_map/ppermute | solution.py:43
  18.8 0.9 collective-permute-start.6
  19.6 3.1 %collective-permute-done.4.refs_3_.refs_0_ = bf16[80,3584]{1,0:T(8,128)(2,1)S(1)} collective-permute-done((bf16[80,3584]{1,0:T(8,128)(2,1)}, bf16[80,3584]{1,0:T(8,128)(2,1)S(1)}, u32[]{:S(2)}, u32[]{:S(2)}) %collective-permute-start.4) | collective-permute-done | bytes 573472 | tf_op jit(solution)/shard_map/ppermute | solution.py:43
  22.7 4.2 %load.2 = (bf16[3584,512]{1,0:T(8,128)(2,1)S(1)}, bf16[3584,512]{1,0:T(8,128)(2,1)S(1)}, bf16[512,3584]{1,0:T(8,128)(2,1)S(1)}) custom-call(bf16[3584,512]{1,0:T(8,128)(2,1)} %collective-permute-done.1.refs_0_.refs_2_, bf16[3584,512]{1,0:T(8,128)(2,1)} %collective-permute-done.2.refs_1_.refs_3_, bf16[512,3584]{1,0:T(8,128)(2,1)} %collective-permute-done.3.refs_2_.refs_4_, ...), custom_call_target="tpu_custom_call" | custom-call | tf_op jit(solution)/shard_map/load/pallas_call | solution.py:165
  27.0 0.8 collective-permute-done.refs_0_.refs_3_.refs_9_
  27.8 1.6 %collective-permute-start.9 = (bf16[80,3584]{1,0:T(8,128)(2,1)S(1)}, bf16[80,3584]{1,0:T(8,128)(2,1)S(1)}, u32[]{:S(2)}, u32[]{:S(2)}) collective-permute-start(bf16[80,3584]{1,0:T(8,128)(2,1)S(1)} %after.5.refs_1_), channel_id=1, source_target_pairs={{0,2},{1,3},{2,0},{3,1},{4,6},{5,7},{6,4},{7,5},{8,10},{9,11},{10,... | collective-permute-start | bytes 1720328 | tf_op jit(solution)/shard_map/ppermute | solution.py:43
  29.4 0.9 route.3
  30.3 1.6 %collective-permute-start.10 = (bf16[80,3584]{1,0:T(8,128)(2,1)S(1)}, bf16[80,3584]{1,0:T(8,128)(2,1)S(1)}, u32[]{:S(2)}, u32[]{:S(2)}) collective-permute-start(bf16[80,3584]{1,0:T(8,128)(2,1)S(1)} %get-tuple-element.59), channel_id=1, source_target_pairs={{0,4},{1,5},{2,6},{3,7},{4,8},{5,9},{6,10},{7,11},{8,12},{9,13},{1... | collective-permute-start | bytes 1720328 | tf_op jit(solution)/shard_map/ppermute | solution.py:43
  31.9 0.5 collective-permute-start.11
  32.4 3.2 %collective-permute-done.5.refs_2_ = bf16[80,3584]{1,0:T(8,128)(2,1)S(1)} collective-permute-done((bf16[80,3584]{1,0:T(8,128)(2,1)S(1)}, bf16[80,3584]{1,0:T(8,128)(2,1)S(1)}, u32[]{:S(2)}, u32[]{:S(2)}) %collective-permute-start.5) | collective-permute-done | bytes 573472 | tf_op jit(solution)/shard_map/ppermute | solution.py:43
  35.6 7.3 %expert.3 = (bf16[80,3584]{1,0:T(8,128)(2,1)S(1)}, bf16[80,3584]{1,0:T(8,128)(2,1)S(1)}, bf16[80,3584]{1,0:T(8,128)(2,1)S(1)}, bf16[80,3584]{1,0:T(8,128)(2,1)S(1)}) custom-call(bf16[80,3584]{1,0:T(8,128)(2,1)S(1)} %copy-done.6, bf16[80,3584]{1,0:T(8,128)(2,1)S(1)} %after.5.refs_1_, bf16[80,3584]{1,0:T(8,128)(2,1)S(1)} %collective-permute-done.5.refs_2_, ...), custom_call_target="tpu_custom_call" | custom-call | tf_op jit(solution)/shard_map/expert/pallas_call | solution.py:230
  42.9 1.0 collective-permute-start.7
  43.9 1.1 collective-permute-start.8
  45.0 3.8 %expert.4 = (bf16[80,3584]{1,0:T(8,128)(2,1)S(1)}, bf16[80,3584]{1,0:T(8,128)(2,1)S(1)}, bf16[80,3584]{1,0:T(8,128)(2,1)S(1)}) custom-call(bf16[80,3584]{1,0:T(8,128)(2,1)S(1)} %collective-permute-done.9.refs_0_, bf16[80,3584]{1,0:T(8,128)(2,1)S(1)} %get-tuple-element.56.refs_1_, bf16[3584,512]{1,0:T(8,128)(2,1)S(1)} %get-tuple-element.46.refs_5_.refs_4_.refs_2_, ...), custom_call_target="tpu_custom_call" | custom-call | tf_op jit(solution)/shard_map/expert/pallas_call | solution.py:230
  48.8 0.9 collective-permute-start.14
  49.7 3.8 %expert.5 = (bf16[80,1792]{1,0:T(8,128)(2,1)S(1)}, bf16[80,1792]{1,0:T(8,128)(2,1)S(1)}, bf16[80,1792]{1,0:T(8,128)(2,1)S(1)}, bf16[80,1792]{1,0:T(8,128)(2,1)S(1)}) custom-call(bf16[80,3584]{1,0:T(8,128)(2,1)S(1)} %collective-permute-done.10.refs_0_, bf16[80,3584]{1,0:T(8,128)(2,1)S(1)} %collective-permute-done.11.refs_1_, ...), custom_call_target="tpu_custom_call" | custom-call | tf_op jit(solution)/shard_map/expert/pallas_call | solution.py:230
  53.5 1.6 %collective-permute-start.12 = (bf16[80,1792]{1,0:T(8,128)(2,1)S(1)}, bf16[80,1792]{1,0:T(8,128)(2,1)S(1)}, u32[]{:S(2)}, u32[]{:S(2)}) collective-permute-start(bf16[80,1792]{1,0:T(8,128)(2,1)S(1)} %get-tuple-element.62), channel_id=1, source_target_pairs={{0,12},{1,13},{2,14},{3,15},{4,0},{5,1},{6,2},{7,3},{8,4},{9,5},{1... | collective-permute-start | bytes 860168 | tf_op jit(solution)/shard_map/ppermute | solution.py:43
  55.1 0.5 collective-permute-start.13
  55.6 4.5 %collective-permute-done.7.refs_1_.refs_2_ = bf16[80,3584]{1,0:T(8,128)(2,1)S(1)} collective-permute-done((bf16[80,3584]{1,0:T(8,128)(2,1)S(1)}, bf16[80,3584]{1,0:T(8,128)(2,1)S(1)}, u32[]{:S(2)}, u32[]{:S(2)}) %collective-permute-start.7) | collective-permute-done | bytes 573472 | tf_op jit(solution)/shard_map/ppermute | solution.py:43
  60.1 0.8 collective-permute-done.8.refs_2_.refs_3_
  60.9 1.5 %collective-permute-start.18 = (bf16[80,1792]{1,0:T(8,128)(2,1)S(1)}, bf16[80,1792]{1,0:T(8,128)(2,1)S(1)}, u32[]{:S(2)}, u32[]{:S(2)}) collective-permute-start(bf16[80,1792]{1,0:T(8,128)(2,1)S(1)} %get-tuple-element.68), channel_id=1, source_target_pairs={{0,12},{1,13},{2,14},{3,15},{4,0},{5,1},{6,2},{7,3},{8,4},{9,5},{1... | collective-permute-start | bytes 860168 | tf_op jit(solution)/shard_map/ppermute | solution.py:43
  62.5 0.5 collective-permute-start.19
  63.1 3.5 %collective-permute-start.15 = (bf16[80,1792]{1,0:T(8,128)(2,1)S(1)}, bf16[80,1792]{1,0:T(8,128)(2,1)S(1)}, u32[]{:S(2)}, u32[]{:S(2)}) collective-permute-start(bf16[80,1792]{1,0:T(8,128)(2,1)S(1)} %get-tuple-element.65), channel_id=1, source_target_pairs={{0,8},{1,9},{2,10},{3,11},{4,12},{5,13},{6,14},{7,15},{8,0},{9,1},... | collective-permute-start | bytes 860168 | tf_op jit(solution)/shard_map/ppermute | solution.py:43
  66.6 0.5 collective-permute-done.13.refs_5_
  67.1 0.4 leave.2
  67.5 1.1 %collective-permute-start.16 = (bf16[128,1792]{1,0:T(8,128)(2,1)S(1)}, bf16[128,1792]{1,0:T(8,128)(2,1)S(1)}, u32[]{:S(2)}, u32[]{:S(2)}) collective-permute-start(bf16[128,1792]{1,0:T(8,128)(2,1)S(1)} %leave.2), channel_id=1, source_target_pairs={{0,2},{1,3},{2,0},{3,1},{4,6},{5,7},{6,4},{7,5},{8,10},{9,11},{10,... | collective-permute-start | bytes 1376264 | tf_op jit(solution)/shard_map/ppermute | solution.py:43
  68.6 4.4 %collective-permute-done.18.refs_4_ = bf16[80,1792]{1,0:T(8,128)(2,1)S(1)} collective-permute-done((bf16[80,1792]{1,0:T(8,128)(2,1)S(1)}, bf16[80,1792]{1,0:T(8,128)(2,1)S(1)}, u32[]{:S(2)}, u32[]{:S(2)}) %collective-permute-start.18) | collective-permute-done | bytes 286752 | tf_op jit(solution)/shard_map/ppermute | solution.py:43
  73.0 0.2 collective-permute-done.19.refs_5_
  73.2 0.4 leave.3
  73.7 1.1 collective-permute-start.21
  74.8 3.1 %collective-permute-done.15.refs_6_.refs_1_ = bf16[80,1792]{1,0:T(8,128)(2,1)S(1)} collective-permute-done((bf16[80,1792]{1,0:T(8,128)(2,1)S(1)}, bf16[80,1792]{1,0:T(8,128)(2,1)S(1)}, u32[]{:S(2)}, u32[]{:S(2)}) %collective-permute-start.15) | collective-permute-done | bytes 286752 | tf_op jit(solution)/shard_map/ppermute | solution.py:43
  77.8 3.9 %collective-permute-start.20 = (bf16[80,1792]{1,0:T(8,128)(2,1)S(1)}, bf16[80,1792]{1,0:T(8,128)(2,1)S(1)}, u32[]{:S(2)}, u32[]{:S(2)}) collective-permute-start(bf16[80,1792]{1,0:T(8,128)(2,1)S(1)} %after.7), channel_id=1, source_target_pairs={{0,8},{1,9},{2,10},{3,11},{4,12},{5,13},{6,14},{7,15},{8,0},{9,1},... | collective-permute-start | bytes 860168 | tf_op jit(solution)/shard_map/ppermute | solution.py:43
  81.7 0.7 stay.2
  82.4 1.4 %collective-permute-start.17 = (bf16[128,1792]{1,0:T(8,128)(2,1)S(1)}, bf16[128,1792]{1,0:T(8,128)(2,1)S(1)}, u32[]{:S(2)}, u32[]{:S(2)}) collective-permute-start(bf16[128,1792]{1,0:T(8,128)(2,1)S(1)} %stay.2), channel_id=1, source_target_pairs={{0,16},{1,17},{2,18},{3,19},{4,20},{5,21},{6,22},{7,23},{8,24},{9,... | collective-permute-start | bytes 1376264 | tf_op jit(solution)/shard_map/ppermute | solution.py:52
  83.8 3.1 %collective-permute-done.20.refs_6_ = bf16[80,1792]{1,0:T(8,128)(2,1)S(1)} collective-permute-done((bf16[80,1792]{1,0:T(8,128)(2,1)S(1)}, bf16[80,1792]{1,0:T(8,128)(2,1)S(1)}, u32[]{:S(2)}, u32[]{:S(2)}) %collective-permute-start.20) | collective-permute-done | bytes 286752 | tf_op jit(solution)/shard_map/ppermute | solution.py:43
  86.9 0.9 collective-permute-done.21.refs_7_
  87.8 0.7 stay.3
  88.5 2.0 %collective-permute-start.22 = (bf16[128,1792]{1,0:T(8,128)(2,1)S(1)}, bf16[128,1792]{1,0:T(8,128)(2,1)S(1)}, u32[]{:S(2)}, u32[]{:S(2)}) collective-permute-start(bf16[128,1792]{1,0:T(8,128)(2,1)S(1)} %stay.3), channel_id=1, source_target_pairs={{0,16},{1,17},{2,18},{3,19},{4,20},{5,21},{6,22},{7,23},{8,24},{9,... | collective-permute-start | bytes 1376264 | tf_op jit(solution)/shard_map/ppermute | solution.py:52
  90.5 9.9 %collective-permute-done.17 = bf16[128,1792]{1,0:T(8,128)(2,1)S(1)} collective-permute-done((bf16[128,1792]{1,0:T(8,128)(2,1)S(1)}, bf16[128,1792]{1,0:T(8,128)(2,1)S(1)}, u32[]{:S(2)}, u32[]{:S(2)}) %collective-permute-start.17) | collective-permute-done | bytes 458784 | tf_op jit(solution)/shard_map/ppermute | solution.py:52
  100.4 7.7 %collective-permute-done.22 = bf16[128,1792]{1,0:T(8,128)(2,1)S(1)} collective-permute-done((bf16[128,1792]{1,0:T(8,128)(2,1)S(1)}, bf16[128,1792]{1,0:T(8,128)(2,1)S(1)}, u32[]{:S(2)}, u32[]{:S(2)}) %collective-permute-start.22) | collective-permute-done | bytes 458784 | tf_op jit(solution)/shard_map/ppermute | solution.py:52
  108.1 1.0 maximum_bitcast_fusion
  (31 shorter events, 0.2 us)
Async XLA Ops:
  0.0 15.3 %collective-permute-start.1 = (bf16[3584,512]{1,0:T(8,128)(2,1)}, bf16[3584,512]{1,0:T(8,128)(2,1)}, u32[]{:S(2)}, u32[]{:S(2)}) collective-permute-start(bf16[3584,512]{1,0:T(8,128)(2,1)} %bitcast.12), channel_id=1, source_target_pairs={{0,1},{1,0},{2,3},{3,2},{4,5},{5,4},{6,7},{7,6},{8,9},{9,8},{10,11... | collective-permute-start | bytes 11010056 | tf_op jit(solution)/shard_map/ppermute | solution.py:43
  0.0 15.3 %collective-permute-start.2 = (bf16[3584,512]{1,0:T(8,128)(2,1)}, bf16[3584,512]{1,0:T(8,128)(2,1)}, u32[]{:S(2)}, u32[]{:S(2)}) collective-permute-start(bf16[3584,512]{1,0:T(8,128)(2,1)} %bitcast.14), channel_id=1, source_target_pairs={{0,1},{1,0},{2,3},{3,2},{4,5},{5,4},{6,7},{7,6},{8,9},{9,8},{10,11... | collective-permute-start | bytes 11010056 | tf_op jit(solution)/shard_map/ppermute | solution.py:43
  0.5 16.7 %collective-permute-start.3 = (bf16[512,3584]{1,0:T(8,128)(2,1)}, bf16[512,3584]{1,0:T(8,128)(2,1)}, u32[]{:S(2)}, u32[]{:S(2)}) collective-permute-start(bf16[512,3584]{1,0:T(8,128)(2,1)} %bitcast.16), channel_id=1, source_target_pairs={{0,1},{1,0},{2,3},{3,2},{4,5},{5,4},{6,7},{7,6},{8,9},{9,8},{10,11... | collective-permute-start | bytes 11010056 | tf_op jit(solution)/shard_map/ppermute | solution.py:43
  4.1 23.8 %collective-permute-start = (bf16[128,3712]{1,0:T(8,128)(2,1)}, bf16[128,3712]{1,0:T(8,128)(2,1)S(1)}, u32[]{:S(2)}, u32[]{:S(2)}) collective-permute-start(bf16[128,3712]{1,0:T(8,128)(2,1)} %get-tuple-element.39.refs_3_.refs_8_), channel_id=1, source_target_pairs={{0,2},{1,3},{2,0},{3,1},{4,6},{5,7},{6,4},{7,5},{8,10},{9,11},{10,... | collective-permute-start | bytes 2850824 | tf_op jit(solution)/shard_map/ppermute | solution.py:43
  5.7 17.0 %collective-permute-start.4 = (bf16[80,3584]{1,0:T(8,128)(2,1)}, bf16[80,3584]{1,0:T(8,128)(2,1)S(1)}, u32[]{:S(2)}, u32[]{:S(2)}) collective-permute-start(bf16[80,3584]{1,0:T(8,128)(2,1)} %get-tuple-element.40), channel_id=1, source_target_pairs={{0,8},{1,9},{2,10},{3,11},{4,12},{5,13},{6,14},{7,15},{8,0},{9,1},... | collective-permute-start | bytes 1720328 | tf_op jit(solution)/shard_map/ppermute | solution.py:43
  7.8 1.2 %copy-start.1 = (bf16[128,3712]{1,0:T(8,128)(2,1)S(1)}, bf16[128,3712]{1,0:T(8,128)(2,1)}, u32[]{:S(2)}) copy-start(bf16[128,3712]{1,0:T(8,128)(2,1)} %get-tuple-element.39.refs_3_.refs_8_) | copy-start | bytes 2850820
  9.0 8.2 %copy-start.4 = (bf16[80,3584]{1,0:T(8,128)(2,1)S(1)}, bf16[80,3584]{1,0:T(8,128)(2,1)}, u32[]{:S(2)}) copy-start(bf16[80,3584]{1,0:T(8,128)(2,1)} %get-tuple-element.44.refs_0_) | copy-start | bytes 1720324
  9.0 8.2 %copy-start.5 = (bf16[80,3584]{1,0:T(8,128)(2,1)S(1)}, bf16[80,3584]{1,0:T(8,128)(2,1)}, u32[]{:S(2)}) copy-start(bf16[80,3584]{1,0:T(8,128)(2,1)} %get-tuple-element.45.refs_1_) | copy-start | bytes 1720324
  17.3 18.4 %collective-permute-start.5 = (bf16[80,3584]{1,0:T(8,128)(2,1)S(1)}, bf16[80,3584]{1,0:T(8,128)(2,1)S(1)}, u32[]{:S(2)}, u32[]{:S(2)}) collective-permute-start(bf16[80,3584]{1,0:T(8,128)(2,1)S(1)} %get-tuple-element.47.refs_1_), channel_id=1, source_target_pairs={{0,4},{1,5},{2,6},{3,7},{4,8},{5,9},{6,10},{7,11},{8,12},{9,13},{1... | collective-permute-start | bytes 1720328 | tf_op jit(solution)/shard_map/ppermute | solution.py:43
  18.7 10.7 %copy-start.7 = (f32[1,3584]{1,0:T(1,128)S(1)}, f32[1,3584]{1,0:T(1,128)}, u32[]{:S(2)}) copy-start(f32[1,3584]{1,0:T(1,128)} %refs_1_.3) | copy-start | bytes 43012
  18.8 16.9 %collective-permute-start.6 = (bf16[80,3584]{1,0:T(8,128)(2,1)S(1)}, bf16[80,3584]{1,0:T(8,128)(2,1)S(1)}, u32[]{:S(2)}, u32[]{:S(2)}) collective-permute-start(bf16[80,3584]{1,0:T(8,128)(2,1)S(1)} %get-tuple-element.48.refs_2_), channel_id=1, source_target_pairs={{0,12},{1,13},{2,14},{3,15},{4,0},{5,1},{6,2},{7,3},{8,4},{9,5},{1... | collective-permute-start | bytes 1720328 | tf_op jit(solution)/shard_map/ppermute | solution.py:43
  27.0 8.7 %copy-start = (bf16[512,3584]{1,0:T(8,128)(2,1)S(1)}, bf16[512,3584]{1,0:T(8,128)(2,1)}, u32[]{:S(2)}) copy-start(bf16[512,3584]{1,0:T(8,128)(2,1)} %get-tuple-element.50.refs_6_.refs_4_) | copy-start | bytes 11010052
  27.0 8.7 %copy-start.6 = (bf16[80,3584]{1,0:T(8,128)(2,1)S(1)}, bf16[80,3584]{1,0:T(8,128)(2,1)}, u32[]{:S(2)}) copy-start(bf16[80,3584]{1,0:T(8,128)(2,1)} %get-tuple-element.43.refs_0_) | copy-start | bytes 1720324
  27.8 17.2 %collective-permute-start.9 = (bf16[80,3584]{1,0:T(8,128)(2,1)S(1)}, bf16[80,3584]{1,0:T(8,128)(2,1)S(1)}, u32[]{:S(2)}, u32[]{:S(2)}) collective-permute-start(bf16[80,3584]{1,0:T(8,128)(2,1)S(1)} %after.5.refs_1_), channel_id=1, source_target_pairs={{0,2},{1,3},{2,0},{3,1},{4,6},{5,7},{6,4},{7,5},{8,10},{9,11},{10,... | collective-permute-start | bytes 1720328 | tf_op jit(solution)/shard_map/ppermute | solution.py:43
  30.3 19.4 %collective-permute-start.10 = (bf16[80,3584]{1,0:T(8,128)(2,1)S(1)}, bf16[80,3584]{1,0:T(8,128)(2,1)S(1)}, u32[]{:S(2)}, u32[]{:S(2)}) collective-permute-start(bf16[80,3584]{1,0:T(8,128)(2,1)S(1)} %get-tuple-element.59), channel_id=1, source_target_pairs={{0,4},{1,5},{2,6},{3,7},{4,8},{5,9},{6,10},{7,11},{8,12},{9,13},{1... | collective-permute-start | bytes 1720328 | tf_op jit(solution)/shard_map/ppermute | solution.py:43
  31.9 17.8 %collective-permute-start.11 = (bf16[80,3584]{1,0:T(8,128)(2,1)S(1)}, bf16[80,3584]{1,0:T(8,128)(2,1)S(1)}, u32[]{:S(2)}, u32[]{:S(2)}) collective-permute-start(bf16[80,3584]{1,0:T(8,128)(2,1)S(1)} %get-tuple-element.60), channel_id=1, source_target_pairs={{0,12},{1,13},{2,14},{3,15},{4,0},{5,1},{6,2},{7,3},{8,4},{9,5},{1... | collective-permute-start | bytes 1720328 | tf_op jit(solution)/shard_map/ppermute | solution.py:43
  42.9 17.2 %collective-permute-start.7 = (bf16[80,3584]{1,0:T(8,128)(2,1)S(1)}, bf16[80,3584]{1,0:T(8,128)(2,1)S(1)}, u32[]{:S(2)}, u32[]{:S(2)}) collective-permute-start(bf16[80,3584]{1,0:T(8,128)(2,1)S(1)} %get-tuple-element.54), channel_id=1, source_target_pairs={{0,12},{1,13},{2,14},{3,15},{4,0},{5,1},{6,2},{7,3},{8,4},{9,5},{1... | collective-permute-start | bytes 1720328 | tf_op jit(solution)/shard_map/ppermute | solution.py:43
  43.9 17.0 %collective-permute-start.8 = (bf16[80,3584]{1,0:T(8,128)(2,1)S(1)}, bf16[80,3584]{1,0:T(8,128)(2,1)S(1)}, u32[]{:S(2)}, u32[]{:S(2)}) collective-permute-start(bf16[80,3584]{1,0:T(8,128)(2,1)S(1)} %get-tuple-element.55), channel_id=1, source_target_pairs={{0,4},{1,5},{2,6},{3,7},{4,8},{5,9},{6,10},{7,11},{8,12},{9,13},{1... | collective-permute-start | bytes 1720328 | tf_op jit(solution)/shard_map/ppermute | solution.py:43
  48.8 18.3 %copy-start.3 = (bf16[4,80,256]{2,1,0:T(8,128)(2,1)S(1)}, bf16[4,80,256]{2,1,0:T(8,128)(2,1)}, u32[]{:S(2)}) copy-start(bf16[4,80,256]{2,1,0:T(8,128)(2,1)} %get-tuple-element.38.w_own_ref) | copy-start | bytes 491524
  48.8 14.1 %collective-permute-start.14 = (bf16[80,3584]{1,0:T(8,128)(2,1)S(1)}, bf16[80,3584]{1,0:T(8,128)(2,1)S(1)}, u32[]{:S(2)}, u32[]{:S(2)}) collective-permute-start(bf16[80,3584]{1,0:T(8,128)(2,1)S(1)} %get-tuple-element.61.refs_8_), channel_id=1, source_target_pairs={{0,2},{1,3},{2,0},{3,1},{4,6},{5,7},{6,4},{7,5},{8,10},{9,11},{10,... | collective-permute-start | bytes 1720328 | tf_op jit(solution)/shard_map/ppermute | solution.py:43
  53.5 13.1 %collective-permute-start.12 = (bf16[80,1792]{1,0:T(8,128)(2,1)S(1)}, bf16[80,1792]{1,0:T(8,128)(2,1)S(1)}, u32[]{:S(2)}, u32[]{:S(2)}) collective-permute-start(bf16[80,1792]{1,0:T(8,128)(2,1)S(1)} %get-tuple-element.62), channel_id=1, source_target_pairs={{0,12},{1,13},{2,14},{3,15},{4,0},{5,1},{6,2},{7,3},{8,4},{9,5},{1... | collective-permute-start | bytes 860168 | tf_op jit(solution)/shard_map/ppermute | solution.py:43
  55.1 12.0 %collective-permute-start.13 = (bf16[80,1792]{1,0:T(8,128)(2,1)S(1)}, bf16[80,1792]{1,0:T(8,128)(2,1)S(1)}, u32[]{:S(2)}, u32[]{:S(2)}) collective-permute-start(bf16[80,1792]{1,0:T(8,128)(2,1)S(1)} %get-tuple-element.63), channel_id=1, source_target_pairs={{0,4},{1,5},{2,6},{3,7},{4,8},{5,9},{6,10},{7,11},{8,12},{9,13},{1... | collective-permute-start | bytes 860168 | tf_op jit(solution)/shard_map/ppermute | solution.py:43
  60.9 12.1 %collective-permute-start.18 = (bf16[80,1792]{1,0:T(8,128)(2,1)S(1)}, bf16[80,1792]{1,0:T(8,128)(2,1)S(1)}, u32[]{:S(2)}, u32[]{:S(2)}) collective-permute-start(bf16[80,1792]{1,0:T(8,128)(2,1)S(1)} %get-tuple-element.68), channel_id=1, source_target_pairs={{0,12},{1,13},{2,14},{3,15},{4,0},{5,1},{6,2},{7,3},{8,4},{9,5},{1... | collective-permute-start | bytes 860168 | tf_op jit(solution)/shard_map/ppermute | solution.py:43
  62.5 10.8 %collective-permute-start.19 = (bf16[80,1792]{1,0:T(8,128)(2,1)S(1)}, bf16[80,1792]{1,0:T(8,128)(2,1)S(1)}, u32[]{:S(2)}, u32[]{:S(2)}) collective-permute-start(bf16[80,1792]{1,0:T(8,128)(2,1)S(1)} %get-tuple-element.69), channel_id=1, source_target_pairs={{0,4},{1,5},{2,6},{3,7},{4,8},{5,9},{6,10},{7,11},{8,12},{9,13},{1... | collective-permute-start | bytes 860168 | tf_op jit(solution)/shard_map/ppermute | solution.py:43
  63.1 14.7 %collective-permute-start.15 = (bf16[80,1792]{1,0:T(8,128)(2,1)S(1)}, bf16[80,1792]{1,0:T(8,128)(2,1)S(1)}, u32[]{:S(2)}, u32[]{:S(2)}) collective-permute-start(bf16[80,1792]{1,0:T(8,128)(2,1)S(1)} %get-tuple-element.65), channel_id=1, source_target_pairs={{0,8},{1,9},{2,10},{3,11},{4,12},{5,13},{6,14},{7,15},{8,0},{9,1},... | collective-permute-start | bytes 860168 | tf_op jit(solution)/shard_map/ppermute | solution.py:43
  67.1 14.6 %copy-start.2 = (bf16[128,3712]{1,0:T(8,128)(2,1)S(1)}, bf16[128,3712]{1,0:T(8,128)(2,1)}, u32[]{:S(2)}) copy-start(bf16[128,3712]{1,0:T(8,128)(2,1)} %get-tuple-element.39.refs_3_.refs_8_) | copy-start | bytes 2850820
  67.5 14.2 %collective-permute-start.16 = (bf16[128,1792]{1,0:T(8,128)(2,1)S(1)}, bf16[128,1792]{1,0:T(8,128)(2,1)S(1)}, u32[]{:S(2)}, u32[]{:S(2)}) collective-permute-start(bf16[128,1792]{1,0:T(8,128)(2,1)S(1)} %leave.2), channel_id=1, source_target_pairs={{0,2},{1,3},{2,0},{3,1},{4,6},{5,7},{6,4},{7,5},{8,10},{9,11},{10,... | collective-permute-start | bytes 1376264 | tf_op jit(solution)/shard_map/ppermute | solution.py:43
  73.7 14.1 %collective-permute-start.21 = (bf16[128,1792]{1,0:T(8,128)(2,1)S(1)}, bf16[128,1792]{1,0:T(8,128)(2,1)S(1)}, u32[]{:S(2)}, u32[]{:S(2)}) collective-permute-start(bf16[128,1792]{1,0:T(8,128)(2,1)S(1)} %leave.3), channel_id=1, source_target_pairs={{0,2},{1,3},{2,0},{3,1},{4,6},{5,7},{6,4},{7,5},{8,10},{9,11},{10,... | collective-permute-start | bytes 1376264 | tf_op jit(solution)/shard_map/ppermute | solution.py:43
  77.8 9.0 %collective-permute-start.20 = (bf16[80,1792]{1,0:T(8,128)(2,1)S(1)}, bf16[80,1792]{1,0:T(8,128)(2,1)S(1)}, u32[]{:S(2)}, u32[]{:S(2)}) collective-permute-start(bf16[80,1792]{1,0:T(8,128)(2,1)S(1)} %after.7), channel_id=1, source_target_pairs={{0,8},{1,9},{2,10},{3,11},{4,12},{5,13},{6,14},{7,15},{8,0},{9,1},... | collective-permute-start | bytes 860168 | tf_op jit(solution)/shard_map/ppermute | solution.py:43
  82.4 18.0 %collective-permute-start.17 = (bf16[128,1792]{1,0:T(8,128)(2,1)S(1)}, bf16[128,1792]{1,0:T(8,128)(2,1)S(1)}, u32[]{:S(2)}, u32[]{:S(2)}) collective-permute-start(bf16[128,1792]{1,0:T(8,128)(2,1)S(1)} %stay.2), channel_id=1, source_target_pairs={{0,16},{1,17},{2,18},{3,19},{4,20},{5,21},{6,22},{7,23},{8,24},{9,... | collective-permute-start | bytes 1376264 | tf_op jit(solution)/shard_map/ppermute | solution.py:52
  88.5 19.6 %collective-permute-start.22 = (bf16[128,1792]{1,0:T(8,128)(2,1)S(1)}, bf16[128,1792]{1,0:T(8,128)(2,1)S(1)}, u32[]{:S(2)}, u32[]{:S(2)}) collective-permute-start(bf16[128,1792]{1,0:T(8,128)(2,1)S(1)} %stay.3), channel_id=1, source_target_pairs={{0,16},{1,17},{2,18},{3,19},{4,20},{5,21},{6,22},{7,23},{8,24},{9,... | collective-permute-start | bytes 1376264 | tf_op jit(solution)/shard_map/ppermute | solution.py:52

commit v6 on v5

--- a/solution.py
+++ b/solution.py
@@ -266,6 +266,31 @@
     )(a, b)
 
 
+def join_kernel(a_ref, b_ref, out_ref, sems):
+    width = a_ref.shape[1]
+    copies = [
+        pltpu.make_async_copy(a_ref, out_ref.at[:, :width], sems.at[0]),
+        pltpu.make_async_copy(b_ref, out_ref.at[:, width:], sems.at[1]),
+    ]
+    for copy in copies:
+        copy.start()
+    for copy in copies:
+        copy.wait()
+
+
+def joined(parts):
+    return pl.pallas_call(
+        join_kernel,
+        out_shape=jax.ShapeDtypeStruct((parts[0].shape[0], sum(PARTS)), BF16),
+        in_specs=[VMEM] * 2,
+        out_specs=HBM,
+        scratch_shapes=[pltpu.SemaphoreType.DMA((2,))],
+        cost_estimate=FREE,
+        compiler_params=limit(2),
+        name="join",
+    )(*parts)
+
+
 def after_kernel(*refs):
     pass
 
@@ -397,7 +422,7 @@
             (*own_back, *across_back, far_back, mine, sent, tok_across),
         )
         outs.append(handed_on(layer_out))
-    return jnp.concatenate(outs, axis=1)[None]
+    return joined(outs)[None]
 
 
 def solution(mesh):

time: 109 us -> 109 us (level)
  no operation moved by 1% of the time
where the time goes in v6:
time: 109 us
  waiting for transfers between devices  44.2 us (41%)
  Pallas kernels  33.1 us (30%)
  starting transfers between devices  30.4 us (28%)
  local copies, waits for them, and re-layouts  1.22 us (1%)
    ppermute x21, starting transfers between devices, moved(): return lax.ppermute(value, 'expert', pairs)  27 us
    ppermute x21, waiting for transfers between devices, moved(): return lax.ppermute(value, 'expert', pairs)  26.6 us
    ppermute x2, waiting for transfers between devices, handed_on(): return lax.ppermute(value, ('section', 'expert'), pairs)  17.6 us
    pallas_call x3, Pallas kernels, expert(): pl.pallas_call(body, out_shape=out_shape, in_specs=[VMEM] * inner + [ANY]...  14.9 us
    pallas_call x2, Pallas kernels, load(): pl.pallas_call(functools.partial(load_kernel, count), out_shape=[jax.Shap...  10.4 us
    pallas_call x2, Pallas kernels, route(): pl.pallas_call(body, out_shape=out_shape, in_specs=[HBM if first_set else...  4.44 us
    ppermute x2, starting transfers between devices, handed_on(): return lax.ppermute(value, ('section', 'expert'), pairs)  3.38 us
    pallas_call x4, Pallas kernels, mix(): pl.pallas_call(functools.partial(kernel, slice(begin, begin + width)), ou...  2.27 us
  transfers between devices with their start and end apart: 23, of which 14 were waited for; matrix products, arithmetic and copies ran while one was open for 0% of the time, Pallas kernels for 29%

profile of v6, /device:TPU:2, one launch (start us, length us, event | category | flops | bytes accessed | tf_op | source)
XLA Modules:
  0.0 109.2 jit_solution(18124700015918983162)
XLA Ops:
  0.0 0.5 collective-permute-start.2
  0.5 3.5 %route.2 = (bf16[80,3584]{1,0:T(8,128)(2,1)}, bf16[80,3584]{1,0:T(8,128)(2,1)}, bf16[80,3584]{1,0:T(8,128)(2,1)}, bf16[80,3584]{1,0:T(8,128)(2,1)}, bf16[4,80,25...) custom-call(bf16[128,3584]{1,0:T(8,128)(2,1)} %bitcast.17, f32[1,3584]{1,0:T(1,128)} %refs_1_.3, s32[2,128]{1,0:T(2,128)} %bitcast.18, ...), custom_call_target="tpu_custom_call" | custom-call | tf_op jit(solution)/shard_map/route/pallas_call | solution.py:133
  4.1 1.7 %collective-permute-start = (bf16[128,3712]{1,0:T(8,128)(2,1)}, bf16[128,3712]{1,0:T(8,128)(2,1)S(1)}, u32[]{:S(2)}, u32[]{:S(2)}) collective-permute-start(bf16[128,3712]{1,0:T(8,128)(2,1)} %get-tuple-element.39.refs_3_.refs_8_), channel_id=1, source_target_pairs={{0,2},{1,3},{2,0},{3,1},{4,6},{5,7},{6,4},{7,5},{8,10},{9,11},{10,... | collective-permute-start | bytes 2850824 | tf_op jit(solution)/shard_map/ppermute | solution.py:43
  5.7 2.1 %collective-permute-start.4 = (bf16[80,3584]{1,0:T(8,128)(2,1)}, bf16[80,3584]{1,0:T(8,128)(2,1)S(1)}, u32[]{:S(2)}, u32[]{:S(2)}) collective-permute-start(bf16[80,3584]{1,0:T(8,128)(2,1)} %get-tuple-element.40), channel_id=1, source_target_pairs={{0,8},{1,9},{2,10},{3,11},{4,12},{5,13},{6,14},{7,15},{8,0},{9,1},... | collective-permute-start | bytes 1720328 | tf_op jit(solution)/shard_map/ppermute | solution.py:43
  7.8 1.2 %copy-done.1 = bf16[128,3712]{1,0:T(8,128)(2,1)S(1)} copy-done((bf16[128,3712]{1,0:T(8,128)(2,1)S(1)}, bf16[128,3712]{1,0:T(8,128)(2,1)}, u32[]{:S(2)}) %copy-start.1) | copy-done | bytes 950296
  9.0 6.2 %load.3 = (bf16[3584,512]{1,0:T(8,128)(2,1)S(1)}, bf16[3584,512]{1,0:T(8,128)(2,1)S(1)}, bf16[512,3584]{1,0:T(8,128)(2,1)}) custom-call(bf16[3584,512]{1,0:T(8,128)(2,1)} %bitcast.12, bf16[3584,512]{1,0:T(8,128)(2,1)} %bitcast.14, bf16[512,3584]{1,0:T(8,128)(2,1)} %bitcast.16, bf16[128,3712]{1,0:T(8,128)(2,1)S(1)} %copy-done.1), custom_call_target="tpu_custom_call" | custom-call | tf_op jit(solution)/shard_map/load/pallas_call | solution.py:165
  15.3 2.0 %collective-permute-done.3.refs_2_.refs_4_ = bf16[512,3584]{1,0:T(8,128)(2,1)} collective-permute-done((bf16[512,3584]{1,0:T(8,128)(2,1)}, bf16[512,3584]{1,0:T(8,128)(2,1)}, u32[]{:S(2)}, u32[]{:S(2)}) %collective-permute-start.3) | collective-permute-done | bytes 3670048 | tf_op jit(solution)/shard_map/ppermute | solution.py:43
  17.3 1.5 %collective-permute-start.5 = (bf16[80,3584]{1,0:T(8,128)(2,1)S(1)}, bf16[80,3584]{1,0:T(8,128)(2,1)S(1)}, u32[]{:S(2)}, u32[]{:S(2)}) collective-permute-start(bf16[80,3584]{1,0:T(8,128)(2,1)S(1)} %get-tuple-element.47.refs_1_), channel_id=1, source_target_pairs={{0,4},{1,5},{2,6},{3,7},{4,8},{5,9},{6,10},{7,11},{8,12},{9,13},{1... | collective-permute-start | bytes 1720328 | tf_op jit(solution)/shard_map/ppermute | solution.py:43
  18.8 0.9 collective-permute-start.6
  19.6 3.1 %collective-permute-done.4.refs_3_.refs_0_ = bf16[80,3584]{1,0:T(8,128)(2,1)S(1)} collective-permute-done((bf16[80,3584]{1,0:T(8,128)(2,1)}, bf16[80,3584]{1,0:T(8,128)(2,1)S(1)}, u32[]{:S(2)}, u32[]{:S(2)}) %collective-permute-start.4) | collective-permute-done | bytes 573472 | tf_op jit(solution)/shard_map/ppermute | solution.py:43
  22.7 4.2 %load.2 = (bf16[3584,512]{1,0:T(8,128)(2,1)S(1)}, bf16[3584,512]{1,0:T(8,128)(2,1)S(1)}, bf16[512,3584]{1,0:T(8,128)(2,1)S(1)}) custom-call(bf16[3584,512]{1,0:T(8,128)(2,1)} %collective-permute-done.1.refs_0_.refs_2_, bf16[3584,512]{1,0:T(8,128)(2,1)} %collective-permute-done.2.refs_1_.refs_3_, bf16[512,3584]{1,0:T(8,128)(2,1)} %collective-permute-done.3.refs_2_.refs_4_, ...), custom_call_target="tpu_custom_call" | custom-call | tf_op jit(solution)/shard_map/load/pallas_call | solution.py:165
  27.0 0.8 collective-permute-done.refs_0_.refs_3_.refs_9_
  27.8 1.6 %collective-permute-start.9 = (bf16[80,3584]{1,0:T(8,128)(2,1)S(1)}, bf16[80,3584]{1,0:T(8,128)(2,1)S(1)}, u32[]{:S(2)}, u32[]{:S(2)}) collective-permute-start(bf16[80,3584]{1,0:T(8,128)(2,1)S(1)} %after.5.refs_1_), channel_id=1, source_target_pairs={{0,2},{1,3},{2,0},{3,1},{4,6},{5,7},{6,4},{7,5},{8,10},{9,11},{10,... | collective-permute-start | bytes 1720328 | tf_op jit(solution)/shard_map/ppermute | solution.py:43
  29.4 0.9 route.3
  30.3 1.6 %collective-permute-start.10 = (bf16[80,3584]{1,0:T(8,128)(2,1)S(1)}, bf16[80,3584]{1,0:T(8,128)(2,1)S(1)}, u32[]{:S(2)}, u32[]{:S(2)}) collective-permute-start(bf16[80,3584]{1,0:T(8,128)(2,1)S(1)} %get-tuple-element.59), channel_id=1, source_target_pairs={{0,4},{1,5},{2,6},{3,7},{4,8},{5,9},{6,10},{7,11},{8,12},{9,13},{1... | collective-permute-start | bytes 1720328 | tf_op jit(solution)/shard_map/ppermute | solution.py:43
  31.9 0.5 collective-permute-start.11
  32.4 3.2 %collective-permute-done.5.refs_2_ = bf16[80,3584]{1,0:T(8,128)(2,1)S(1)} collective-permute-done((bf16[80,3584]{1,0:T(8,128)(2,1)S(1)}, bf16[80,3584]{1,0:T(8,128)(2,1)S(1)}, u32[]{:S(2)}, u32[]{:S(2)}) %collective-permute-start.5) | collective-permute-done | bytes 573472 | tf_op jit(solution)/shard_map/ppermute | solution.py:43
  35.6 7.3 %expert.3 = (bf16[80,3584]{1,0:T(8,128)(2,1)S(1)}, bf16[80,3584]{1,0:T(8,128)(2,1)S(1)}, bf16[80,3584]{1,0:T(8,128)(2,1)S(1)}, bf16[80,3584]{1,0:T(8,128)(2,1)S(1)}) custom-call(bf16[80,3584]{1,0:T(8,128)(2,1)S(1)} %copy-done.6, bf16[80,3584]{1,0:T(8,128)(2,1)S(1)} %after.5.refs_1_, bf16[80,3584]{1,0:T(8,128)(2,1)S(1)} %collective-permute-done.5.refs_2_, ...), custom_call_target="tpu_custom_call" | custom-call | tf_op jit(solution)/shard_map/expert/pallas_call | solution.py:230
  42.9 1.0 collective-permute-start.7
  43.9 1.1 collective-permute-start.8
  45.0 3.8 %expert.4 = (bf16[80,3584]{1,0:T(8,128)(2,1)S(1)}, bf16[80,3584]{1,0:T(8,128)(2,1)S(1)}, bf16[80,3584]{1,0:T(8,128)(2,1)S(1)}) custom-call(bf16[80,3584]{1,0:T(8,128)(2,1)S(1)} %collective-permute-done.9.refs_0_, bf16[80,3584]{1,0:T(8,128)(2,1)S(1)} %get-tuple-element.56.refs_1_, bf16[3584,512]{1,0:T(8,128)(2,1)S(1)} %get-tuple-element.46.refs_5_.refs_4_.refs_2_, ...), custom_call_target="tpu_custom_call" | custom-call | tf_op jit(solution)/shard_map/expert/pallas_call | solution.py:230
  48.8 0.9 collective-permute-start.14
  49.7 3.8 %expert.5 = (bf16[80,1792]{1,0:T(8,128)(2,1)S(1)}, bf16[80,1792]{1,0:T(8,128)(2,1)S(1)}, bf16[80,1792]{1,0:T(8,128)(2,1)S(1)}, bf16[80,1792]{1,0:T(8,128)(2,1)S(1)}) custom-call(bf16[80,3584]{1,0:T(8,128)(2,1)S(1)} %collective-permute-done.10.refs_0_, bf16[80,3584]{1,0:T(8,128)(2,1)S(1)} %collective-permute-done.11.refs_1_, ...), custom_call_target="tpu_custom_call" | custom-call | tf_op jit(solution)/shard_map/expert/pallas_call | solution.py:230
  53.5 1.6 %collective-permute-start.12 = (bf16[80,1792]{1,0:T(8,128)(2,1)S(1)}, bf16[80,1792]{1,0:T(8,128)(2,1)S(1)}, u32[]{:S(2)}, u32[]{:S(2)}) collective-permute-start(bf16[80,1792]{1,0:T(8,128)(2,1)S(1)} %get-tuple-element.62), channel_id=1, source_target_pairs={{0,12},{1,13},{2,14},{3,15},{4,0},{5,1},{6,2},{7,3},{8,4},{9,5},{1... | collective-permute-start | bytes 860168 | tf_op jit(solution)/shard_map/ppermute | solution.py:43
  55.1 0.5 collective-permute-start.13
  55.6 4.5 %collective-permute-done.7.refs_1_.refs_2_ = bf16[80,3584]{1,0:T(8,128)(2,1)S(1)} collective-permute-done((bf16[80,3584]{1,0:T(8,128)(2,1)S(1)}, bf16[80,3584]{1,0:T(8,128)(2,1)S(1)}, u32[]{:S(2)}, u32[]{:S(2)}) %collective-permute-start.7) | collective-permute-done | bytes 573472 | tf_op jit(solution)/shard_map/ppermute | solution.py:43
  60.1 0.8 collective-permute-done.8.refs_2_.refs_3_
  60.9 1.5 %collective-permute-start.18 = (bf16[80,1792]{1,0:T(8,128)(2,1)S(1)}, bf16[80,1792]{1,0:T(8,128)(2,1)S(1)}, u32[]{:S(2)}, u32[]{:S(2)}) collective-permute-start(bf16[80,1792]{1,0:T(8,128)(2,1)S(1)} %get-tuple-element.68), channel_id=1, source_target_pairs={{0,12},{1,13},{2,14},{3,15},{4,0},{5,1},{6,2},{7,3},{8,4},{9,5},{1... | collective-permute-start | bytes 860168 | tf_op jit(solution)/shard_map/ppermute | solution.py:43
  62.5 0.5 collective-permute-start.19
  63.1 3.5 %collective-permute-start.15 = (bf16[80,1792]{1,0:T(8,128)(2,1)S(1)}, bf16[80,1792]{1,0:T(8,128)(2,1)S(1)}, u32[]{:S(2)}, u32[]{:S(2)}) collective-permute-start(bf16[80,1792]{1,0:T(8,128)(2,1)S(1)} %get-tuple-element.65), channel_id=1, source_target_pairs={{0,8},{1,9},{2,10},{3,11},{4,12},{5,13},{6,14},{7,15},{8,0},{9,1},... | collective-permute-start | bytes 860168 | tf_op jit(solution)/shard_map/ppermute | solution.py:43
  66.6 0.5 collective-permute-done.13.refs_5_
  67.1 0.4 leave.2
  67.5 1.1 %collective-permute-start.16 = (bf16[128,1792]{1,0:T(8,128)(2,1)S(1)}, bf16[128,1792]{1,0:T(8,128)(2,1)S(1)}, u32[]{:S(2)}, u32[]{:S(2)}) collective-permute-start(bf16[128,1792]{1,0:T(8,128)(2,1)S(1)} %leave.2), channel_id=1, source_target_pairs={{0,2},{1,3},{2,0},{3,1},{4,6},{5,7},{6,4},{7,5},{8,10},{9,11},{10,... | collective-permute-start | bytes 1376264 | tf_op jit(solution)/shard_map/ppermute | solution.py:43
  68.6 4.4 %collective-permute-done.18.refs_4_ = bf16[80,1792]{1,0:T(8,128)(2,1)S(1)} collective-permute-done((bf16[80,1792]{1,0:T(8,128)(2,1)S(1)}, bf16[80,1792]{1,0:T(8,128)(2,1)S(1)}, u32[]{:S(2)}, u32[]{:S(2)}) %collective-permute-start.18) | collective-permute-done | bytes 286752 | tf_op jit(solution)/shard_map/ppermute | solution.py:43
  73.0 0.2 collective-permute-done.19.refs_5_
  73.2 0.4 leave.3
  73.7 1.1 collective-permute-start.21
  74.8 3.1 %collective-permute-done.15.refs_6_.refs_1_ = bf16[80,1792]{1,0:T(8,128)(2,1)S(1)} collective-permute-done((bf16[80,1792]{1,0:T(8,128)(2,1)S(1)}, bf16[80,1792]{1,0:T(8,128)(2,1)S(1)}, u32[]{:S(2)}, u32[]{:S(2)}) %collective-permute-start.15) | collective-permute-done | bytes 286752 | tf_op jit(solution)/shard_map/ppermute | solution.py:43
  77.8 3.9 %collective-permute-start.20 = (bf16[80,1792]{1,0:T(8,128)(2,1)S(1)}, bf16[80,1792]{1,0:T(8,128)(2,1)S(1)}, u32[]{:S(2)}, u32[]{:S(2)}) collective-permute-start(bf16[80,1792]{1,0:T(8,128)(2,1)S(1)} %after.7), channel_id=1, source_target_pairs={{0,8},{1,9},{2,10},{3,11},{4,12},{5,13},{6,14},{7,15},{8,0},{9,1},... | collective-permute-start | bytes 860168 | tf_op jit(solution)/shard_map/ppermute | solution.py:43
  81.7 0.7 stay.2
  82.4 1.4 %collective-permute-start.17 = (bf16[128,1792]{1,0:T(8,128)(2,1)S(1)}, bf16[128,1792]{1,0:T(8,128)(2,1)S(1)}, u32[]{:S(2)}, u32[]{:S(2)}) collective-permute-start(bf16[128,1792]{1,0:T(8,128)(2,1)S(1)} %stay.2), channel_id=1, source_target_pairs={{0,16},{1,17},{2,18},{3,19},{4,20},{5,21},{6,22},{7,23},{8,24},{9,... | collective-permute-start | bytes 1376264 | tf_op jit(solution)/shard_map/ppermute | solution.py:52
  83.8 3.1 %collective-permute-done.20.refs_6_ = bf16[80,1792]{1,0:T(8,128)(2,1)S(1)} collective-permute-done((bf16[80,1792]{1,0:T(8,128)(2,1)S(1)}, bf16[80,1792]{1,0:T(8,128)(2,1)S(1)}, u32[]{:S(2)}, u32[]{:S(2)}) %collective-permute-start.20) | collective-permute-done | bytes 286752 | tf_op jit(solution)/shard_map/ppermute | solution.py:43
  86.9 0.9 collective-permute-done.21.refs_7_
  87.8 0.7 stay.3
  88.5 2.0 %collective-permute-start.22 = (bf16[128,1792]{1,0:T(8,128)(2,1)S(1)}, bf16[128,1792]{1,0:T(8,128)(2,1)S(1)}, u32[]{:S(2)}, u32[]{:S(2)}) collective-permute-start(bf16[128,1792]{1,0:T(8,128)(2,1)S(1)} %stay.3), channel_id=1, source_target_pairs={{0,16},{1,17},{2,18},{3,19},{4,20},{5,21},{6,22},{7,23},{8,24},{9,... | collective-permute-start | bytes 1376264 | tf_op jit(solution)/shard_map/ppermute | solution.py:52
  90.5 9.9 %collective-permute-done.17.a_ref = bf16[128,1792]{1,0:T(8,128)(2,1)S(1)} collective-permute-done((bf16[128,1792]{1,0:T(8,128)(2,1)S(1)}, bf16[128,1792]{1,0:T(8,128)(2,1)S(1)}, u32[]{:S(2)}, u32[]{:S(2)}) %collective-permute-start.17) | collective-permute-done | bytes 458784 | tf_op jit(solution)/shard_map/ppermute | solution.py:52
  100.4 7.7 %collective-permute-done.22.b_ref = bf16[128,1792]{1,0:T(8,128)(2,1)S(1)} collective-permute-done((bf16[128,1792]{1,0:T(8,128)(2,1)S(1)}, bf16[128,1792]{1,0:T(8,128)(2,1)S(1)}, u32[]{:S(2)}, u32[]{:S(2)}) %collective-permute-start.22) | collective-permute-done | bytes 458784 | tf_op jit(solution)/shard_map/ppermute | solution.py:52
  108.1 0.9 join.1
  (31 shorter events, 0.2 us)
Async XLA Ops:
  0.0 15.3 %collective-permute-start.1 = (bf16[3584,512]{1,0:T(8,128)(2,1)}, bf16[3584,512]{1,0:T(8,128)(2,1)}, u32[]{:S(2)}, u32[]{:S(2)}) collective-permute-start(bf16[3584,512]{1,0:T(8,128)(2,1)} %bitcast.11), channel_id=1, source_target_pairs={{0,1},{1,0},{2,3},{3,2},{4,5},{5,4},{6,7},{7,6},{8,9},{9,8},{10,11... | collective-permute-start | bytes 11010056 | tf_op jit(solution)/shard_map/ppermute | solution.py:43
  0.0 15.3 %collective-permute-start.2 = (bf16[3584,512]{1,0:T(8,128)(2,1)}, bf16[3584,512]{1,0:T(8,128)(2,1)}, u32[]{:S(2)}, u32[]{:S(2)}) collective-permute-start(bf16[3584,512]{1,0:T(8,128)(2,1)} %bitcast.13), channel_id=1, source_target_pairs={{0,1},{1,0},{2,3},{3,2},{4,5},{5,4},{6,7},{7,6},{8,9},{9,8},{10,11... | collective-permute-start | bytes 11010056 | tf_op jit(solution)/shard_map/ppermute | solution.py:43
  0.5 16.7 %collective-permute-start.3 = (bf16[512,3584]{1,0:T(8,128)(2,1)}, bf16[512,3584]{1,0:T(8,128)(2,1)}, u32[]{:S(2)}, u32[]{:S(2)}) collective-permute-start(bf16[512,3584]{1,0:T(8,128)(2,1)} %bitcast.15), channel_id=1, source_target_pairs={{0,1},{1,0},{2,3},{3,2},{4,5},{5,4},{6,7},{7,6},{8,9},{9,8},{10,11... | collective-permute-start | bytes 11010056 | tf_op jit(solution)/shard_map/ppermute | solution.py:43
  4.1 23.8 %collective-permute-start = (bf16[128,3712]{1,0:T(8,128)(2,1)}, bf16[128,3712]{1,0:T(8,128)(2,1)S(1)}, u32[]{:S(2)}, u32[]{:S(2)}) collective-permute-start(bf16[128,3712]{1,0:T(8,128)(2,1)} %get-tuple-element.39.refs_3_.refs_8_), channel_id=1, source_target_pairs={{0,2},{1,3},{2,0},{3,1},{4,6},{5,7},{6,4},{7,5},{8,10},{9,11},{10,... | collective-permute-start | bytes 2850824 | tf_op jit(solution)/shard_map/ppermute | solution.py:43
  5.7 17.0 %collective-permute-start.4 = (bf16[80,3584]{1,0:T(8,128)(2,1)}, bf16[80,3584]{1,0:T(8,128)(2,1)S(1)}, u32[]{:S(2)}, u32[]{:S(2)}) collective-permute-start(bf16[80,3584]{1,0:T(8,128)(2,1)} %get-tuple-element.40), channel_id=1, source_target_pairs={{0,8},{1,9},{2,10},{3,11},{4,12},{5,13},{6,14},{7,15},{8,0},{9,1},... | collective-permute-start | bytes 1720328 | tf_op jit(solution)/shard_map/ppermute | solution.py:43
  7.8 1.2 %copy-start.1 = (bf16[128,3712]{1,0:T(8,128)(2,1)S(1)}, bf16[128,3712]{1,0:T(8,128)(2,1)}, u32[]{:S(2)}) copy-start(bf16[128,3712]{1,0:T(8,128)(2,1)} %get-tuple-element.39.refs_3_.refs_8_) | copy-start | bytes 2850820
  9.0 8.2 %copy-start.4 = (bf16[80,3584]{1,0:T(8,128)(2,1)S(1)}, bf16[80,3584]{1,0:T(8,128)(2,1)}, u32[]{:S(2)}) copy-start(bf16[80,3584]{1,0:T(8,128)(2,1)} %get-tuple-element.44.refs_0_) | copy-start | bytes 1720324
  9.0 8.2 %copy-start.5 = (bf16[80,3584]{1,0:T(8,128)(2,1)S(1)}, bf16[80,3584]{1,0:T(8,128)(2,1)}, u32[]{:S(2)}) copy-start(bf16[80,3584]{1,0:T(8,128)(2,1)} %get-tuple-element.45.refs_1_) | copy-start | bytes 1720324
  17.3 18.4 %collective-permute-start.5 = (bf16[80,3584]{1,0:T(8,128)(2,1)S(1)}, bf16[80,3584]{1,0:T(8,128)(2,1)S(1)}, u32[]{:S(2)}, u32[]{:S(2)}) collective-permute-start(bf16[80,3584]{1,0:T(8,128)(2,1)S(1)} %get-tuple-element.47.refs_1_), channel_id=1, source_target_pairs={{0,4},{1,5},{2,6},{3,7},{4,8},{5,9},{6,10},{7,11},{8,12},{9,13},{1... | collective-permute-start | bytes 1720328 | tf_op jit(solution)/shard_map/ppermute | solution.py:43
  18.7 10.7 %copy-start.7 = (f32[1,3584]{1,0:T(1,128)S(1)}, f32[1,3584]{1,0:T(1,128)}, u32[]{:S(2)}) copy-start(f32[1,3584]{1,0:T(1,128)} %refs_1_.3) | copy-start | bytes 43012
  18.8 16.9 %collective-permute-start.6 = (bf16[80,3584]{1,0:T(8,128)(2,1)S(1)}, bf16[80,3584]{1,0:T(8,128)(2,1)S(1)}, u32[]{:S(2)}, u32[]{:S(2)}) collective-permute-start(bf16[80,3584]{1,0:T(8,128)(2,1)S(1)} %get-tuple-element.48.refs_2_), channel_id=1, source_target_pairs={{0,12},{1,13},{2,14},{3,15},{4,0},{5,1},{6,2},{7,3},{8,4},{9,5},{1... | collective-permute-start | bytes 1720328 | tf_op jit(solution)/shard_map/ppermute | solution.py:43
  27.0 8.7 %copy-start = (bf16[512,3584]{1,0:T(8,128)(2,1)S(1)}, bf16[512,3584]{1,0:T(8,128)(2,1)}, u32[]{:S(2)}) copy-start(bf16[512,3584]{1,0:T(8,128)(2,1)} %get-tuple-element.50.refs_6_.refs_4_) | copy-start | bytes 11010052
  27.0 8.7 %copy-start.6 = (bf16[80,3584]{1,0:T(8,128)(2,1)S(1)}, bf16[80,3584]{1,0:T(8,128)(2,1)}, u32[]{:S(2)}) copy-start(bf16[80,3584]{1,0:T(8,128)(2,1)} %get-tuple-element.43.refs_0_) | copy-start | bytes 1720324
  27.8 17.2 %collective-permute-start.9 = (bf16[80,3584]{1,0:T(8,128)(2,1)S(1)}, bf16[80,3584]{1,0:T(8,128)(2,1)S(1)}, u32[]{:S(2)}, u32[]{:S(2)}) collective-permute-start(bf16[80,3584]{1,0:T(8,128)(2,1)S(1)} %after.5.refs_1_), channel_id=1, source_target_pairs={{0,2},{1,3},{2,0},{3,1},{4,6},{5,7},{6,4},{7,5},{8,10},{9,11},{10,... | collective-permute-start | bytes 1720328 | tf_op jit(solution)/shard_map/ppermute | solution.py:43
  30.3 19.4 %collective-permute-start.10 = (bf16[80,3584]{1,0:T(8,128)(2,1)S(1)}, bf16[80,3584]{1,0:T(8,128)(2,1)S(1)}, u32[]{:S(2)}, u32[]{:S(2)}) collective-permute-start(bf16[80,3584]{1,0:T(8,128)(2,1)S(1)} %get-tuple-element.59), channel_id=1, source_target_pairs={{0,4},{1,5},{2,6},{3,7},{4,8},{5,9},{6,10},{7,11},{8,12},{9,13},{1... | collective-permute-start | bytes 1720328 | tf_op jit(solution)/shard_map/ppermute | solution.py:43
  31.9 17.8 %collective-permute-start.11 = (bf16[80,3584]{1,0:T(8,128)(2,1)S(1)}, bf16[80,3584]{1,0:T(8,128)(2,1)S(1)}, u32[]{:S(2)}, u32[]{:S(2)}) collective-permute-start(bf16[80,3584]{1,0:T(8,128)(2,1)S(1)} %get-tuple-element.60), channel_id=1, source_target_pairs={{0,12},{1,13},{2,14},{3,15},{4,0},{5,1},{6,2},{7,3},{8,4},{9,5},{1... | collective-permute-start | bytes 1720328 | tf_op jit(solution)/shard_map/ppermute | solution.py:43
  42.9 17.2 %collective-permute-start.7 = (bf16[80,3584]{1,0:T(8,128)(2,1)S(1)}, bf16[80,3584]{1,0:T(8,128)(2,1)S(1)}, u32[]{:S(2)}, u32[]{:S(2)}) collective-permute-start(bf16[80,3584]{1,0:T(8,128)(2,1)S(1)} %get-tuple-element.54), channel_id=1, source_target_pairs={{0,12},{1,13},{2,14},{3,15},{4,0},{5,1},{6,2},{7,3},{8,4},{9,5},{1... | collective-permute-start | bytes 1720328 | tf_op jit(solution)/shard_map/ppermute | solution.py:43
  43.9 17.0 %collective-permute-start.8 = (bf16[80,3584]{1,0:T(8,128)(2,1)S(1)}, bf16[80,3584]{1,0:T(8,128)(2,1)S(1)}, u32[]{:S(2)}, u32[]{:S(2)}) collective-permute-start(bf16[80,3584]{1,0:T(8,128)(2,1)S(1)} %get-tuple-element.55), channel_id=1, source_target_pairs={{0,4},{1,5},{2,6},{3,7},{4,8},{5,9},{6,10},{7,11},{8,12},{9,13},{1... | collective-permute-start | bytes 1720328 | tf_op jit(solution)/shard_map/ppermute | solution.py:43
  48.8 18.3 %copy-start.3 = (bf16[4,80,256]{2,1,0:T(8,128)(2,1)S(1)}, bf16[4,80,256]{2,1,0:T(8,128)(2,1)}, u32[]{:S(2)}) copy-start(bf16[4,80,256]{2,1,0:T(8,128)(2,1)} %get-tuple-element.38.w_own_ref) | copy-start | bytes 491524
  48.8 14.1 %collective-permute-start.14 = (bf16[80,3584]{1,0:T(8,128)(2,1)S(1)}, bf16[80,3584]{1,0:T(8,128)(2,1)S(1)}, u32[]{:S(2)}, u32[]{:S(2)}) collective-permute-start(bf16[80,3584]{1,0:T(8,128)(2,1)S(1)} %get-tuple-element.61.refs_8_), channel_id=1, source_target_pairs={{0,2},{1,3},{2,0},{3,1},{4,6},{5,7},{6,4},{7,5},{8,10},{9,11},{10,... | collective-permute-start | bytes 1720328 | tf_op jit(solution)/shard_map/ppermute | solution.py:43
  53.5 13.1 %collective-permute-start.12 = (bf16[80,1792]{1,0:T(8,128)(2,1)S(1)}, bf16[80,1792]{1,0:T(8,128)(2,1)S(1)}, u32[]{:S(2)}, u32[]{:S(2)}) collective-permute-start(bf16[80,1792]{1,0:T(8,128)(2,1)S(1)} %get-tuple-element.62), channel_id=1, source_target_pairs={{0,12},{1,13},{2,14},{3,15},{4,0},{5,1},{6,2},{7,3},{8,4},{9,5},{1... | collective-permute-start | bytes 860168 | tf_op jit(solution)/shard_map/ppermute | solution.py:43
  55.1 12.0 %collective-permute-start.13 = (bf16[80,1792]{1,0:T(8,128)(2,1)S(1)}, bf16[80,1792]{1,0:T(8,128)(2,1)S(1)}, u32[]{:S(2)}, u32[]{:S(2)}) collective-permute-start(bf16[80,1792]{1,0:T(8,128)(2,1)S(1)} %get-tuple-element.63), channel_id=1, source_target_pairs={{0,4},{1,5},{2,6},{3,7},{4,8},{5,9},{6,10},{7,11},{8,12},{9,13},{1... | collective-permute-start | bytes 860168 | tf_op jit(solution)/shard_map/ppermute | solution.py:43
  60.9 12.1 %collective-permute-start.18 = (bf16[80,1792]{1,0:T(8,128)(2,1)S(1)}, bf16[80,1792]{1,0:T(8,128)(2,1)S(1)}, u32[]{:S(2)}, u32[]{:S(2)}) collective-permute-start(bf16[80,1792]{1,0:T(8,128)(2,1)S(1)} %get-tuple-element.68), channel_id=1, source_target_pairs={{0,12},{1,13},{2,14},{3,15},{4,0},{5,1},{6,2},{7,3},{8,4},{9,5},{1... | collective-permute-start | bytes 860168 | tf_op jit(solution)/shard_map/ppermute | solution.py:43
  62.5 10.8 %collective-permute-start.19 = (bf16[80,1792]{1,0:T(8,128)(2,1)S(1)}, bf16[80,1792]{1,0:T(8,128)(2,1)S(1)}, u32[]{:S(2)}, u32[]{:S(2)}) collective-permute-start(bf16[80,1792]{1,0:T(8,128)(2,1)S(1)} %get-tuple-element.69), channel_id=1, source_target_pairs={{0,4},{1,5},{2,6},{3,7},{4,8},{5,9},{6,10},{7,11},{8,12},{9,13},{1... | collective-permute-start | bytes 860168 | tf_op jit(solution)/shard_map/ppermute | solution.py:43
  63.1 14.7 %collective-permute-start.15 = (bf16[80,1792]{1,0:T(8,128)(2,1)S(1)}, bf16[80,1792]{1,0:T(8,128)(2,1)S(1)}, u32[]{:S(2)}, u32[]{:S(2)}) collective-permute-start(bf16[80,1792]{1,0:T(8,128)(2,1)S(1)} %get-tuple-element.65), channel_id=1, source_target_pairs={{0,8},{1,9},{2,10},{3,11},{4,12},{5,13},{6,14},{7,15},{8,0},{9,1},... | collective-permute-start | bytes 860168 | tf_op jit(solution)/shard_map/ppermute | solution.py:43
  67.1 14.6 %copy-start.2 = (bf16[128,3712]{1,0:T(8,128)(2,1)S(1)}, bf16[128,3712]{1,0:T(8,128)(2,1)}, u32[]{:S(2)}) copy-start(bf16[128,3712]{1,0:T(8,128)(2,1)} %get-tuple-element.39.refs_3_.refs_8_) | copy-start | bytes 2850820
  67.5 14.2 %collective-permute-start.16 = (bf16[128,1792]{1,0:T(8,128)(2,1)S(1)}, bf16[128,1792]{1,0:T(8,128)(2,1)S(1)}, u32[]{:S(2)}, u32[]{:S(2)}) collective-permute-start(bf16[128,1792]{1,0:T(8,128)(2,1)S(1)} %leave.2), channel_id=1, source_target_pairs={{0,2},{1,3},{2,0},{3,1},{4,6},{5,7},{6,4},{7,5},{8,10},{9,11},{10,... | collective-permute-start | bytes 1376264 | tf_op jit(solution)/shard_map/ppermute | solution.py:43
  73.7 14.1 %collective-permute-start.21 = (bf16[128,1792]{1,0:T(8,128)(2,1)S(1)}, bf16[128,1792]{1,0:T(8,128)(2,1)S(1)}, u32[]{:S(2)}, u32[]{:S(2)}) collective-permute-start(bf16[128,1792]{1,0:T(8,128)(2,1)S(1)} %leave.3), channel_id=1, source_target_pairs={{0,2},{1,3},{2,0},{3,1},{4,6},{5,7},{6,4},{7,5},{8,10},{9,11},{10,... | collective-permute-start | bytes 1376264 | tf_op jit(solution)/shard_map/ppermute | solution.py:43
  77.8 9.0 %collective-permute-start.20 = (bf16[80,1792]{1,0:T(8,128)(2,1)S(1)}, bf16[80,1792]{1,0:T(8,128)(2,1)S(1)}, u32[]{:S(2)}, u32[]{:S(2)}) collective-permute-start(bf16[80,1792]{1,0:T(8,128)(2,1)S(1)} %after.7), channel_id=1, source_target_pairs={{0,8},{1,9},{2,10},{3,11},{4,12},{5,13},{6,14},{7,15},{8,0},{9,1},... | collective-permute-start | bytes 860168 | tf_op jit(solution)/shard_map/ppermute | solution.py:43
  82.4 18.0 %collective-permute-start.17 = (bf16[128,1792]{1,0:T(8,128)(2,1)S(1)}, bf16[128,1792]{1,0:T(8,128)(2,1)S(1)}, u32[]{:S(2)}, u32[]{:S(2)}) collective-permute-start(bf16[128,1792]{1,0:T(8,128)(2,1)S(1)} %stay.2), channel_id=1, source_target_pairs={{0,16},{1,17},{2,18},{3,19},{4,20},{5,21},{6,22},{7,23},{8,24},{9,... | collective-permute-start | bytes 1376264 | tf_op jit(solution)/shard_map/ppermute | solution.py:52
  88.5 19.6 %collective-permute-start.22 = (bf16[128,1792]{1,0:T(8,128)(2,1)S(1)}, bf16[128,1792]{1,0:T(8,128)(2,1)S(1)}, u32[]{:S(2)}, u32[]{:S(2)}) collective-permute-start(bf16[128,1792]{1,0:T(8,128)(2,1)S(1)} %stay.3), channel_id=1, source_target_pairs={{0,16},{1,17},{2,18},{3,19},{4,20},{5,21},{6,22},{7,23},{8,24},{9,... | collective-permute-start | bytes 1376264 | tf_op jit(solution)/shard_map/ppermute | solution.py:52
